TPU v7x, 512 devices: a whole 4x4x16 slice. The times are simulated.
512 devices in a mesh: gx: 8 (over z_hi, x), gy: 64 (over y, z_lo, core).
Axes of the slice: x: 4, y: 4, z: 16 (z_hi: 2, z_lo: 8; z = z_hi * 8 + z_lo), core: 2. Of those that a mesh axis runs over, the one named last changes fastest.
Arguments:
- grid_latent: bfloat16 [16, 4096, 512], P('gx', 'gy'), may hold values from -6 to 6
- mesh_latent: bfloat16 [8, 64, 256, 512], P('gx', 'gy'), may hold values from -6 to 6
- encode_message: bfloat16 [512, 512], replicated, may hold values from -0.25 to 0.25
- encode_update: bfloat16 [512, 512], replicated, may hold values from -0.25 to 0.25
- process_message: bfloat16 [512, 512], replicated, may hold values from -0.25 to 0.25
- process_update: bfloat16 [512, 512], replicated, may hold values from -0.25 to 0.25
- decode_message: bfloat16 [512, 512], replicated, may hold values from -0.25 to 0.25
- decode_update: bfloat16 [512, 512], replicated, may hold values from -0.25 to 0.25
- encode_source: int32 [8, 64, 1024], P('gx', 'gy'), may hold values from 0 to 65535, as said below
- encode_target: int32 [8, 64, 1024], P('gx', 'gy'), may hold values from -1 to 255, as said below
- process_source: int32 [8, 64, 1024], P('gx', 'gy'), may hold values from 0 to 255
- process_target: int32 [8, 64, 1024], P('gx', 'gy'), may hold values from -1 to 255, as said below
- decode_source: int32 [8, 64, 1024], P('gx', 'gy'), may hold values from 0 to 131071, as said below
- decode_target: int32 [8, 64, 1024], P('gx', 'gy'), may hold values from -1 to 127
Outputs:
- grid_output: bfloat16 [16, 4096, 512], P('gx', 'gy')
- mesh_output: bfloat16 [8, 64, 256, 512], P('gx', 'gy')
Inputs may be any that keep to these rules, and one draw needn't show every extreme that they name: `encode_source`: the source of a slot of band b and sector s lies in grid rows b * 2 - 1 to (b + 1) * 2 and in the 80 columns from s * 64 - 8, modulo 4096. `encode_target`: every slot of the first and the last band is live. `process_target`: slots whose source sector is the device's own sector or one next to it (with wrapping) are all live. `decode_source`: the source of a slot of band b and sector s lies in band b and in sectors s - 1, s or s + 1, modulo 64.
All inputs are finite; a program needn't handle non-finite values.
Results may differ from a plain program's by a relative error of at most 0.008.
Values may be sent and summed in bfloat16 or wider, within the bound.
No kernel may reach another device: no remote copies, remote signals or barrier semaphores. Data moves between devices by JAX's collectives and lax.ppermute only.
A program may use at most 64 MiB of HBM per device.

v0:
```python
import jax
import jax.numpy as jnp
from jax import lax
from jax.sharding import PartitionSpec as P

HALO = 8


EPSILON = 1e-05


def padded(value, sides, width, wrap):
    for axis, dim in sides:
        devices, length = (lax.axis_size(axis), value.shape[dim])
        up = [(i, (i + 1) % devices) for i in range(devices if wrap else devices - 1)]
        down = [(j, i) for i, j in up]
        last = lax.slice_in_dim(value, length - width, length, axis=dim)
        initial = lax.slice_in_dim(value, 0, width, axis=dim)
        before = lax.ppermute(last, axis, up)
        after = lax.ppermute(initial, axis, down)
        value = jnp.concatenate([before, value, after], axis=dim)
    return value


def edge_messages(rows, targets):
    summed = rows.astype(jnp.float32) + targets.astype(jnp.float32)
    return jax.nn.silu(summed).astype(jnp.bfloat16)


def refresh(latent, summed, weight):
    scaled = summed * lax.rsqrt(jnp.mean(summed * summed, axis=-1, keepdims=True) + EPSILON)
    branch = jnp.dot(scaled.astype(jnp.bfloat16), weight, preferred_element_type=jnp.float32)
    return (latent.astype(jnp.float32) + branch).astype(jnp.bfloat16)


def aggregate(rows, targets, target_index, count):
    live = target_index >= 0
    clamped = jnp.where(live, target_index, 0)
    messages = edge_messages(rows, targets[clamped])
    onehot = (target_index[:, None] == jnp.arange(count, dtype=jnp.int32)[None, :]).astype(
        jnp.bfloat16
    )
    return jnp.einsum("ec,ed->cd", onehot, messages, preferred_element_type=jnp.float32)


def on_device(
    grid_latent,
    mesh_latent,
    encode_message,
    encode_update,
    process_message,
    process_update,
    decode_message,
    decode_update,
    encode_source,
    encode_target,
    process_source,
    process_target,
    decode_source,
    decode_target,
):
    lat_rows, lon_cols, width = grid_latent.shape
    sectors = lax.axis_size("gy")
    lon_total = lon_cols * sectors
    band_index = lax.axis_index("gx")
    sector_index = lax.axis_index("gy")
    mesh_rows = mesh_latent.reshape(-1, width)
    mesh_count = mesh_rows.shape[0]
    grid_rows = grid_latent.reshape(-1, width)
    grid_table = jnp.dot(grid_rows, encode_message, preferred_element_type=jnp.float32).astype(
        jnp.bfloat16
    )
    grid_table = grid_table.reshape(lat_rows, lon_cols, width)
    widened = padded(grid_table, (("gy", 1),), HALO, True)
    widened = padded(widened, (("gx", 0),), 1, False)
    span = lon_cols + 2 * HALO
    source = encode_source.reshape(-1)
    lat_local = source // lon_total - band_index * lat_rows + 1
    lon_local = (source % lon_total - sector_index * lon_cols + HALO) % lon_total
    gathered = widened.reshape(-1, width)[lat_local * span + lon_local]
    summed = aggregate(gathered, mesh_rows, encode_target.reshape(-1), mesh_count)
    mesh_first = refresh(mesh_rows, summed, encode_update)
    mesh_table = jnp.dot(mesh_first, process_message, preferred_element_type=jnp.float32).astype(
        jnp.bfloat16
    )
    requests = process_source.reshape(sectors, -1)
    band_table = lax.all_gather(mesh_table, "gy", axis=0, tiled=True)
    owners = jnp.arange(requests.size, dtype=jnp.int32) // requests.shape[1]
    picked = band_table[owners * mesh_count + process_source.reshape(-1)]
    summed = aggregate(picked, mesh_first, process_target.reshape(-1), mesh_count)
    mesh_second = refresh(mesh_first, summed, process_update)
    decode_table = jnp.dot(mesh_second, decode_message, preferred_element_type=jnp.float32).astype(
        jnp.bfloat16
    )
    decode_table = decode_table.reshape(1, 1, mesh_count, width)
    neighbours = padded(decode_table, (("gy", 1),), 1, True).reshape(-1, width)
    source = decode_source.reshape(-1)
    source_sector = source // mesh_count % sectors
    offset = (source_sector - sector_index + 1) % sectors
    picked = neighbours[offset * mesh_count + source % mesh_count]
    summed = aggregate(picked, grid_rows, decode_target.reshape(-1), grid_rows.shape[0])
    grid_output = refresh(grid_rows, summed, decode_update).reshape(lat_rows, lon_cols, width)
    return (grid_output, mesh_second.reshape(1, 1, mesh_count, width))


def solution(mesh):
    return jax.shard_map(
        on_device,
        mesh=mesh,
        in_specs=(
            P("gx", "gy", None),
            P("gx", "gy", None, None),
            P(),
            P(),
            P(),
            P(),
            P(),
            P(),
            P("gx", "gy", None),
            P("gx", "gy", None),
            P("gx", "gy", None),
            P("gx", "gy", None),
            P("gx", "gy", None),
            P("gx", "gy", None),
        ),
        out_specs=(P("gx", "gy", None), P("gx", "gy", None, None)),
        check_vma=False,
    )
```

profile of v0, /device:TPU:6, one launch (start us, length us, event | category | flops | bytes accessed | tf_op | source)
XLA Modules:
  0.0 244.6 jit_solution(9071079383937139321)
XLA Ops:
  7.2 1.4 convolution_convert_fusion.2
  8.7 1.9 collective-permute-start
  10.6 15.0 %collective-permute-start.1 = (bf16[2,8,512]{2,1,0:T(8,128)(2,1)S(1)}, bf16[2,8,512]{2,1,0:T(8,128)(2,1)S(1)}, u32[]{:S(2)}, u32[]{:S(2)}) collective-permute-start(bf16[2,8,512]{2,1,0:T(8,128)(2,1)S(1)} %get-tuple-element.5), channel_id=1, source_target_pairs={{1,0},{2,1},{3,2},{4,3},{5,4},{6,5},{7,6},{8,7},{9,8},{10,9},{11,1... | collective-permute-start | bytes 49160 | tf_op jit(solution)/shard_map/ppermute | solution.py:20
  25.7 0.7 compare_select_fusion.8
  26.4 0.7 compare_select_fusion.6
  27.2 12.9 %collective-permute-start.2 = (bf16[1,80,512]{2,1,0:T(8,128)(2,1)S(1)}, bf16[1,80,512]{2,1,0:T(8,128)(2,1)S(1)}, u32[]{:S(2)}, u32[]{:S(2)}) collective-permute-start(bf16[1,80,512]{2,1,0:T(8,128)(2,1)S(1)} %get-tuple-element.2), channel_id=1, source_target_pairs={{0,64},{64,128},{128,192},{192,256},{256,320},{320,384},{384,448},... | collective-permute-start | bytes 245768 | tf_op jit(solution)/shard_map/ppermute | solution.py:19
  40.1 1.9 collective-permute-start.3
  42.1 4.0 %gather_fusion.1 = bf16[1024,512]{1,0:T(8,128)(2,1)S(1)} fusion(bf16[256,512]{1,0:T(8,128)(2,1)S(1)} %bitcast.69, s32[1024]{0:T(1024)S(1)} %broadcast_clamp_fusion.4), kind=kCustom, calls=%fused_computation.1 | custom fusion | bytes 2101248 | tf_op jit(solution)/shard_map/gather | solution.py:39
  46.1 11.2 %collective-permute-done.3 = bf16[1,80,512]{2,1,0:T(8,128)(2,1)S(1)} collective-permute-done((bf16[1,80,512]{2,1,0:T(8,128)(2,1)S(1)}, bf16[1,80,512]{2,1,0:T(8,128)(2,1)S(1)}, u32[]{:S(2)}, u32[]{:S(2)}) %collective-permute-start.3) | collective-permute-done | bytes 81952 | tf_op jit(solution)/shard_map/ppermute | solution.py:20
  57.3 4.0 %gather_fusion = bf16[1024,512]{1,0:T(8,128)(2,1)S(1)} fusion(bf16[320,512]{1,0:T(8,128)(2,1)S(1)} %bitcast.70, s32[1024]{0:T(1024)S(1)} %broadcast_clamp_fusion.5), kind=kCustom, calls=%fused_computation | custom fusion | bytes 2101248 | tf_op jit(solution)/shard_map/gather | solution.py:80
  61.3 1.2 multiply_reduce_fusion.1
  62.6 0.3 fusion
  62.9 1.0 convolution_convert_fusion.1
  64.1 4.0 %gather_fusion.3 = bf16[1024,512]{1,0:T(8,128)(2,1)S(1)} fusion(bf16[256,512]{1,0:T(8,128)(2,1)S(1)} %fusion, s32[1024]{0:T(1024)S(1)} %broadcast_clamp_fusion.3), kind=kCustom, calls=%fused_computation.3 | custom fusion | bytes 2101248 | tf_op jit(solution)/shard_map/gather | solution.py:39
  68.1 131.4 %all-gather.2.cloned.1.call-done = bf16[16384,512]{1,0:T(8,128)(2,1)} async-done(((bf16[256,512]{1,0:T(8,128)(2,1)}), bf16[16384,512]{1,0:T(8,128)(2,1)}) %all-gather.2.cloned.1.call-update) | async-done | bytes 16777232 | tf_op jit(solution)/shard_map/all_gather | solution.py:87
  199.5 11.9 %gather_fusion.2 = bf16[1024,512]{1,0:T(8,128)(2,1)S(1)} fusion(bf16[16384,512]{1,0:T(8,128)(2,1)} %all-gather.2.cloned.1.call-done, s32[1024]{0:T(1024)S(1)} %broadcast_clamp_fusion.2), kind=kCustom, calls=%fused_computation.2 | custom fusion | bytes 2101248 | tf_op jit(solution)/shard_map/gather | solution.py:89
  211.5 1.2 multiply_reduce_fusion
  212.7 0.3 fusion.1
  213.4 2.2 collective-permute-start.4
  215.5 12.1 %collective-permute-start.5 = (bf16[1,1,256,512]{3,2,1,0:T(8,128)(2,1)S(1)}, bf16[1,1,256,512]{3,2,1,0:T(8,128)(2,1)S(1)}, u32[]{:S(2)}, u32[]{:S(2)}) collective-permute-start(bf16[1,1,256,512]{3,2,1,0:T(8,128)(2,1)S(1)} %fusion.2), channel_id=1, source_target_pairs={{1,0},{2,1},{3,2},{4,3},{5,4},{6,5},{7,6},{8,7},{9,8},{10,9},{11,1... | collective-permute-start | bytes 786440 | tf_op jit(solution)/shard_map/ppermute | solution.py:20
  227.7 4.0 %gather_fusion.5 = bf16[1024,512]{1,0:T(8,128)(2,1)S(1)} fusion(bf16[128,512]{1,0:T(8,128)(2,1)S(1)} %bitcast.67, s32[1024]{0:T(1024)S(1)} %broadcast_clamp_fusion), kind=kCustom, calls=%fused_computation.5 | custom fusion | bytes 2101248 | tf_op jit(solution)/shard_map/gather | solution.py:39
  231.8 4.0 %gather_fusion.4 = bf16[1024,512]{1,0:T(8,128)(2,1)S(1)} fusion(bf16[768,512]{1,0:T(8,128)(2,1)S(1)} %bitcast.71, s32[1024]{0:T(1024)S(1)} %broadcast_clamp_fusion.1), kind=kCustom, calls=%fused_computation.4 | custom fusion | bytes 2101248 | tf_op jit(solution)/shard_map/gather | solution.py:100
  235.8 1.0 multiply_reduce_fusion.2
  236.8 0.9 fusion.3
  (52 shorter events, 0.8 us)
Async XLA Ops:
  7.2 55.4 %copy-start = (bf16[512,512]{1,0:T(8,128)(2,1)S(1)}, bf16[512,512]{1,0:T(8,128)(2,1)}, u32[]{:S(2)}) copy-start(bf16[512,512]{1,0:T(8,128)(2,1)} %param.17) | copy-start | bytes 1572868
  7.2 34.9 %copy-start.2 = (bf16[1,1,256,512]{3,2,1,0:T(8,128)(2,1)S(1)}, bf16[1,1,256,512]{3,2,1,0:T(8,128)(2,1)}, u32[]{:S(2)}) copy-start(bf16[1,1,256,512]{3,2,1,0:T(8,128)(2,1)} %param.15) | copy-start | bytes 786436
  7.2 192.3 %all-gather.2.cloned.1.call-start = ((), (), s32[]{:S(2)}) async-start(), calls=%async_computation | async-start | bytes 17039360 | tf_op jit(solution)/shard_map/all_gather | solution.py:87
  8.7 18.5 %collective-permute-start = (bf16[2,8,512]{2,1,0:T(8,128)(2,1)S(1)}, bf16[2,8,512]{2,1,0:T(8,128)(2,1)S(1)}, u32[]{:S(2)}, u32[]{:S(2)}) collective-permute-start(bf16[2,8,512]{2,1,0:T(8,128)(2,1)S(1)} %get-tuple-element.4), channel_id=1, source_target_pairs={{0,1},{1,2},{2,3},{3,4},{4,5},{5,6},{6,7},{7,8},{8,9},{9,10},{10,1... | collective-permute-start | bytes 49160 | tf_op jit(solution)/shard_map/ppermute | solution.py:19
  10.6 16.5 %collective-permute-start.1 = (bf16[2,8,512]{2,1,0:T(8,128)(2,1)S(1)}, bf16[2,8,512]{2,1,0:T(8,128)(2,1)S(1)}, u32[]{:S(2)}, u32[]{:S(2)}) collective-permute-start(bf16[2,8,512]{2,1,0:T(8,128)(2,1)S(1)} %get-tuple-element.5), channel_id=1, source_target_pairs={{1,0},{2,1},{3,2},{4,3},{5,4},{6,5},{7,6},{8,7},{9,8},{10,9},{11,1... | collective-permute-start | bytes 49160 | tf_op jit(solution)/shard_map/ppermute | solution.py:20
  27.2 18.9 %collective-permute-start.2 = (bf16[1,80,512]{2,1,0:T(8,128)(2,1)S(1)}, bf16[1,80,512]{2,1,0:T(8,128)(2,1)S(1)}, u32[]{:S(2)}, u32[]{:S(2)}) collective-permute-start(bf16[1,80,512]{2,1,0:T(8,128)(2,1)S(1)} %get-tuple-element.2), channel_id=1, source_target_pairs={{0,64},{64,128},{128,192},{192,256},{256,320},{320,384},{384,448},... | collective-permute-start | bytes 245768 | tf_op jit(solution)/shard_map/ppermute | solution.py:19
  40.1 17.2 %collective-permute-start.3 = (bf16[1,80,512]{2,1,0:T(8,128)(2,1)S(1)}, bf16[1,80,512]{2,1,0:T(8,128)(2,1)S(1)}, u32[]{:S(2)}, u32[]{:S(2)}) collective-permute-start(bf16[1,80,512]{2,1,0:T(8,128)(2,1)S(1)} %get-tuple-element.3), channel_id=1, source_target_pairs={{64,0},{128,64},{192,128},{256,192},{320,256},{384,320},{448,384},... | collective-permute-start | bytes 245768 | tf_op jit(solution)/shard_map/ppermute | solution.py:20
  57.3 4.0 %copy-start.8 = (s32[1,1,1024]{2,1,0:T(1,128)S(1)}, s32[1,1,1024]{2,1,0:T(1,128)}, u32[]{:S(2)}) copy-start(s32[1,1,1024]{2,1,0:T(1,128)} %param.23) | copy-start | bytes 12292
  61.3 1.6 copy-start.4
  62.5 1.5 copy-start.9
  62.5 1.5 copy-start.11
  62.5 1.5 copy-start.10
  62.5 1.6 copy-start.12
  211.5 1.2 copy-start.7
  211.5 1.6 copy-start.5
  212.6 15.0 %copy-start.1 = (bf16[2,64,512]{2,1,0:T(8,128)(2,1)S(1)}, bf16[2,64,512]{2,1,0:T(8,128)(2,1)}, u32[]{:S(2)}) copy-start(bf16[2,64,512]{2,1,0:T(8,128)(2,1)} %param.14) | copy-start | bytes 393220
  213.0 14.6 %copy-start.3 = (bf16[256,512]{1,0:T(8,128)(2,1)}, bf16[256,512]{1,0:T(8,128)(2,1)S(1)}, u32[]{:S(2)}) copy-start(bf16[256,512]{1,0:T(8,128)(2,1)S(1)} %fusion.1) | copy-start | bytes 786436
  213.4 18.3 %collective-permute-start.4 = (bf16[1,1,256,512]{3,2,1,0:T(8,128)(2,1)S(1)}, bf16[1,1,256,512]{3,2,1,0:T(8,128)(2,1)S(1)}, u32[]{:S(2)}, u32[]{:S(2)}) collective-permute-start(bf16[1,1,256,512]{3,2,1,0:T(8,128)(2,1)S(1)} %fusion.2), channel_id=1, source_target_pairs={{0,1},{1,2},{2,3},{3,4},{4,5},{5,6},{6,7},{7,8},{8,9},{9,10},{10,1... | collective-permute-start | bytes 786440 | tf_op jit(solution)/shard_map/ppermute | solution.py:19
  215.5 16.2 %collective-permute-start.5 = (bf16[1,1,256,512]{3,2,1,0:T(8,128)(2,1)S(1)}, bf16[1,1,256,512]{3,2,1,0:T(8,128)(2,1)S(1)}, u32[]{:S(2)}, u32[]{:S(2)}) collective-permute-start(bf16[1,1,256,512]{3,2,1,0:T(8,128)(2,1)S(1)} %fusion.2), channel_id=1, source_target_pairs={{1,0},{2,1},{3,2},{4,3},{5,4},{6,5},{7,6},{8,7},{9,8},{10,9},{11,1... | collective-permute-start | bytes 786440 | tf_op jit(solution)/shard_map/ppermute | solution.py:20
  235.8 1.0 copy-start.6
Sparse Core Ops, SparseCore 0:
  64.1 135.4 all-gather.1
where the time goes:
time: 245 us
  waiting for transfers between devices  143 us (58%)
  starting transfers between devices  46.1 us (19%)
  local copies, waits for them, and re-layouts  31.8 us (13%)
  between operations  14.5 us (6%)
  matrix products  7.67 us (3%)
    all_gather x1, waiting for transfers between devices, on_device(): band_table = lax.all_gather(mesh_table, 'gy', axis=0, tiled=True)  131 us
    ppermute x3, starting transfers between devices, padded(): after = lax.ppermute(initial, axis, down)  29.1 us
    ppermute x3, starting transfers between devices, padded(): before = lax.ppermute(last, axis, up)  17 us
    gather x1, local copies, waits for them, and re-layouts, on_device(): picked = band_table[owners * mesh_count + process_source.reshape(-1)]  11.9 us
    gather x3, local copies, waits for them, and re-layouts, aggregate(): messages = edge_messages(rows, targets[clamped])  11.9 us
    ppermute x3, waiting for transfers between devices, padded(): after = lax.ppermute(initial, axis, down)  11.2 us
  transfers between devices with their start and end apart: 7, of which 2 were waited for; matrix products, arithmetic and copies ran while one was open for 6% of the time, Pallas kernels for 0%

commit v1 on v0

v1 whole, which is shorter than its diff:
```python
import jax
import jax.numpy as jnp
from jax import lax
from jax.experimental import pallas as pl
from jax.experimental.pallas import tpu as pltpu
from jax.sharding import PartitionSpec as P

HALO = 8
EPSILON = 1e-05
LANES = 128
CHUNK = 256


def column(index, rows):
    parts = []
    for i in range(rows.start // LANES, rows.stop // LANES):
        row = jnp.broadcast_to(index[i : i + 1, :], (LANES, LANES))
        parts.append(row.T)
    return jnp.concatenate(parts, axis=0)


def pick(col, count):
    lane = lax.broadcasted_iota(jnp.int32, col.shape, 1)
    parts = [
        jnp.where(col == lane + k, 1.0, 0.0).astype(jnp.bfloat16)
        for k in range(0, count, LANES)
    ]
    return jnp.concatenate(parts, axis=1)


def spread(index, count):
    sub = lax.broadcasted_iota(jnp.int32, (count, LANES), 0)
    parts = [
        jnp.where(index[i : i + 1, :] == sub, 1.0, 0.0).astype(jnp.bfloat16)
        for i in range(index.shape[0])
    ]
    return jnp.concatenate(parts, axis=1)


def dot(a, b):
    return jnp.dot(a, b, preferred_element_type=jnp.float32)


def message(summed):
    half = 0.5 * summed
    return (half * jnp.tanh(half) + half).astype(jnp.bfloat16)


def refresh(latent, summed, weight):
    scaled = summed * lax.rsqrt(jnp.mean(summed * summed, axis=-1, keepdims=True) + EPSILON)
    return (latent.astype(jnp.float32) + dot(scaled.astype(jnp.bfloat16), weight)).astype(
        jnp.bfloat16
    )


def encode_kernel(
    grid, up, down, left, right, mesh, w_message, w_update, w_next,
    source, target, request, first_out, send_out, table, messages,
):
    w = w_message[...]
    cells = up.shape[0]
    inner = grid.shape[0]
    edge = left.shape[0]
    at = 0
    for ref, rows in ((up, cells), (grid, inner), (down, cells), (left, edge), (right, edge)):
        table[at : at + rows, :] = dot(ref[...], w).astype(jnp.bfloat16)
        at += rows
    pad = table.shape[0] - at
    table[at:, :] = jnp.zeros((pad, table.shape[1]), jnp.bfloat16)
    latent = mesh[...]
    nodes = latent.shape[0]
    src, tgt, req = source[...], target[...], request[...]
    edges = src.shape[0] * LANES
    for c in range(0, edges, CHUNK):
        rows = slice(c, c + CHUNK)
        acc = dot(pick(column(src, rows), table.shape[0]), table[...])
        acc = acc + dot(pick(column(tgt, rows), nodes), latent)
        messages[rows, :] = message(acc)
    summed = dot(spread(tgt, nodes), messages[...])
    first = refresh(latent, summed, w_update[...])
    first_out[...] = first
    following = dot(first, w_next[...]).astype(jnp.bfloat16)
    for c in range(0, edges, CHUNK):
        rows = slice(c, c + CHUNK)
        send_out[rows, :] = dot(pick(column(req, rows), nodes), following).astype(jnp.bfloat16)


def process_kernel(
    picked, first, w_update, w_next, target, second_out, table_out, messages
):
    latent = first[...]
    nodes = latent.shape[0]
    tgt = target[...]
    edges = tgt.shape[0] * LANES
    for c in range(0, edges, CHUNK):
        rows = slice(c, c + CHUNK)
        acc = dot(pick(column(tgt, rows), nodes), latent)
        messages[rows, :] = message(acc + picked[rows, :].astype(jnp.float32))
    summed = dot(spread(tgt, nodes), messages[...])
    second = refresh(latent, summed, w_update[...])
    second_out[...] = second
    table_out[...] = dot(second, w_next[...]).astype(jnp.bfloat16)


def decode_kernel(
    own, mate, other, grid, w_update, source, target, grid_out, messages
):
    latent = grid[...]
    cells = latent.shape[0]
    nodes = own.shape[0]
    src, tgt = source[...], target[...]
    edges = src.shape[0] * LANES
    for c in range(0, edges, CHUNK):
        rows = slice(c, c + CHUNK)
        col = column(src, rows)
        acc = dot(pick(column(tgt, rows), cells), latent)
        for at, ref in ((0, own), (nodes, mate), (2 * nodes, other)):
            acc = acc + dot(pick(col - at, nodes), ref[...])
        messages[rows, :] = message(acc)
    summed = dot(spread(tgt, cells), messages[...])
    grid_out[...] = refresh(latent, summed, w_update[...])


def on_device(
    grid_latent,
    mesh_latent,
    encode_message,
    encode_update,
    process_message,
    process_update,
    decode_message,
    decode_update,
    encode_source,
    encode_target,
    process_source,
    process_target,
    decode_source,
    decode_target,
):
    lat_rows, lon_cols, width = grid_latent.shape
    bands = lax.axis_size("gx")
    sectors = lax.axis_size("gy")
    lon_total = lon_cols * sectors
    band = lax.axis_index("gx")
    sector = lax.axis_index("gy")
    mesh_rows = mesh_latent.reshape(-1, width)
    nodes = mesh_rows.shape[0]
    grid_rows = grid_latent.reshape(-1, width)
    cells = grid_rows.shape[0]
    edges = encode_source.size
    bf16 = jnp.bfloat16
    params = pltpu.CompilerParams(vmem_limit_bytes=40 * 1024 * 1024)

    request = lax.all_to_all(
        process_source.reshape(sectors, -1), "gy", 0, 0, tiled=True
    ).reshape(-1, LANES)

    above = [(i, i + 1) for i in range(bands - 1)]
    below = [(i + 1, i) for i in range(bands - 1)]
    up = lax.ppermute(grid_latent[lat_rows - 1], "gx", above)
    down = lax.ppermute(grid_latent[0], "gx", below)
    tall = jnp.concatenate([up[None], grid_latent, down[None]])
    east = [(i, (i + 1) % sectors) for i in range(sectors)]
    west = [((i + 1) % sectors, i) for i in range(sectors)]
    left = lax.ppermute(tall[:, lon_cols - HALO :], "gy", east).reshape(-1, width)
    right = lax.ppermute(tall[:, :HALO], "gy", west).reshape(-1, width)

    source = encode_source.reshape(-1, LANES)
    lat = source // lon_total - band * lat_rows + 1
    lon = (source % lon_total - sector * lon_cols + HALO) % lon_total
    tall_cells = (lat_rows + 2) * lon_cols
    side = (lat_rows + 2) * HALO
    row = jnp.where(
        lon < HALO,
        tall_cells + lat * HALO + lon,
        jnp.where(
            lon < HALO + lon_cols,
            lat * lon_cols + lon - HALO,
            tall_cells + side + lat * HALO + lon - HALO - lon_cols,
        ),
    )
    depth = -(-(tall_cells + 2 * side) // LANES) * LANES
    first, send = pl.pallas_call(
        encode_kernel,
        out_shape=(
            jax.ShapeDtypeStruct((nodes, width), bf16),
            jax.ShapeDtypeStruct((edges, width), bf16),
        ),
        scratch_shapes=[pltpu.VMEM((depth, width), bf16), pltpu.VMEM((edges, width), bf16)],
        compiler_params=params,
    )(
        grid_rows, up, down, left, right, mesh_rows, encode_message, encode_update,
        process_message, row, encode_target.reshape(-1, LANES), request,
    )
    picked = lax.all_to_all(
        send.reshape(sectors, -1, width), "gy", 0, 0, tiled=True
    ).reshape(edges, width)
    second, table = pl.pallas_call(
        process_kernel,
        out_shape=(
            jax.ShapeDtypeStruct((nodes, width), bf16),
            jax.ShapeDtypeStruct((nodes, width), bf16),
        ),
        scratch_shapes=[pltpu.VMEM((edges, width), bf16)],
        compiler_params=params,
    )(picked, first, process_update, decode_message, process_target.reshape(-1, LANES))

    partner = [i + 1 if i % 2 else i - 1 for i in range(sectors)]
    other = lax.ppermute(table, "gy", [(i, partner[i] % sectors) for i in range(sectors)])
    mate = lax.ppermute(table, "gy", [(i, i ^ 1) for i in range(sectors)])
    source = decode_source.reshape(-1, LANES)
    owner = source // nodes % sectors
    piece = jnp.where(owner == sector, 0, jnp.where(owner == sector ^ 1, 1, 2))
    row = piece * nodes + source % nodes
    grid_output = pl.pallas_call(
        decode_kernel,
        out_shape=jax.ShapeDtypeStruct((cells, width), bf16),
        scratch_shapes=[pltpu.VMEM((edges, width), bf16)],
        compiler_params=params,
    )(table, mate, other, grid_rows, decode_update, row, decode_target.reshape(-1, LANES))
    return (
        grid_output.reshape(lat_rows, lon_cols, width),
        second.reshape(1, 1, nodes, width),
    )


def solution(mesh):
    edge = P("gx", "gy", None)
    return jax.shard_map(
        on_device,
        mesh=mesh,
        in_specs=(
            P("gx", "gy", None),
            P("gx", "gy", None, None),
            *([P()] * 6),
            *([edge] * 6),
        ),
        out_specs=(P("gx", "gy", None), P("gx", "gy", None, None)),
        check_vma=False,
    )
```

time: 245 us -> 146 us (0.60)
  waiting for transfers between devices: 143 us -> 15 us
  blocking collectives: 0 us -> 64.1 us
  local copies, waits for them, and re-layouts: 31.8 us -> 6.7 us
  between operations: 14.5 us -> 0.83 us
  Pallas kernels: 0 us -> 7.71 us
  matrix products: 7.67 us -> 0 us
  starting transfers between devices: 46.1 us -> 49.2 us
    all_gather x1 -> x0, waiting for transfers between devices: 131 us -> none  [on_device(): band_table = lax.all_gather(mesh_table, 'gy', axis=0, tiled=True)]
    all_to_all x0 -> x1, blocking collectives: none -> 64.1 us  [on_device(): lax.all_to_all(send.reshape(sectors, -1, width), 'gy', 0, 0, tiled=True)]
    gather x6 -> x0, local copies, waits for them, and re-layouts: 31.7 us -> none  [the longest x1 11.9 us: on_device(): picked = band_table[owners * mesh_count + process_source.reshape(-1)]]
    all_to_all x0 -> x1, starting transfers between devices: none -> 8.79 us  [on_device(): lax.all_to_all(process_source.reshape(sectors, -1), 'gy', 0, 0, tiled=True)]
    pallas_call x0 -> x3, Pallas kernels: none -> 7.71 us  [the longest x1 2.88 us: on_device(): pl.pallas_call(encode_kernel, out_shape=(jax.ShapeDtypeStruct((nodes, wid...]
    dot_general x9 -> x0, matrix products: 7.67 us -> none  [the longest x3 3.35 us: aggregate(): jnp.einsum('ec,ed->cd', onehot, messages, preferred_element_type=jnp.floa...]
    ppermute x6, starting transfers between devices: 46.1 us -> 40.4 us  [the longest x1 15.8 us: on_device(): up = lax.ppermute(grid_latent[lat_rows - 1], 'gx', above)]
    unnamed x26 -> x29, local copies, waits for them, and re-layouts: 0.09 us -> 5.05 us
  transfers between devices with their start and end apart: 7 -> 7, of which waited for: 2 -> 3; matrix products, arithmetic and copies ran while one was open for 6% -> 1% of each run, Pallas kernels for 0% -> 0%
where the time goes in v1:
time: 146 us; the launch traced here: 145 us
  blocking collectives  64.1 us (44%)
  starting transfers between devices  49.2 us (34%)
  waiting for transfers between devices  15 us (10%)
  Pallas kernels  7.71 us (5%)
  local copies, waits for them, and re-layouts  6.7 us (5%)
    all_to_all x1, blocking collectives, on_device(): lax.all_to_all(send.reshape(sectors, -1, width), 'gy', 0, 0, tiled=True)  64.1 us
    ppermute x1, starting transfers between devices, on_device(): up = lax.ppermute(grid_latent[lat_rows - 1], 'gx', above)  15.8 us
    ppermute x1, starting transfers between devices, on_device(): right = lax.ppermute(tall[:, :HALO], 'gy', west).reshape(-1, width)  12.4 us
    ppermute x1, waiting for transfers between devices, on_device(): lax.ppermute(table, 'gy', [(i, partner[i] % sectors) for i in range(secto...  9.96 us
    all_to_all x1, starting transfers between devices, on_device(): lax.all_to_all(process_source.reshape(sectors, -1), 'gy', 0, 0, tiled=True)  8.79 us
    ppermute x1, starting transfers between devices, on_device(): lax.ppermute(table, 'gy', [(i, partner[i] % sectors) for i in range(secto...  6.37 us
    unnamed x29, local copies, waits for them, and re-layouts  5.05 us
    ppermute x1, waiting for transfers between devices, on_device(): down = lax.ppermute(grid_latent[0], 'gx', below)  4.36 us
  transfers between devices with their start and end apart: 7, of which 3 were waited for; matrix products, arithmetic and copies ran while one was open for 1% of the time, Pallas kernels for 0%

profile of v1, /device:TPU:6, one launch (start us, length us, event | category | flops | bytes accessed | tf_op | source)
XLA Modules:
  0.0 145.0 jit_solution(14971440200437850744)
XLA Ops:
  0.6 0.9 slice_bitcast_fusion
  1.5 15.8 %collective-permute-start = (bf16[64,512]{1,0:T(8,128)(2,1)S(1)}, bf16[64,512]{1,0:T(8,128)(2,1)S(1)}, u32[]{:S(2)}, u32[]{:S(2)}) collective-permute-start(bf16[64,512]{1,0:T(8,128)(2,1)S(1)} %get-tuple-element.13), channel_id=1, source_target_pairs={{0,64},{64,128},{128,192},{192,256},{256,320},{320,384},{384,448},... | collective-permute-start | bytes 196616 | tf_op jit(solution)/shard_map/ppermute | solution.py:160
  17.3 1.9 %collective-permute-start.1 = (bf16[64,512]{1,0:T(8,128)(2,1)S(1)}, bf16[64,512]{1,0:T(8,128)(2,1)S(1)}, u32[]{:S(2)}, u32[]{:S(2)}) collective-permute-start(bf16[64,512]{1,0:T(8,128)(2,1)S(1)} %get-tuple-element.12), channel_id=1, source_target_pairs={{64,0},{128,64},{192,128},{256,192},{320,256},{384,320},{448,384},... | collective-permute-start | bytes 196616 | tf_op jit(solution)/shard_map/ppermute | solution.py:161
  19.2 0.5 broadcast.65
  19.8 0.7 reduce.6
  20.4 0.7 all_to_all.9
  21.1 8.8 %all-to-all-start = ((s32[64,1,16]{2,1,0:T(1,128)}), s32[64,1,16]{2,1,0:T(1,128)S(1)}, u32[]{:S(2)}, u32[]{:S(2)}) async-start(s32[64,1,16]{2,1,0:T(1,128)} %bitcast.10), calls=%async_computation | async-start | bytes 65536 | tf_op jit(solution)/shard_map/all_to_all | solution.py:154
  29.9 4.4 %collective-permute-done.1.down = bf16[64,512]{1,0:T(8,128)(2,1)S(1)} collective-permute-done((bf16[64,512]{1,0:T(8,128)(2,1)S(1)}, bf16[64,512]{1,0:T(8,128)(2,1)S(1)}, u32[]{:S(2)}, u32[]{:S(2)}) %collective-permute-start.1) | collective-permute-done | bytes 65568 | tf_op jit(solution)/shard_map/ppermute | solution.py:161
  34.3 1.9 %collective-permute-start.2 = (bf16[4,8,512]{2,1,0:T(8,128)(2,1)S(1)}, bf16[4,8,512]{2,1,0:T(8,128)(2,1)S(1)}, u32[]{:S(2)}, u32[]{:S(2)}) collective-permute-start(bf16[4,8,512]{2,1,0:T(8,128)(2,1)S(1)} %get-tuple-element.11), channel_id=1, source_target_pairs={{0,1},{1,2},{2,3},{3,4},{4,5},{5,6},{6,7},{7,8},{8,9},{9,10},{10,1... | collective-permute-start | bytes 98312 | tf_op jit(solution)/shard_map/ppermute | solution.py:165
  36.3 12.4 %collective-permute-start.3 = (bf16[4,8,512]{2,1,0:T(8,128)(2,1)S(1)}, bf16[4,8,512]{2,1,0:T(8,128)(2,1)S(1)}, u32[]{:S(2)}, u32[]{:S(2)}) collective-permute-start(bf16[4,8,512]{2,1,0:T(8,128)(2,1)S(1)} %get-tuple-element.10), channel_id=1, source_target_pairs={{1,0},{2,1},{3,2},{4,3},{5,4},{6,5},{7,6},{8,7},{9,8},{10,9},{11,1... | collective-permute-start | bytes 98312 | tf_op jit(solution)/shard_map/ppermute | solution.py:166
  48.7 0.7 reduce.7
  49.5 0.7 collective-permute-done.3
  50.2 0.7 copy-done.8
  50.9 1.0 copy-done.2
  51.9 1.0 copy-done.3
  53.0 1.0 copy-done.4
  54.0 2.9 %shard_map.149 = (bf16[256,512]{1,0:T(8,128)(2,1)S(1)}, bf16[1024,512]{1,0:T(8,128)(2,1)S(1)}) custom-call(bf16[128,512]{1,0:T(8,128)(2,1)S(1)} %bitcast.21, bf16[64,512]{1,0:T(8,128)(2,1)S(1)} %collective-permute-done.up, bf16[64,512]{1,0:T(8,128)(2,1)S(1)} %collective-permute-done.1.down, bf16[32,512]{1,0:T(8,128)(2,1)S(1)} %bitcast.27, ...), custom_call_target="tpu_custom_call" | custom-call | tf_op jit(solution)/shard_map/pallas_call | solution.py:183
  56.9 64.1 %all_to_all.14 = bf16[64,16,512]{2,1,0:T(8,128)(2,1)S(1)} all-to-all(bf16[64,16,512]{2,1,0:T(8,128)(2,1)S(1)} %bitcast.23), channel_id=1, replica_groups=mesh['gx'=8,'gy'=64] {'gy'}, dimensions={0} | all-to-all | bytes 2097152 | tf_op jit(solution)/shard_map/all_to_all | solution.py:195
  121.0 0.7 copy-done.9
  121.7 2.2 %shard_map.150 = (bf16[256,512]{1,0:T(8,128)(2,1)}, bf16[256,512]{1,0:T(8,128)(2,1)S(1)}) custom-call(bf16[1024,512]{1,0:T(8,128)(2,1)S(1)} %bitcast.20, bf16[256,512]{1,0:T(8,128)(2,1)S(1)} %get-tuple-element.7.first, bf16[512,512]{1,0:T(8,128)(2,1)S(1)} %copy-done.5, bf16[512,512]{1,0:T(8,128)(2,1)S(1)} %copy-done.6, s32[8,128]{1,0:T(8,128)S(1)} %bitcast.30), custom_call_target="tpu_custom_call" | custom-call | tf_op jit(solution)/shard_map/pallas_call | solution.py:198
  123.9 2.0 %collective-permute-start.4 = (bf16[256,512]{1,0:T(8,128)(2,1)S(1)}, bf16[256,512]{1,0:T(8,128)(2,1)S(1)}, u32[]{:S(2)}, u32[]{:S(2)}) collective-permute-start(bf16[256,512]{1,0:T(8,128)(2,1)S(1)} %get-tuple-element.8.own), channel_id=1, source_target_pairs={{0,1},{1,0},{2,3},{3,2},{4,5},{5,4},{6,7},{7,6},{8,9},{9,8},{10,11... | collective-permute-start | bytes 786440 | tf_op jit(solution)/shard_map/ppermute | solution.py:210
  126.0 6.4 %collective-permute-start.5 = (bf16[256,512]{1,0:T(8,128)(2,1)S(1)}, bf16[256,512]{1,0:T(8,128)(2,1)S(1)}, u32[]{:S(2)}, u32[]{:S(2)}) collective-permute-start(bf16[256,512]{1,0:T(8,128)(2,1)S(1)} %get-tuple-element.8.own), channel_id=1, source_target_pairs={{0,63},{1,2},{2,1},{3,4},{4,3},{5,6},{6,5},{7,8},{8,7},{9,10},{10,... | collective-permute-start | bytes 786440 | tf_op jit(solution)/shard_map/ppermute | solution.py:209
  132.4 10.0 %collective-permute-done.5.other = bf16[256,512]{1,0:T(8,128)(2,1)S(1)} collective-permute-done((bf16[256,512]{1,0:T(8,128)(2,1)S(1)}, bf16[256,512]{1,0:T(8,128)(2,1)S(1)}, u32[]{:S(2)}, u32[]{:S(2)}) %collective-permute-start.5) | collective-permute-done | bytes 262176 | tf_op jit(solution)/shard_map/ppermute | solution.py:209
  142.4 2.6 %shard_map.151 = bf16[128,512]{1,0:T(8,128)(2,1)} custom-call(bf16[256,512]{1,0:T(8,128)(2,1)S(1)} %get-tuple-element.8.own, bf16[256,512]{1,0:T(8,128)(2,1)S(1)} %collective-permute-done.4.mate, bf16[256,512]{1,0:T(8,128)(2,1)S(1)} %collective-permute-done.5.other, bf16[128,512]{1,0:T(8,128)(2,1)S(1)} %bitcast.22, bf16[512,512]{1,0:T(8,128)(2,1)S(1)} %copy-done.1, ...), custom_call_target="tpu_custom_call" | custom-call | tf_op jit(solution)/shard_map/pallas_call | solution.py:215
  (31 shorter events, 0.2 us)
Async XLA Ops:
  0.6 19.1 %copy-start.11 = (s32[1,1,1024]{2,1,0:T(1,128)S(1)}, s32[1,1,1024]{2,1,0:T(1,128)}, u32[]{:S(2)}) copy-start(s32[1,1,1024]{2,1,0:T(1,128)} %param.24) | copy-start | bytes 12292
  1.5 32.8 %copy-start = (bf16[2,64,512]{2,1,0:T(8,128)(2,1)S(1)}, bf16[2,64,512]{2,1,0:T(8,128)(2,1)}, u32[]{:S(2)}) copy-start(bf16[2,64,512]{2,1,0:T(8,128)(2,1)} %param.14) | copy-start | bytes 393220
  1.5 28.4 %collective-permute-start = (bf16[64,512]{1,0:T(8,128)(2,1)S(1)}, bf16[64,512]{1,0:T(8,128)(2,1)S(1)}, u32[]{:S(2)}, u32[]{:S(2)}) collective-permute-start(bf16[64,512]{1,0:T(8,128)(2,1)S(1)} %get-tuple-element.13), channel_id=1, source_target_pairs={{0,64},{64,128},{128,192},{192,256},{256,320},{320,384},{384,448},... | collective-permute-start | bytes 196616 | tf_op jit(solution)/shard_map/ppermute | solution.py:160
  17.3 17.0 %collective-permute-start.1 = (bf16[64,512]{1,0:T(8,128)(2,1)S(1)}, bf16[64,512]{1,0:T(8,128)(2,1)S(1)}, u32[]{:S(2)}, u32[]{:S(2)}) collective-permute-start(bf16[64,512]{1,0:T(8,128)(2,1)S(1)} %get-tuple-element.12), channel_id=1, source_target_pairs={{64,0},{128,64},{192,128},{256,192},{320,256},{384,320},{448,384},... | collective-permute-start | bytes 196616 | tf_op jit(solution)/shard_map/ppermute | solution.py:161
  21.1 29.1 %copy-start.7 = (bf16[1,1,256,512]{3,2,1,0:T(8,128)(2,1)S(1)}, bf16[1,1,256,512]{3,2,1,0:T(8,128)(2,1)}, u32[]{:S(2)}) copy-start(bf16[1,1,256,512]{3,2,1,0:T(8,128)(2,1)} %param.15) | copy-start | bytes 786436
  21.1 27.5 %all-to-all-start = ((s32[64,1,16]{2,1,0:T(1,128)}), s32[64,1,16]{2,1,0:T(1,128)S(1)}, u32[]{:S(2)}, u32[]{:S(2)}) async-start(s32[64,1,16]{2,1,0:T(1,128)} %bitcast.10), calls=%async_computation | async-start | bytes 65536 | tf_op jit(solution)/shard_map/all_to_all | solution.py:154
  34.3 14.3 %copy-start.12 = (s32[1,1,1024]{2,1,0:T(1,128)S(1)}, s32[1,1,1024]{2,1,0:T(1,128)}, u32[]{:S(2)}) copy-start(s32[1,1,1024]{2,1,0:T(1,128)} %param.22) | copy-start | bytes 12292
  34.3 15.2 %collective-permute-start.2 = (bf16[4,8,512]{2,1,0:T(8,128)(2,1)S(1)}, bf16[4,8,512]{2,1,0:T(8,128)(2,1)S(1)}, u32[]{:S(2)}, u32[]{:S(2)}) collective-permute-start(bf16[4,8,512]{2,1,0:T(8,128)(2,1)S(1)} %get-tuple-element.11), channel_id=1, source_target_pairs={{0,1},{1,2},{2,3},{3,4},{4,5},{5,6},{6,7},{7,8},{8,9},{9,10},{10,1... | collective-permute-start | bytes 98312 | tf_op jit(solution)/shard_map/ppermute | solution.py:165
  36.3 13.9 %collective-permute-start.3 = (bf16[4,8,512]{2,1,0:T(8,128)(2,1)S(1)}, bf16[4,8,512]{2,1,0:T(8,128)(2,1)S(1)}, u32[]{:S(2)}, u32[]{:S(2)}) collective-permute-start(bf16[4,8,512]{2,1,0:T(8,128)(2,1)S(1)} %get-tuple-element.10), channel_id=1, source_target_pairs={{1,0},{2,1},{3,2},{4,3},{5,4},{6,5},{7,6},{8,7},{9,8},{10,9},{11,1... | collective-permute-start | bytes 98312 | tf_op jit(solution)/shard_map/ppermute | solution.py:166
  50.2 0.7 copy-start.8
  50.9 1.0 copy-start.2
  51.9 1.0 copy-start.3
  53.0 1.0 copy-start.4
  56.9 64.1 %copy-start.5 = (bf16[512,512]{1,0:T(8,128)(2,1)S(1)}, bf16[512,512]{1,0:T(8,128)(2,1)}, u32[]{:S(2)}) copy-start(bf16[512,512]{1,0:T(8,128)(2,1)} %w_update.4) | copy-start | bytes 1572868
  56.9 64.1 %copy-start.6 = (bf16[512,512]{1,0:T(8,128)(2,1)S(1)}, bf16[512,512]{1,0:T(8,128)(2,1)}, u32[]{:S(2)}) copy-start(bf16[512,512]{1,0:T(8,128)(2,1)} %w_next.3) | copy-start | bytes 1572868
  121.0 0.7 copy-start.9
  121.7 20.7 %copy-start.1 = (bf16[512,512]{1,0:T(8,128)(2,1)S(1)}, bf16[512,512]{1,0:T(8,128)(2,1)}, u32[]{:S(2)}) copy-start(bf16[512,512]{1,0:T(8,128)(2,1)} %w_update.5) | copy-start | bytes 1572868
  123.9 8.4 %copy-start.13 = (s32[1,1,1024]{2,1,0:T(1,128)S(1)}, s32[1,1,1024]{2,1,0:T(1,128)}, u32[]{:S(2)}) copy-start(s32[1,1,1024]{2,1,0:T(1,128)} %param.26) | copy-start | bytes 12292
  123.9 8.5 %collective-permute-start.4 = (bf16[256,512]{1,0:T(8,128)(2,1)S(1)}, bf16[256,512]{1,0:T(8,128)(2,1)S(1)}, u32[]{:S(2)}, u32[]{:S(2)}) collective-permute-start(bf16[256,512]{1,0:T(8,128)(2,1)S(1)} %get-tuple-element.8.own), channel_id=1, source_target_pairs={{0,1},{1,0},{2,3},{3,2},{4,5},{5,4},{6,7},{7,6},{8,9},{9,8},{10,11... | collective-permute-start | bytes 786440 | tf_op jit(solution)/shard_map/ppermute | solution.py:210
  126.0 16.4 %collective-permute-start.5 = (bf16[256,512]{1,0:T(8,128)(2,1)S(1)}, bf16[256,512]{1,0:T(8,128)(2,1)S(1)}, u32[]{:S(2)}, u32[]{:S(2)}) collective-permute-start(bf16[256,512]{1,0:T(8,128)(2,1)S(1)} %get-tuple-element.8.own), channel_id=1, source_target_pairs={{0,63},{1,2},{2,1},{3,4},{4,3},{5,6},{6,5},{7,8},{8,7},{9,10},{10,... | collective-permute-start | bytes 786440 | tf_op jit(solution)/shard_map/ppermute | solution.py:209
  132.4 10.0 %copy-start.10 = (s32[1,1,1024]{2,1,0:T(1,128)S(1)}, s32[1,1,1024]{2,1,0:T(1,128)}, u32[]{:S(2)}) copy-start(s32[1,1,1024]{2,1,0:T(1,128)} %param.27) | copy-start | bytes 12292

commit v2 on v1

v2 whole, which is shorter than its diff:
```python
import jax
import jax.numpy as jnp
from jax import lax
from jax.experimental import pallas as pl
from jax.experimental.pallas import tpu as pltpu
from jax.sharding import PartitionSpec as P

HALO = 8
LON_DEV = 64
EPSILON = 1e-05
LANES = 128
CHUNK = 256


def column(index, rows):
    parts = []
    for i in range(rows.start // LANES, rows.stop // LANES):
        row = jnp.broadcast_to(index[i : i + 1, :], (LANES, LANES))
        parts.append(row.T)
    return jnp.concatenate(parts, axis=0)


def pick(col, count):
    lane = lax.broadcasted_iota(jnp.int32, col.shape, 1)
    parts = [
        jnp.where(col == lane + k, 1.0, 0.0).astype(jnp.bfloat16)
        for k in range(0, count, LANES)
    ]
    return jnp.concatenate(parts, axis=1)


def spread(index, count):
    sub = lax.broadcasted_iota(jnp.int32, (count, LANES), 0)
    parts = [
        jnp.where(index[i : i + 1, :] == sub, 1.0, 0.0).astype(jnp.bfloat16)
        for i in range(index.shape[0])
    ]
    return jnp.concatenate(parts, axis=1)


def dot(a, b):
    return jnp.dot(a, b, preferred_element_type=jnp.float32)


def message(summed):
    half = 0.5 * summed
    return (half * jnp.tanh(half) + half).astype(jnp.bfloat16)


def refresh(latent, summed, weight):
    scaled = summed * lax.rsqrt(jnp.mean(summed * summed, axis=-1, keepdims=True) + EPSILON)
    return (latent.astype(jnp.float32) + dot(scaled.astype(jnp.bfloat16), weight)).astype(
        jnp.bfloat16
    )


def log2(value):
    assert value & (value - 1) == 0
    return value.bit_length() - 1


def edges_kernel(grid, slots, far_out, near_out, slots_out, held, sems):
    even = lax.rem(lax.axis_index("gx"), 2) == 0
    last = grid.shape[0] - 1
    near = pltpu.make_async_copy(grid.at[jnp.where(even, last, 0)], near_out, sems.at[0])
    far = pltpu.make_async_copy(grid.at[jnp.where(even, 0, last)], far_out, sems.at[1])
    index = pltpu.make_async_copy(slots, held, sems.at[2])
    index.start()
    near.start()
    far.start()
    count = held.shape[0]
    groups = slots_out.shape[0] // count
    cap = LANES // groups
    index.wait()
    for g in range(groups):
        moved = pltpu.roll(held[...], LANES - g * cap, 1) if g else held[...]
        slots_out[pl.ds(g, count, stride=groups), :] = moved
    near.wait()
    far.wait()


def sides_kernel(far, grid, near, slots, far_out, near_out, slots_out, held, sems):
    even = lax.rem(lax.axis_index("gy"), 2) == 0
    lats, lons, _ = grid.shape
    west = pltpu.make_async_copy(grid.at[:, :HALO], held.at[0], sems.at[0])
    east = pltpu.make_async_copy(grid.at[:, lons - HALO :], held.at[1], sems.at[1])
    west.start()
    east.start()
    count = slots_out.shape[0]
    groups = slots.shape[0] // count
    cap = LANES // groups
    lane = lax.broadcasted_iota(jnp.int32, slots_out.shape, 1)
    kept = jnp.zeros_like(lane)
    for g in range(groups):
        part = slots[pl.ds(g, count, stride=groups), :]
        moved = pltpu.roll(part, g * cap, 1) if g else part
        kept = jnp.where((lane >= g * cap) & (lane < (g + 1) * cap), moved, kept)
    slots_out[...] = kept
    west.wait()
    east.wait()

    def put(out, side):
        out[0] = near[side, :]
        for i in range(lats):
            out[i + 1] = held[0 if side.start == 0 else 1, i]
        out[lats + 1] = far[side, :]

    first, last = slice(0, HALO), slice(lons - HALO, lons)

    @pl.when(even)
    def _():
        put(near_out, last)
        put(far_out, first)

    @pl.when(jnp.logical_not(even))
    def _():
        put(near_out, first)
        put(far_out, last)


def places(source, lats, lons):
    band, sector = lax.axis_index("gx"), lax.axis_index("gy")
    lon_total = lons * lax.axis_size("gy")
    lat = (source >> log2(lon_total)) - band * lats + 1
    outer = (lat == 0) | (lat == lats + 1)
    lat = jnp.where(outer & (lax.rem(band, 2) == 0), lats + 1 - lat, lat)
    lon = ((source & (lon_total - 1)) - sector * lons + HALO) & (lon_total - 1)
    inner = (lon >= HALO) & (lon < HALO + lons)
    return lat, lon, inner


def gather_kernel(
    far, grid, near, mesh, w_message, w_update, w_next, source, target,
    partial, spread_out, mesh_out, w_out, held, source_held, target_held, table, sems,
):
    pairs = [(source, source_held), (target, target_held)]
    pairs += [(grid, held), (w_message, w_out.at[0]), (mesh, mesh_out)]
    pairs += [(w_update, w_out.at[1]), (w_next, w_out.at[2])]
    copies = [pltpu.make_async_copy(a, b, sems.at[i]) for i, (a, b) in enumerate(pairs)]
    for copy in copies:
        copy.start()
    lats, lons, width = grid.shape
    nodes = mesh.shape[0]
    copies[0].wait()
    copies[1].wait()
    lat, lon, inner = places(source_held[...], lats, lons)
    src = jnp.where(inner, lat * lons + lon - HALO, -1)
    tgt = target_held[...]
    edges = src.shape[0] * LANES
    spread_out[...] = spread(tgt, nodes)
    copies[2].wait()
    copies[3].wait()
    w = w_out[0]
    table[:lons, :] = dot(near[...], w).astype(jnp.bfloat16)
    inside = held[...].reshape(lats * lons, width)
    table[lons : (lats + 1) * lons, :] = dot(inside, w).astype(jnp.bfloat16)
    table[(lats + 1) * lons :, :] = dot(far[...], w).astype(jnp.bfloat16)
    copies[4].wait()
    depth = table.shape[0]
    for c in range(0, edges, CHUNK):
        rows = slice(c, c + CHUNK)
        acc = dot(pick(column(src, rows), depth), table[...])
        partial[rows, :] = acc + dot(pick(column(tgt, rows), nodes), mesh_out[...])
    copies[5].wait()
    copies[6].wait()


def encode_kernel(
    partial, other, mate, spreading, mesh, weights, source, request,
    first_out, send_out, table, messages,
):
    w = weights[0]
    tall, halo, width = mate.shape
    side = tall * halo
    table[:side, :] = dot(mate[...].reshape(side, width), w).astype(jnp.bfloat16)
    table[side : 2 * side, :] = dot(other[...].reshape(side, width), w).astype(jnp.bfloat16)
    depth = table.shape[0]
    table[2 * side :, :] = jnp.zeros((depth - 2 * side, width), jnp.bfloat16)
    nodes = mesh.shape[0]
    lons = LON_DEV
    lat, lon, inner = places(source[...], tall - 2, lons)
    on_mate = (lon >= HALO) == (lax.rem(lax.axis_index("gy"), 2) == 0)
    src = jnp.where(on_mate, 0, side) + lat * halo + (lon & (halo - 1))
    src = jnp.where(inner, -1, src)
    req = request[...]
    edges = src.shape[0] * LANES
    for c in range(0, edges, CHUNK):
        rows = slice(c, c + CHUNK)
        acc = dot(pick(column(src, rows), depth), table[...])
        messages[rows, :] = message(partial[rows, :] + acc)
    summed = dot(spreading[...], messages[...])
    first = refresh(mesh[...], summed, weights[1])
    first_out[...] = first
    following = dot(first, weights[2]).astype(jnp.bfloat16)
    for c in range(0, edges, CHUNK):
        rows = slice(c, c + CHUNK)
        send_out[rows, :] = dot(pick(column(req, rows), nodes), following).astype(jnp.bfloat16)


def process_kernel(
    picked, first, w_update, w_next, target, second_out, table_out, messages
):
    latent = first[...]
    nodes = latent.shape[0]
    tgt = target[...]
    edges = tgt.shape[0] * LANES
    for c in range(0, edges, CHUNK):
        rows = slice(c, c + CHUNK)
        acc = dot(pick(column(tgt, rows), nodes), latent)
        messages[rows, :] = message(acc + picked[rows, :].astype(jnp.float32))
    summed = dot(spread(tgt, nodes), messages[...])
    second = refresh(latent, summed, w_update[...])
    second_out[...] = second
    table_out[...] = dot(second, w_next[...]).astype(jnp.bfloat16)


def reach_kernel(own, grid, source, target, partial):
    latent = grid[...]
    cells = latent.shape[0]
    nodes = own.shape[0]
    src, tgt = source[...], target[...]
    edges = src.shape[0] * LANES
    for c in range(0, edges, CHUNK):
        rows = slice(c, c + CHUNK)
        acc = dot(pick(column(tgt, rows), cells), latent)
        partial[rows, :] = acc + dot(pick(column(src, rows), nodes), own[...])


def decode_kernel(
    partial, other, mate, grid, w_update, source, target, grid_out, messages
):
    latent = grid[...]
    cells = latent.shape[0]
    nodes = mate.shape[0]
    src, tgt = source[...], target[...]
    edges = src.shape[0] * LANES
    for c in range(0, edges, CHUNK):
        rows = slice(c, c + CHUNK)
        col = column(src, rows)
        acc = partial[rows, :]
        for at, ref in ((nodes, mate), (2 * nodes, other)):
            acc = acc + dot(pick(col - at, nodes), ref[...])
        messages[rows, :] = message(acc)
    summed = dot(spread(tgt, cells), messages[...])
    grid_out[...] = refresh(latent, summed, w_update[...])


def on_device(
    grid_latent,
    mesh_latent,
    encode_message,
    encode_update,
    process_message,
    process_update,
    decode_message,
    decode_update,
    encode_source,
    encode_target,
    process_source,
    process_target,
    decode_source,
    decode_target,
):
    lat_rows, lon_cols, width = grid_latent.shape
    bands = lax.axis_size("gx")
    sectors = lax.axis_size("gy")
    sector = lax.axis_index("gy")
    mesh_rows = mesh_latent.reshape(-1, width)
    nodes = mesh_rows.shape[0]
    grid_rows = grid_latent.reshape(-1, width)
    cells = grid_rows.shape[0]
    edges = encode_source.size
    bf16 = jnp.bfloat16
    params = pltpu.CompilerParams(vmem_limit_bytes=40 * 1024 * 1024)
    hbm = pl.BlockSpec(memory_space=pltpu.HBM)
    vmem = pl.BlockSpec(memory_space=pltpu.VMEM)
    assert lon_cols == LON_DEV

    def pinned(array):
        return pltpu.with_memory_space_constraint(array, pltpu.HBM)

    partner = [i + 1 if i % 2 else i - 1 for i in range(max(bands, sectors))]
    far_bands = [(i, partner[i]) for i in range(1, bands - 1)]
    near_bands = [(i, i ^ 1) for i in range(bands)]
    far_sectors = [(i, partner[i] % sectors) for i in range(sectors)]
    near_sectors = [(i, i ^ 1) for i in range(sectors)]

    band_edge = jax.ShapeDtypeStruct((lon_cols, width), bf16)
    far, near, slots = pl.pallas_call(
        edges_kernel,
        in_specs=[hbm, hbm],
        out_specs=(vmem,) * 3,
        out_shape=(band_edge, band_edge, jax.ShapeDtypeStruct((sectors, LANES), jnp.int32)),
        scratch_shapes=[
            pltpu.VMEM((edges // LANES, LANES), jnp.int32),
            pltpu.SemaphoreType.DMA((3,)),
        ],
        compiler_params=params,
    )(pinned(grid_latent), pinned(process_source.reshape(-1, LANES)))
    far = lax.ppermute(far, "gx", far_bands)
    near = lax.ppermute(near, "gx", near_bands)
    slots = lax.all_to_all(slots, "gy", 0, 0, tiled=True)
    sector_edge = jax.ShapeDtypeStruct((lat_rows + 2, HALO, width), bf16)
    other, mate, request = pl.pallas_call(
        sides_kernel,
        in_specs=[vmem, hbm, vmem, vmem],
        out_specs=(vmem,) * 3,
        out_shape=(
            sector_edge, sector_edge, jax.ShapeDtypeStruct((edges // LANES, LANES), jnp.int32)
        ),
        scratch_shapes=[
            pltpu.VMEM((2, lat_rows, HALO, width), bf16),
            pltpu.SemaphoreType.DMA((2,)),
        ],
        compiler_params=params,
    )(far, pinned(grid_latent), near, slots)
    other = lax.ppermute(other, "gy", far_sectors)
    mate = lax.ppermute(mate, "gy", near_sectors)

    source = encode_source.reshape(-1, LANES)
    tall_cells = (lat_rows + 2) * lon_cols
    side = (lat_rows + 2) * HALO
    partial, spreading, mesh_held, weights = pl.pallas_call(
        gather_kernel,
        in_specs=[vmem, hbm, vmem] + [hbm] * 6,
        out_specs=(vmem,) * 4,
        out_shape=(
            jax.ShapeDtypeStruct((edges, width), jnp.float32),
            jax.ShapeDtypeStruct((nodes, edges), bf16),
            jax.ShapeDtypeStruct((nodes, width), bf16),
            jax.ShapeDtypeStruct((3, width, width), bf16),
        ),
        scratch_shapes=[
            pltpu.VMEM((lat_rows, lon_cols, width), bf16),
            pltpu.VMEM((edges // LANES, LANES), jnp.int32),
            pltpu.VMEM((edges // LANES, LANES), jnp.int32),
            pltpu.VMEM((tall_cells, width), bf16),
            pltpu.SemaphoreType.DMA((7,)),
        ],
        compiler_params=params,
    )(
        far, pinned(grid_latent), near, pinned(mesh_rows), pinned(encode_message),
        pinned(encode_update), pinned(process_message),
        pinned(source), pinned(encode_target.reshape(-1, LANES)),
    )
    first, send = pl.pallas_call(
        encode_kernel,
        out_shape=(
            jax.ShapeDtypeStruct((nodes, width), bf16),
            jax.ShapeDtypeStruct((edges, width), bf16),
        ),
        scratch_shapes=[
            pltpu.VMEM((-(-2 * side // LANES) * LANES, width), bf16),
            pltpu.VMEM((edges, width), bf16),
        ],
        compiler_params=params,
    )(partial, other, mate, spreading, mesh_held, weights, source, request)
    picked = lax.all_to_all(
        send.reshape(sectors, -1, width), "gy", 0, 0, tiled=True
    ).reshape(edges, width)
    second, table = pl.pallas_call(
        process_kernel,
        out_shape=(
            jax.ShapeDtypeStruct((nodes, width), bf16),
            jax.ShapeDtypeStruct((nodes, width), bf16),
        ),
        scratch_shapes=[pltpu.VMEM((edges, width), bf16)],
        compiler_params=params,
    )(picked, first, process_update, decode_message, process_target.reshape(-1, LANES))

    other = lax.ppermute(table, "gy", far_sectors)
    mate = lax.ppermute(table, "gy", near_sectors)
    source = decode_source.reshape(-1, LANES)
    owner = source // nodes % sectors
    piece = jnp.where(owner == sector, 0, jnp.where(owner == sector ^ 1, 1, 2))
    row = piece * nodes + source % nodes
    target = decode_target.reshape(-1, LANES)
    partial = pl.pallas_call(
        reach_kernel,
        out_shape=jax.ShapeDtypeStruct((edges, width), jnp.float32),
        compiler_params=params,
    )(table, grid_rows, row, target)
    grid_output = pl.pallas_call(
        decode_kernel,
        out_shape=jax.ShapeDtypeStruct((cells, width), bf16),
        scratch_shapes=[pltpu.VMEM((edges, width), bf16)],
        compiler_params=params,
    )(partial, other, mate, grid_rows, decode_update, row, target)
    return (
        grid_output.reshape(lat_rows, lon_cols, width),
        second.reshape(1, 1, nodes, width),
    )


def solution(mesh):
    edge = P("gx", "gy", None)
    return jax.shard_map(
        on_device,
        mesh=mesh,
        in_specs=(
            P("gx", "gy", None),
            P("gx", "gy", None, None),
            *([P()] * 6),
            *([edge] * 6),
        ),
        out_specs=(P("gx", "gy", None), P("gx", "gy", None, None)),
        check_vma=False,
    )
```

time: 146 us -> 137 us (0.938)
  local copies, waits for them, and re-layouts: 6.7 us -> 0.05 us
  Pallas kernels: 7.71 us -> 12.1 us
  blocking collectives: 64.1 us -> 61.3 us
  starting transfers between devices: 49.2 us -> 47.3 us
    ppermute x6, starting transfers between devices: 40.4 us -> 31.2 us  [the longest x1 10.9 us: on_device(): other = lax.ppermute(other, 'gy', far_sectors)]
    all_to_all x1, starting transfers between devices: 8.79 us -> 16.2 us  [on_device(): slots = lax.all_to_all(slots, 'gy', 0, 0, tiled=True)]
    pallas_call x0 -> x4, Pallas kernels: none -> 5.41 us  [the longest x1 2.36 us: on_device(): pl.pallas_call(gather_kernel, in_specs=[vmem, hbm, vmem] + [hbm] * 6, out...]
    unnamed x29 -> x16, local copies, waits for them, and re-layouts: 5.05 us -> 0.05 us
    all_to_all x1, blocking collectives: 64.1 us -> 61.3 us  [on_device(): lax.all_to_all(send.reshape(sectors, -1, width), 'gy', 0, 0, tiled=True)]
  transfers between devices with their start and end apart: 7 -> 7, of which waited for: 3 -> 2; matrix products, arithmetic and copies ran while one was open for 1% -> 0% of each run, Pallas kernels for 0% -> 2%
where the time goes in v2:
time: 137 us; the launch traced here: 136 us
  blocking collectives  61.3 us (45%)
  starting transfers between devices  47.3 us (35%)
  waiting for transfers between devices  14.4 us (11%)
  Pallas kernels  12.1 us (9%)
    all_to_all x1, blocking collectives, on_device(): lax.all_to_all(send.reshape(sectors, -1, width), 'gy', 0, 0, tiled=True)  61.3 us
    all_to_all x1, starting transfers between devices, on_device(): slots = lax.all_to_all(slots, 'gy', 0, 0, tiled=True)  16.2 us
    ppermute x1, starting transfers between devices, on_device(): other = lax.ppermute(other, 'gy', far_sectors)  10.9 us
    ppermute x1, starting transfers between devices, on_device(): far = lax.ppermute(far, 'gx', far_bands)  8.13 us
    ppermute x1, waiting for transfers between devices, on_device(): other = lax.ppermute(table, 'gy', far_sectors)  7.28 us
    ppermute x1, waiting for transfers between devices, on_device(): far = lax.ppermute(far, 'gx', far_bands)  7.11 us
    ppermute x1, starting transfers between devices, on_device(): other = lax.ppermute(table, 'gy', far_sectors)  6.35 us
  transfers between devices with their start and end apart: 7, of which 2 were waited for; matrix products, arithmetic and copies ran while one was open for 0% of the time, Pallas kernels for 2%

profile of v2, /device:TPU:6, one launch (start us, length us, event | category | flops | bytes accessed | tf_op | source)
XLA Modules:
  0.0 136.1 jit_solution(8052446923081172215)
XLA Ops:
  0.6 0.0 copy-start.5
  0.6 1.5 %shard_map.149 = (bf16[64,512]{1,0:T(8,128)(2,1)S(1)}, bf16[64,512]{1,0:T(8,128)(2,1)S(1)}, s32[64,128]{1,0:T(8,128)}) custom-call(bf16[2,64,512]{2,1,0:T(8,128)(2,1)} %grid.5, s32[8,128]{1,0:T(8,128)} %bitcast.29), custom_call_target="tpu_custom_call" | custom-call | tf_op jit(solution)/shard_map/pallas_call | solution.py:289
  2.2 16.2 %all-to-all-start = ((s32[64,1,128]{2,1,0:T(1,128)}), s32[64,1,128]{2,1,0:T(1,128)S(1)}, u32[]{:S(2)}, u32[]{:S(2)}) async-start(s32[64,1,128]{2,1,0:T(1,128)} %bitcast.5), calls=%async_computation | async-start | bytes 65536 | tf_op jit(solution)/shard_map/all_to_all | solution.py:302
  18.4 8.1 %collective-permute-start = (bf16[64,512]{1,0:T(8,128)(2,1)S(1)}, bf16[64,512]{1,0:T(8,128)(2,1)S(1)}, u32[]{:S(2)}, u32[]{:S(2)}) collective-permute-start(bf16[64,512]{1,0:T(8,128)(2,1)S(1)} %get-tuple-element.16), channel_id=1, source_target_pairs={{64,128},{128,64},{192,256},{256,192},{320,384},{384,320},{65,129}... | collective-permute-start | bytes 196616 | tf_op jit(solution)/shard_map/ppermute | solution.py:300
  26.5 1.9 %collective-permute-start.1 = (bf16[64,512]{1,0:T(8,128)(2,1)S(1)}, bf16[64,512]{1,0:T(8,128)(2,1)S(1)}, u32[]{:S(2)}, u32[]{:S(2)}) collective-permute-start(bf16[64,512]{1,0:T(8,128)(2,1)S(1)} %get-tuple-element.17), channel_id=1, source_target_pairs={{0,64},{64,0},{128,192},{192,128},{256,320},{320,256},{384,448},{4... | collective-permute-start | bytes 196616 | tf_op jit(solution)/shard_map/ppermute | solution.py:301
  28.4 7.1 %collective-permute-done.far = bf16[64,512]{1,0:T(8,128)(2,1)S(1)} collective-permute-done((bf16[64,512]{1,0:T(8,128)(2,1)S(1)}, bf16[64,512]{1,0:T(8,128)(2,1)S(1)}, u32[]{:S(2)}, u32[]{:S(2)}) %collective-permute-start) | collective-permute-done | bytes 65568 | tf_op jit(solution)/shard_map/ppermute | solution.py:300
  35.6 0.8 shard_map.151
  36.3 10.9 %collective-permute-start.2 = (bf16[4,8,512]{2,1,0:T(8,128)(2,1)S(1)}, bf16[4,8,512]{2,1,0:T(8,128)(2,1)S(1)}, u32[]{:S(2)}, u32[]{:S(2)}) collective-permute-start(bf16[4,8,512]{2,1,0:T(8,128)(2,1)S(1)} %get-tuple-element.20), channel_id=1, source_target_pairs={{0,63},{1,2},{2,1},{3,4},{4,3},{5,6},{6,5},{7,8},{8,7},{9,10},{10,... | collective-permute-start | bytes 98312 | tf_op jit(solution)/shard_map/ppermute | solution.py:317
  47.2 1.9 %collective-permute-start.3 = (bf16[4,8,512]{2,1,0:T(8,128)(2,1)S(1)}, bf16[4,8,512]{2,1,0:T(8,128)(2,1)S(1)}, u32[]{:S(2)}, u32[]{:S(2)}) collective-permute-start(bf16[4,8,512]{2,1,0:T(8,128)(2,1)S(1)} %get-tuple-element.21), channel_id=1, source_target_pairs={{0,1},{1,0},{2,3},{3,2},{4,5},{5,4},{6,7},{7,6},{8,9},{9,8},{10,11... | collective-permute-start | bytes 98312 | tf_op jit(solution)/shard_map/ppermute | solution.py:318
  49.2 2.4 %shard_map.150 = (f32[1024,512]{1,0:T(8,128)S(1)}, bf16[256,1024]{1,0:T(8,128)(2,1)S(1)}, bf16[256,512]{1,0:T(8,128)(2,1)S(1)}, bf16[3,512,512]{2,1,0:T(8,128)(2,1)S(1)}) custom-call(bf16[64,512]{1,0:T(8,128)(2,1)S(1)} %collective-permute-done.far, bf16[2,64,512]{2,1,0:T(8,128)(2,1)} %grid.5, bf16[64,512]{1,0:T(8,128)(2,1)S(1)} %collective-permute-done.1.near, ...), custom_call_target="tpu_custom_call" | custom-call | tf_op jit(solution)/shard_map/pallas_call | solution.py:323
  51.6 2.3 %shard_map.152 = (bf16[256,512]{1,0:T(8,128)(2,1)S(1)}, bf16[1024,512]{1,0:T(8,128)(2,1)S(1)}) custom-call(f32[1024,512]{1,0:T(8,128)S(1)} %get-tuple-element.18.partial, bf16[4,8,512]{2,1,0:T(8,128)(2,1)S(1)} %collective-permute-done.2.other, bf16[4,8,512]{2,1,0:T(8,128)(2,1)S(1)} %collective-permute-done.3.mate, ...), custom_call_target="tpu_custom_call" | custom-call | tf_op jit(solution)/shard_map/pallas_call | solution.py:346
  53.9 0.0 copy-start.1
  53.9 0.0 copy-start.2
  53.9 0.0 copy-start.6
  53.9 0.0 copy-start.7
  53.9 0.0 copy-start.4
  54.0 61.3 %all_to_all.16 = bf16[64,16,512]{2,1,0:T(8,128)(2,1)S(1)} all-to-all(bf16[64,16,512]{2,1,0:T(8,128)(2,1)S(1)} %bitcast.19), channel_id=1, replica_groups=mesh['gx'=8,'gy'=64] {'gy'}, dimensions={0} | all-to-all | bytes 2097152 | tf_op jit(solution)/shard_map/all_to_all | solution.py:358
  115.3 0.0 copy-start.3
  115.3 2.2 %shard_map.153 = (bf16[256,512]{1,0:T(8,128)(2,1)}, bf16[256,512]{1,0:T(8,128)(2,1)S(1)}) custom-call(bf16[1024,512]{1,0:T(8,128)(2,1)S(1)} %bitcast.16, bf16[256,512]{1,0:T(8,128)(2,1)S(1)} %get-tuple-element.27.first, bf16[512,512]{1,0:T(8,128)(2,1)S(1)} %copy-done.1, bf16[512,512]{1,0:T(8,128)(2,1)S(1)} %copy-done.2, s32[8,128]{1,0:T(8,128)S(1)} %bitcast.25), custom_call_target="tpu_custom_call" | custom-call | tf_op jit(solution)/shard_map/pallas_call | solution.py:361
  117.5 6.4 %collective-permute-start.4 = (bf16[256,512]{1,0:T(8,128)(2,1)S(1)}, bf16[256,512]{1,0:T(8,128)(2,1)S(1)}, u32[]{:S(2)}, u32[]{:S(2)}) collective-permute-start(bf16[256,512]{1,0:T(8,128)(2,1)S(1)} %get-tuple-element.28.own), channel_id=1, source_target_pairs={{0,63},{1,2},{2,1},{3,4},{4,3},{5,6},{6,5},{7,8},{8,7},{9,10},{10,... | collective-permute-start | bytes 786440 | tf_op jit(solution)/shard_map/ppermute | solution.py:371
  123.9 1.9 %collective-permute-start.5 = (bf16[256,512]{1,0:T(8,128)(2,1)S(1)}, bf16[256,512]{1,0:T(8,128)(2,1)S(1)}, u32[]{:S(2)}, u32[]{:S(2)}) collective-permute-start(bf16[256,512]{1,0:T(8,128)(2,1)S(1)} %get-tuple-element.28.own), channel_id=1, source_target_pairs={{0,1},{1,0},{2,3},{3,2},{4,5},{5,4},{6,7},{7,6},{8,9},{9,8},{10,11... | collective-permute-start | bytes 786440 | tf_op jit(solution)/shard_map/ppermute | solution.py:372
  125.9 0.8 shard_map.154.partial
  126.6 7.3 %collective-permute-done.4.other = bf16[256,512]{1,0:T(8,128)(2,1)S(1)} collective-permute-done((bf16[256,512]{1,0:T(8,128)(2,1)S(1)}, bf16[256,512]{1,0:T(8,128)(2,1)S(1)}, u32[]{:S(2)}, u32[]{:S(2)}) %collective-permute-start.4) | collective-permute-done | bytes 262176 | tf_op jit(solution)/shard_map/ppermute | solution.py:371
  133.9 2.2 %shard_map.155 = bf16[128,512]{1,0:T(8,128)(2,1)} custom-call(f32[1024,512]{1,0:T(8,128)S(1)} %shard_map.154.partial, bf16[256,512]{1,0:T(8,128)(2,1)S(1)} %collective-permute-done.4.other, bf16[256,512]{1,0:T(8,128)(2,1)S(1)} %collective-permute-done.5.mate, bf16[128,512]{1,0:T(8,128)(2,1)S(1)} %bitcast.18, bf16[512,512]{1,0:T(8,128)(2,1)S(1)} %copy-done.3, ...), custom_call_target="tpu_custom_call" | custom-call | tf_op jit(solution)/shard_map/pallas_call | solution.py:383
  (15 shorter events, 0.1 us)
Async XLA Ops:
  0.6 50.9 %copy-start.5 = (s32[1,1,1024]{2,1,0:T(1,128)S(1)}, s32[1,1,1024]{2,1,0:T(1,128)}, u32[]{:S(2)}) copy-start(s32[1,1,1024]{2,1,0:T(1,128)} %param.22) | copy-start | bytes 12292
  2.2 33.4 %all-to-all-start = ((s32[64,1,128]{2,1,0:T(1,128)}), s32[64,1,128]{2,1,0:T(1,128)S(1)}, u32[]{:S(2)}, u32[]{:S(2)}) async-start(s32[64,1,128]{2,1,0:T(1,128)} %bitcast.5), calls=%async_computation | async-start | bytes 65536 | tf_op jit(solution)/shard_map/all_to_all | solution.py:302
  18.4 17.2 %collective-permute-start = (bf16[64,512]{1,0:T(8,128)(2,1)S(1)}, bf16[64,512]{1,0:T(8,128)(2,1)S(1)}, u32[]{:S(2)}, u32[]{:S(2)}) collective-permute-start(bf16[64,512]{1,0:T(8,128)(2,1)S(1)} %get-tuple-element.16), channel_id=1, source_target_pairs={{64,128},{128,64},{192,256},{256,192},{320,384},{384,320},{65,129}... | collective-permute-start | bytes 196616 | tf_op jit(solution)/shard_map/ppermute | solution.py:300
  26.5 9.0 %collective-permute-start.1 = (bf16[64,512]{1,0:T(8,128)(2,1)S(1)}, bf16[64,512]{1,0:T(8,128)(2,1)S(1)}, u32[]{:S(2)}, u32[]{:S(2)}) collective-permute-start(bf16[64,512]{1,0:T(8,128)(2,1)S(1)} %get-tuple-element.17), channel_id=1, source_target_pairs={{0,64},{64,0},{128,192},{192,128},{256,320},{320,256},{384,448},{4... | collective-permute-start | bytes 196616 | tf_op jit(solution)/shard_map/ppermute | solution.py:301
  36.3 15.2 %collective-permute-start.2 = (bf16[4,8,512]{2,1,0:T(8,128)(2,1)S(1)}, bf16[4,8,512]{2,1,0:T(8,128)(2,1)S(1)}, u32[]{:S(2)}, u32[]{:S(2)}) collective-permute-start(bf16[4,8,512]{2,1,0:T(8,128)(2,1)S(1)} %get-tuple-element.20), channel_id=1, source_target_pairs={{0,63},{1,2},{2,1},{3,4},{4,3},{5,6},{6,5},{7,8},{8,7},{9,10},{10,... | collective-permute-start | bytes 98312 | tf_op jit(solution)/shard_map/ppermute | solution.py:317
  47.2 4.3 %collective-permute-start.3 = (bf16[4,8,512]{2,1,0:T(8,128)(2,1)S(1)}, bf16[4,8,512]{2,1,0:T(8,128)(2,1)S(1)}, u32[]{:S(2)}, u32[]{:S(2)}) collective-permute-start(bf16[4,8,512]{2,1,0:T(8,128)(2,1)S(1)} %get-tuple-element.21), channel_id=1, source_target_pairs={{0,1},{1,0},{2,3},{3,2},{4,5},{5,4},{6,7},{7,6},{8,9},{9,8},{10,11... | collective-permute-start | bytes 98312 | tf_op jit(solution)/shard_map/ppermute | solution.py:318
  53.9 61.4 %copy-start.1 = (bf16[512,512]{1,0:T(8,128)(2,1)S(1)}, bf16[512,512]{1,0:T(8,128)(2,1)}, u32[]{:S(2)}) copy-start(bf16[512,512]{1,0:T(8,128)(2,1)} %w_update.4) | copy-start | bytes 1572868
  53.9 61.4 %copy-start.2 = (bf16[512,512]{1,0:T(8,128)(2,1)S(1)}, bf16[512,512]{1,0:T(8,128)(2,1)}, u32[]{:S(2)}) copy-start(bf16[512,512]{1,0:T(8,128)(2,1)} %w_next.3) | copy-start | bytes 1572868
  53.9 61.4 %copy-start.6 = (s32[1,1,1024]{2,1,0:T(1,128)S(1)}, s32[1,1,1024]{2,1,0:T(1,128)}, u32[]{:S(2)}) copy-start(s32[1,1,1024]{2,1,0:T(1,128)} %param.25) | copy-start | bytes 12292
  53.9 71.9 %copy-start.7 = (s32[1,1,1024]{2,1,0:T(1,128)S(1)}, s32[1,1,1024]{2,1,0:T(1,128)}, u32[]{:S(2)}) copy-start(s32[1,1,1024]{2,1,0:T(1,128)} %param.26) | copy-start | bytes 12292
  53.9 71.9 %copy-start = (bf16[2,64,512]{2,1,0:T(8,128)(2,1)S(1)}, bf16[2,64,512]{2,1,0:T(8,128)(2,1)}, u32[]{:S(2)}) copy-start(bf16[2,64,512]{2,1,0:T(8,128)(2,1)} %grid.5) | copy-start | bytes 393220
  53.9 71.9 %copy-start.4 = (s32[1,1,1024]{2,1,0:T(1,128)S(1)}, s32[1,1,1024]{2,1,0:T(1,128)}, u32[]{:S(2)}) copy-start(s32[1,1,1024]{2,1,0:T(1,128)} %param.27) | copy-start | bytes 12292
  115.3 18.6 %copy-start.3 = (bf16[512,512]{1,0:T(8,128)(2,1)S(1)}, bf16[512,512]{1,0:T(8,128)(2,1)}, u32[]{:S(2)}) copy-start(bf16[512,512]{1,0:T(8,128)(2,1)} %w_update.5) | copy-start | bytes 1572868
  117.5 16.4 %collective-permute-start.4 = (bf16[256,512]{1,0:T(8,128)(2,1)S(1)}, bf16[256,512]{1,0:T(8,128)(2,1)S(1)}, u32[]{:S(2)}, u32[]{:S(2)}) collective-permute-start(bf16[256,512]{1,0:T(8,128)(2,1)S(1)} %get-tuple-element.28.own), channel_id=1, source_target_pairs={{0,63},{1,2},{2,1},{3,4},{4,3},{5,6},{6,5},{7,8},{8,7},{9,10},{10,... | collective-permute-start | bytes 786440 | tf_op jit(solution)/shard_map/ppermute | solution.py:371
  123.9 10.0 %collective-permute-start.5 = (bf16[256,512]{1,0:T(8,128)(2,1)S(1)}, bf16[256,512]{1,0:T(8,128)(2,1)S(1)}, u32[]{:S(2)}, u32[]{:S(2)}) collective-permute-start(bf16[256,512]{1,0:T(8,128)(2,1)S(1)} %get-tuple-element.28.own), channel_id=1, source_target_pairs={{0,1},{1,0},{2,3},{3,2},{4,5},{5,4},{6,7},{7,6},{8,9},{9,8},{10,11... | collective-permute-start | bytes 786440 | tf_op jit(solution)/shard_map/ppermute | solution.py:372

commit v3 on v2

--- a/solution.py
+++ b/solution.py
@@ -1,3 +1,5 @@
+import functools
+
 import jax
 import jax.numpy as jnp
 from jax import lax
@@ -10,6 +12,9 @@
 EPSILON = 1e-05
 LANES = 128
 CHUNK = 256
+CAP = 16
+GROUPS = LANES // CAP
+HALF = 8
 
 
 def column(index, rows):
@@ -57,6 +62,18 @@
 def log2(value):
     assert value & (value - 1) == 0
     return value.bit_length() - 1
+
+
+def roll(value, shift):
+    return pltpu.roll(value, shift % LANES, 1) if shift % LANES else value
+
+
+def halves(index):
+    upper = lax.rem(lax.axis_index("gy") // HALF, 2) == 1
+    count = index.shape[0] // 2
+    low = index[pl.ds(0, count, stride=2), :]
+    high = index[pl.ds(1, count, stride=2), :]
+    return jnp.where(upper, high, low), jnp.where(upper, low, high)
 
 
 def edges_kernel(grid, slots, far_out, near_out, slots_out, held, sems):
@@ -68,13 +85,13 @@
     index.start()
     near.start()
     far.start()
-    count = held.shape[0]
-    groups = slots_out.shape[0] // count
-    cap = LANES // groups
     index.wait()
-    for g in range(groups):
-        moved = pltpu.roll(held[...], LANES - g * cap, 1) if g else held[...]
-        slots_out[pl.ds(g, count, stride=groups), :] = moved
+    own, mirror = halves(held)
+    lane = lax.broadcasted_iota(jnp.int32, own.shape, 1)
+    for g in range(GROUPS):
+        first = roll(own, -g * CAP)
+        second = roll(mirror, CAP - g * CAP)
+        slots_out[pl.ds(g, own.shape[0], stride=GROUPS), :] = jnp.where(lane < CAP, first, second)
     near.wait()
     far.wait()
 
@@ -86,16 +103,15 @@
     east = pltpu.make_async_copy(grid.at[:, lons - HALO :], held.at[1], sems.at[1])
     west.start()
     east.start()
-    count = slots_out.shape[0]
-    groups = slots.shape[0] // count
-    cap = LANES // groups
-    lane = lax.broadcasted_iota(jnp.int32, slots_out.shape, 1)
-    kept = jnp.zeros_like(lane)
-    for g in range(groups):
-        part = slots[pl.ds(g, count, stride=groups), :]
-        moved = pltpu.roll(part, g * cap, 1) if g else part
-        kept = jnp.where((lane >= g * cap) & (lane < (g + 1) * cap), moved, kept)
-    slots_out[...] = kept
+    count = slots_out.shape[0] // 2
+    lane = lax.broadcasted_iota(jnp.int32, (count, LANES), 1)
+    for half in range(2):
+        kept = jnp.zeros_like(lane)
+        for g in range(GROUPS):
+            part = slots[pl.ds(g, count, stride=GROUPS), :]
+            moved = roll(part, g * CAP - half * CAP)
+            kept = jnp.where((lane >= g * CAP) & (lane < (g + 1) * CAP), moved, kept)
+        slots_out[half * count : (half + 1) * count, :] = kept
     west.wait()
     east.wait()
 
@@ -166,8 +182,8 @@
 
 
 def encode_kernel(
-    partial, other, mate, spreading, mesh, weights, source, request,
-    first_out, send_out, table, messages,
+    partial, other, mate, spreading, mesh, weights, source,
+    first_out, next_out, table, messages,
 ):
     w = weights[0]
     tall, halo, width = mate.shape
@@ -182,7 +198,6 @@
     on_mate = (lon >= HALO) == (lax.rem(lax.axis_index("gy"), 2) == 0)
     src = jnp.where(on_mate, 0, side) + lat * halo + (lon & (halo - 1))
     src = jnp.where(inner, -1, src)
-    req = request[...]
     edges = src.shape[0] * LANES
     for c in range(0, edges, CHUNK):
         rows = slice(c, c + CHUNK)
@@ -191,24 +206,39 @@
     summed = dot(spreading[...], messages[...])
     first = refresh(mesh[...], summed, weights[1])
     first_out[...] = first
-    following = dot(first, weights[2]).astype(jnp.bfloat16)
+    next_out[...] = dot(first, weights[2]).astype(jnp.bfloat16)
+
+
+def request_kernel(half, table, request, send_out):
+    nodes = table.shape[0]
+    count = request.shape[0] // 2
+    req = request[half * count : (half + 1) * count, :]
+    for c in range(0, count * LANES, CHUNK):
+        rows = slice(c, c + CHUNK)
+        send_out[rows, :] = dot(pick(column(req, rows), nodes), table[...]).astype(jnp.bfloat16)
+
+
+def half_kernel(picked, first, target, summed_out, messages):
+    own, _ = halves(target)
+    summed_out[...] = half_sum(picked, first[...], own, messages)
+
+
+def half_sum(picked, latent, target, messages):
+    nodes = latent.shape[0]
+    edges = target.shape[0] * LANES
     for c in range(0, edges, CHUNK):
         rows = slice(c, c + CHUNK)
-        send_out[rows, :] = dot(pick(column(req, rows), nodes), following).astype(jnp.bfloat16)
+        acc = dot(pick(column(target, rows), nodes), latent)
+        messages[rows, :] = message(acc + picked[rows, :].astype(jnp.float32))
+    return dot(spread(target, nodes), messages[...])
 
 
 def process_kernel(
-    picked, first, w_update, w_next, target, second_out, table_out, messages
+    partial, picked, first, w_update, w_next, target, second_out, table_out, messages
 ):
     latent = first[...]
-    nodes = latent.shape[0]
-    tgt = target[...]
-    edges = tgt.shape[0] * LANES
-    for c in range(0, edges, CHUNK):
-        rows = slice(c, c + CHUNK)
-        acc = dot(pick(column(tgt, rows), nodes), latent)
-        messages[rows, :] = message(acc + picked[rows, :].astype(jnp.float32))
-    summed = dot(spread(tgt, nodes), messages[...])
+    _, mirror = halves(target)
+    summed = partial[...] + half_sum(picked, latent, mirror, messages)
     second = refresh(latent, summed, w_update[...])
     second_out[...] = second
     table_out[...] = dot(second, w_next[...]).astype(jnp.bfloat16)
@@ -285,12 +315,17 @@
     far_sectors = [(i, partner[i] % sectors) for i in range(sectors)]
     near_sectors = [(i, i ^ 1) for i in range(sectors)]
 
+    group = [[i for i in range(sectors) if i // HALF % 2 == h] for h in range(2)]
+
+    def exchange(array):
+        return lax.all_to_all(array, "gy", 0, 0, axis_index_groups=group, tiled=True)
+
     band_edge = jax.ShapeDtypeStruct((lon_cols, width), bf16)
     far, near, slots = pl.pallas_call(
         edges_kernel,
         in_specs=[hbm, hbm],
         out_specs=(vmem,) * 3,
-        out_shape=(band_edge, band_edge, jax.ShapeDtypeStruct((sectors, LANES), jnp.int32)),
+        out_shape=(band_edge, band_edge, jax.ShapeDtypeStruct((sectors // 2, LANES), jnp.int32)),
         scratch_shapes=[
             pltpu.VMEM((edges // LANES, LANES), jnp.int32),
             pltpu.SemaphoreType.DMA((3,)),
@@ -299,7 +334,7 @@
     )(pinned(grid_latent), pinned(process_source.reshape(-1, LANES)))
     far = lax.ppermute(far, "gx", far_bands)
     near = lax.ppermute(near, "gx", near_bands)
-    slots = lax.all_to_all(slots, "gy", 0, 0, tiled=True)
+    slots = exchange(slots)
     sector_edge = jax.ShapeDtypeStruct((lat_rows + 2, HALO, width), bf16)
     other, mate, request = pl.pallas_call(
         sides_kernel,
@@ -343,30 +378,48 @@
         pinned(encode_update), pinned(process_message),
         pinned(source), pinned(encode_target.reshape(-1, LANES)),
     )
-    first, send = pl.pallas_call(
+    first, following = pl.pallas_call(
         encode_kernel,
         out_shape=(
             jax.ShapeDtypeStruct((nodes, width), bf16),
-            jax.ShapeDtypeStruct((edges, width), bf16),
+            jax.ShapeDtypeStruct((nodes, width), bf16),
         ),
         scratch_shapes=[
             pltpu.VMEM((-(-2 * side // LANES) * LANES, width), bf16),
             pltpu.VMEM((edges, width), bf16),
         ],
         compiler_params=params,
-    )(partial, other, mate, spreading, mesh_held, weights, source, request)
-    picked = lax.all_to_all(
-        send.reshape(sectors, -1, width), "gy", 0, 0, tiled=True
-    ).reshape(edges, width)
+    )(partial, other, mate, spreading, mesh_held, weights, source)
+
+    def requested(half, table):
+        rows = pl.pallas_call(
+            functools.partial(request_kernel, half),
+            out_shape=jax.ShapeDtypeStruct((edges // 2, width), bf16),
+            compiler_params=params,
+            cost_estimate=pl.CostEstimate(
+                flops=half * 35 * 10**9, bytes_accessed=10**6, transcendentals=0
+            ),
+        )(table, request)
+        return exchange(rows.reshape(sectors // 2, -1, width)).reshape(edges // 2, width)
+
+    mirror = lax.ppermute(following, "gy", [(i, i ^ HALF) for i in range(sectors)])
+    target = process_target.reshape(-1, LANES)
+    messages = pltpu.VMEM((edges // 2, width), bf16)
+    partial = pl.pallas_call(
+        half_kernel,
+        out_shape=jax.ShapeDtypeStruct((nodes, width), jnp.float32),
+        scratch_shapes=[messages],
+        compiler_params=params,
+    )(requested(0, following), first, target)
     second, table = pl.pallas_call(
         process_kernel,
         out_shape=(
             jax.ShapeDtypeStruct((nodes, width), bf16),
             jax.ShapeDtypeStruct((nodes, width), bf16),
         ),
-        scratch_shapes=[pltpu.VMEM((edges, width), bf16)],
-        compiler_params=params,
-    )(picked, first, process_update, decode_message, process_target.reshape(-1, LANES))
+        scratch_shapes=[messages],
+        compiler_params=params,
+    )(partial, requested(1, mirror), first, process_update, decode_message, target)
 
     other = lax.ppermute(table, "gy", far_sectors)
     mate = lax.ppermute(table, "gy", near_sectors)

time: 137 us -> 129 us (0.942); the launches traced: 136 us -> 127 us
  blocking collectives: 61.3 us -> 13.7 us
  waiting for transfers between devices: 14.4 us -> 55.6 us
  starting transfers between devices: 47.3 us -> 42.9 us
  Pallas kernels: 12.1 us -> 13.6 us
    all_to_all x1, blocking collectives: 61.3 us -> 13.7 us  [exchange(): lax.all_to_all(array, 'gy', 0, 0, axis_index_groups=group, tiled=True)]
    all_to_all x1 -> x2, waiting for transfers between devices: 0.01 us -> 26.4 us  [exchange(): lax.all_to_all(array, 'gy', 0, 0, axis_index_groups=group, tiled=True)]
    ppermute x0 -> x1, waiting for transfers between devices: none -> 16.2 us  [on_device(): lax.ppermute(following, 'gy', [(i, i ^ HALF) for i in range(sectors)])]
    ppermute x1, starting transfers between devices: 8.13 us -> 15.6 us  [on_device(): far = lax.ppermute(far, 'gx', far_bands)]
    ppermute x1, waiting for transfers between devices: 7.11 us -> 0.01 us  [on_device(): far = lax.ppermute(far, 'gx', far_bands)]
    all_to_all x1 -> x2, starting transfers between devices: 16.2 us -> 9.24 us  [exchange(): lax.all_to_all(array, 'gy', 0, 0, axis_index_groups=group, tiled=True)]
    ppermute x1, starting transfers between devices: 10.9 us -> 4.38 us  [on_device(): other = lax.ppermute(other, 'gy', far_sectors)]
    ppermute x1, waiting for transfers between devices: 0.01 us -> 5.27 us  [on_device(): other = lax.ppermute(other, 'gy', far_sectors)]
  transfers between devices with their start and end apart: 7 -> 9, of which waited for: 2 -> 5; matrix products, arithmetic and copies ran while one was open for 0% -> 0% of each run, Pallas kernels for 2% -> 5%
where the time goes in v3:
time: 129 us; the launch traced here: 127 us
  waiting for transfers between devices  55.6 us (43%)
  starting transfers between devices  42.9 us (33%)
  blocking collectives  13.7 us (11%)
  Pallas kernels  13.6 us (11%)
    all_to_all x2, waiting for transfers between devices, exchange(): lax.all_to_all(array, 'gy', 0, 0, axis_index_groups=group, tiled=True)  26.4 us
    ppermute x1, waiting for transfers between devices, on_device(): lax.ppermute(following, 'gy', [(i, i ^ HALF) for i in range(sectors)])  16.2 us
    ppermute x1, starting transfers between devices, on_device(): far = lax.ppermute(far, 'gx', far_bands)  15.6 us
    all_to_all x1, blocking collectives, exchange(): lax.all_to_all(array, 'gy', 0, 0, axis_index_groups=group, tiled=True)  13.7 us
    all_to_all x2, starting transfers between devices, exchange(): lax.all_to_all(array, 'gy', 0, 0, axis_index_groups=group, tiled=True)  9.24 us
    ppermute x1, waiting for transfers between devices, on_device(): other = lax.ppermute(table, 'gy', far_sectors)  7.71 us
    ppermute x1, starting transfers between devices, on_device(): other = lax.ppermute(table, 'gy', far_sectors)  5.92 us
    ppermute x1, waiting for transfers between devices, on_device(): other = lax.ppermute(other, 'gy', far_sectors)  5.27 us
  transfers between devices with their start and end apart: 9, of which 5 were waited for; matrix products, arithmetic and copies ran while one was open for 0% of the time, Pallas kernels for 5%

profile of v3, /device:TPU:6, one launch (start us, length us, event | category | flops | bytes accessed | tf_op | source)
XLA Modules:
  0.0 126.7 jit_solution(235538918529298351)
XLA Ops:
  0.6 0.9 shard_map.149
  1.6 15.6 %collective-permute-start = (bf16[64,512]{1,0:T(8,128)(2,1)S(1)}, bf16[64,512]{1,0:T(8,128)(2,1)S(1)}, u32[]{:S(2)}, u32[]{:S(2)}) collective-permute-start(bf16[64,512]{1,0:T(8,128)(2,1)S(1)} %get-tuple-element.16), channel_id=1, source_target_pairs={{64,128},{128,64},{192,256},{256,192},{320,384},{384,320},{65,129}... | collective-permute-start | bytes 196616 | tf_op jit(solution)/shard_map/ppermute | solution.py:335
  17.2 1.9 %collective-permute-start.1 = (bf16[64,512]{1,0:T(8,128)(2,1)S(1)}, bf16[64,512]{1,0:T(8,128)(2,1)S(1)}, u32[]{:S(2)}, u32[]{:S(2)}) collective-permute-start(bf16[64,512]{1,0:T(8,128)(2,1)S(1)} %get-tuple-element.17), channel_id=1, source_target_pairs={{0,64},{64,0},{128,192},{192,128},{256,320},{320,256},{384,448},{4... | collective-permute-start | bytes 196616 | tf_op jit(solution)/shard_map/ppermute | solution.py:336
  19.1 13.7 %all_to_all.21 = s32[32,1,128]{2,1,0:T(1,128)S(1)} all-to-all(s32[32,1,128]{2,1,0:T(1,128)S(1)} %bitcast.29), channel_id=1, replica_groups={{0,1,2,3,4,5,6,7,16,17,18,19,20,21,22,23,32,33,34,35,36,37,38,39,48,49,..., dimensions={0} | all-to-all | bytes 32768 | tf_op jit(solution)/shard_map/all_to_all | solution.py:321
  32.9 0.8 shard_map.151
  33.7 4.4 %collective-permute-start.2 = (bf16[4,8,512]{2,1,0:T(8,128)(2,1)S(1)}, bf16[4,8,512]{2,1,0:T(8,128)(2,1)S(1)}, u32[]{:S(2)}, u32[]{:S(2)}) collective-permute-start(bf16[4,8,512]{2,1,0:T(8,128)(2,1)S(1)} %get-tuple-element.20), channel_id=1, source_target_pairs={{0,63},{1,2},{2,1},{3,4},{4,3},{5,6},{6,5},{7,8},{8,7},{9,10},{10,... | collective-permute-start | bytes 98312 | tf_op jit(solution)/shard_map/ppermute | solution.py:352
  38.0 1.9 %collective-permute-start.3 = (bf16[4,8,512]{2,1,0:T(8,128)(2,1)S(1)}, bf16[4,8,512]{2,1,0:T(8,128)(2,1)S(1)}, u32[]{:S(2)}, u32[]{:S(2)}) collective-permute-start(bf16[4,8,512]{2,1,0:T(8,128)(2,1)S(1)} %get-tuple-element.21), channel_id=1, source_target_pairs={{0,1},{1,0},{2,3},{3,2},{4,5},{5,4},{6,7},{7,6},{8,9},{9,8},{10,11... | collective-permute-start | bytes 98312 | tf_op jit(solution)/shard_map/ppermute | solution.py:353
  40.0 2.4 %shard_map.150 = (f32[1024,512]{1,0:T(8,128)S(1)}, bf16[256,1024]{1,0:T(8,128)(2,1)S(1)}, bf16[256,512]{1,0:T(8,128)(2,1)S(1)}, bf16[3,512,512]{2,1,0:T(8,128)(2,1)S(1)}) custom-call(bf16[64,512]{1,0:T(8,128)(2,1)S(1)} %collective-permute-done.far, bf16[2,64,512]{2,1,0:T(8,128)(2,1)} %grid.5, bf16[64,512]{1,0:T(8,128)(2,1)S(1)} %collective-permute-done.1.near, ...), custom_call_target="tpu_custom_call" | custom-call | tf_op jit(solution)/shard_map/pallas_call | solution.py:358
  42.3 5.3 %collective-permute-done.2.other = bf16[4,8,512]{2,1,0:T(8,128)(2,1)S(1)} collective-permute-done((bf16[4,8,512]{2,1,0:T(8,128)(2,1)S(1)}, bf16[4,8,512]{2,1,0:T(8,128)(2,1)S(1)}, u32[]{:S(2)}, u32[]{:S(2)}) %collective-permute-start.2) | collective-permute-done | bytes 32800 | tf_op jit(solution)/shard_map/ppermute | solution.py:352
  47.6 1.9 %shard_map.152 = (bf16[256,512]{1,0:T(8,128)(2,1)S(1)}, bf16[256,512]{1,0:T(8,128)(2,1)S(1)}) custom-call(f32[1024,512]{1,0:T(8,128)S(1)} %get-tuple-element.18.partial, bf16[4,8,512]{2,1,0:T(8,128)(2,1)S(1)} %collective-permute-done.2.other, bf16[4,8,512]{2,1,0:T(8,128)(2,1)S(1)} %collective-permute-done.3.mate, ...), custom_call_target="tpu_custom_call" | custom-call | tf_op jit(solution)/shard_map/pallas_call | solution.py:381
  49.5 1.9 %collective-permute-start.4 = (bf16[256,512]{1,0:T(8,128)(2,1)S(1)}, bf16[256,512]{1,0:T(8,128)(2,1)S(1)}, u32[]{:S(2)}, u32[]{:S(2)}) collective-permute-start(bf16[256,512]{1,0:T(8,128)(2,1)S(1)} %get-tuple-element.25.table), channel_id=1, source_target_pairs={{0,8},{1,9},{2,10},{3,11},{4,12},{5,13},{6,14},{7,15},{8,0},{9,1},... | collective-permute-start | bytes 786440 | tf_op jit(solution)/shard_map/ppermute | solution.py:405
  51.4 1.2 shard_map.153
  52.6 5.4 %all-to-all-start.1 = ((bf16[32,16,512]{2,1,0:T(8,128)(2,1)}), bf16[32,16,512]{2,1,0:T(8,128)(2,1)S(1)}, u32[]{:S(2)}, u32[]{:S(2)}) async-start(bf16[32,16,512]{2,1,0:T(8,128)(2,1)} %bitcast.7), calls=%async_computation.1 | async-start | bytes 1048576 | tf_op jit(solution)/shard_map/all_to_all | solution.py:321
  58.0 16.2 %collective-permute-done.4.table = bf16[256,512]{1,0:T(8,128)(2,1)S(1)} collective-permute-done((bf16[256,512]{1,0:T(8,128)(2,1)S(1)}, bf16[256,512]{1,0:T(8,128)(2,1)S(1)}, u32[]{:S(2)}, u32[]{:S(2)}) %collective-permute-start.4) | collective-permute-done | bytes 262176 | tf_op jit(solution)/shard_map/ppermute | solution.py:405
  74.1 1.1 shard_map.155
  75.3 10.4 %all-to-all-done.1 = bf16[32,16,512]{2,1,0:T(8,128)(2,1)S(1)} async-done(((bf16[32,16,512]{2,1,0:T(8,128)(2,1)}), bf16[32,16,512]{2,1,0:T(8,128)(2,1)S(1)}, u32[]{:S(2)}, u32[]{:S(2)}) %all-to-all-start.1) | async-done | bytes 524320 | tf_op jit(solution)/shard_map/all_to_all | solution.py:321
  85.7 3.9 %all-to-all-start.2 = ((bf16[32,16,512]{2,1,0:T(8,128)(2,1)}), bf16[32,16,512]{2,1,0:T(8,128)(2,1)S(1)}, u32[]{:S(2)}, u32[]{:S(2)}) async-start(bf16[32,16,512]{2,1,0:T(8,128)(2,1)} %bitcast.10), calls=%async_computation.2 | async-start | bytes 1048576 | tf_op jit(solution)/shard_map/all_to_all | solution.py:321
  90.4 16.0 %all-to-all-done.2 = bf16[32,16,512]{2,1,0:T(8,128)(2,1)S(1)} async-done(((bf16[32,16,512]{2,1,0:T(8,128)(2,1)}), bf16[32,16,512]{2,1,0:T(8,128)(2,1)S(1)}, u32[]{:S(2)}, u32[]{:S(2)}) %all-to-all-start.2) | async-done | bytes 524320 | tf_op jit(solution)/shard_map/all_to_all | solution.py:321
  106.4 1.8 %shard_map.156 = (bf16[256,512]{1,0:T(8,128)(2,1)}, bf16[256,512]{1,0:T(8,128)(2,1)S(1)}) custom-call(f32[256,512]{1,0:T(8,128)S(1)} %shard_map.154.partial, bf16[512,512]{1,0:T(8,128)(2,1)S(1)} %bitcast.21, bf16[256,512]{1,0:T(8,128)(2,1)S(1)} %get-tuple-element.27.first, bf16[512,512]{1,0:T(8,128)(2,1)S(1)} %copy-done.1, bf16[512,512]{1,0:T(8,128)(2,1)S(1)} %copy-done.2, ...), custom_call_target="tpu_custom_call" | custom-call | tf_op jit(solution)/shard_map/pallas_call | solution.py:414
  108.1 5.9 %collective-permute-start.5 = (bf16[256,512]{1,0:T(8,128)(2,1)S(1)}, bf16[256,512]{1,0:T(8,128)(2,1)S(1)}, u32[]{:S(2)}, u32[]{:S(2)}) collective-permute-start(bf16[256,512]{1,0:T(8,128)(2,1)S(1)} %get-tuple-element.28.own), channel_id=1, source_target_pairs={{0,63},{1,2},{2,1},{3,4},{4,3},{5,6},{6,5},{7,8},{8,7},{9,10},{10,... | collective-permute-start | bytes 786440 | tf_op jit(solution)/shard_map/ppermute | solution.py:424
  114.1 1.9 %collective-permute-start.6 = (bf16[256,512]{1,0:T(8,128)(2,1)S(1)}, bf16[256,512]{1,0:T(8,128)(2,1)S(1)}, u32[]{:S(2)}, u32[]{:S(2)}) collective-permute-start(bf16[256,512]{1,0:T(8,128)(2,1)S(1)} %get-tuple-element.28.own), channel_id=1, source_target_pairs={{0,1},{1,0},{2,3},{3,2},{4,5},{5,4},{6,7},{7,6},{8,9},{9,8},{10,11... | collective-permute-start | bytes 786440 | tf_op jit(solution)/shard_map/ppermute | solution.py:425
  116.0 0.8 shard_map.157.partial
  116.8 7.7 %collective-permute-done.5.other = bf16[256,512]{1,0:T(8,128)(2,1)S(1)} collective-permute-done((bf16[256,512]{1,0:T(8,128)(2,1)S(1)}, bf16[256,512]{1,0:T(8,128)(2,1)S(1)}, u32[]{:S(2)}, u32[]{:S(2)}) %collective-permute-start.5) | collective-permute-done | bytes 262176 | tf_op jit(solution)/shard_map/ppermute | solution.py:424
  124.5 2.2 %shard_map.158 = bf16[128,512]{1,0:T(8,128)(2,1)} custom-call(f32[1024,512]{1,0:T(8,128)S(1)} %shard_map.157.partial, bf16[256,512]{1,0:T(8,128)(2,1)S(1)} %collective-permute-done.5.other, bf16[256,512]{1,0:T(8,128)(2,1)S(1)} %collective-permute-done.6.mate, bf16[128,512]{1,0:T(8,128)(2,1)S(1)} %bitcast.19, bf16[512,512]{1,0:T(8,128)(2,1)S(1)} %copy-done.3, ...), custom_call_target="tpu_custom_call" | custom-call | tf_op jit(solution)/shard_map/pallas_call | solution.py:436
  (22 shorter events, 0.8 us)
Async XLA Ops:
  0.6 47.0 %copy-start.4 = (s32[1,1,1024]{2,1,0:T(1,128)S(1)}, s32[1,1,1024]{2,1,0:T(1,128)}, u32[]{:S(2)}) copy-start(s32[1,1,1024]{2,1,0:T(1,128)} %param.22) | copy-start | bytes 12292
  1.6 31.3 %collective-permute-start = (bf16[64,512]{1,0:T(8,128)(2,1)S(1)}, bf16[64,512]{1,0:T(8,128)(2,1)S(1)}, u32[]{:S(2)}, u32[]{:S(2)}) collective-permute-start(bf16[64,512]{1,0:T(8,128)(2,1)S(1)} %get-tuple-element.16), channel_id=1, source_target_pairs={{64,128},{128,64},{192,256},{256,192},{320,384},{384,320},{65,129}... | collective-permute-start | bytes 196616 | tf_op jit(solution)/shard_map/ppermute | solution.py:335
  17.2 15.7 %collective-permute-start.1 = (bf16[64,512]{1,0:T(8,128)(2,1)S(1)}, bf16[64,512]{1,0:T(8,128)(2,1)S(1)}, u32[]{:S(2)}, u32[]{:S(2)}) collective-permute-start(bf16[64,512]{1,0:T(8,128)(2,1)S(1)} %get-tuple-element.17), channel_id=1, source_target_pairs={{0,64},{64,0},{128,192},{192,128},{256,320},{320,256},{384,448},{4... | collective-permute-start | bytes 196616 | tf_op jit(solution)/shard_map/ppermute | solution.py:336
  33.7 13.9 %collective-permute-start.2 = (bf16[4,8,512]{2,1,0:T(8,128)(2,1)S(1)}, bf16[4,8,512]{2,1,0:T(8,128)(2,1)S(1)}, u32[]{:S(2)}, u32[]{:S(2)}) collective-permute-start(bf16[4,8,512]{2,1,0:T(8,128)(2,1)S(1)} %get-tuple-element.20), channel_id=1, source_target_pairs={{0,63},{1,2},{2,1},{3,4},{4,3},{5,6},{6,5},{7,8},{8,7},{9,10},{10,... | collective-permute-start | bytes 98312 | tf_op jit(solution)/shard_map/ppermute | solution.py:352
  38.0 9.6 %collective-permute-start.3 = (bf16[4,8,512]{2,1,0:T(8,128)(2,1)S(1)}, bf16[4,8,512]{2,1,0:T(8,128)(2,1)S(1)}, u32[]{:S(2)}, u32[]{:S(2)}) collective-permute-start(bf16[4,8,512]{2,1,0:T(8,128)(2,1)S(1)} %get-tuple-element.21), channel_id=1, source_target_pairs={{0,1},{1,0},{2,3},{3,2},{4,5},{5,4},{6,7},{7,6},{8,9},{9,8},{10,11... | collective-permute-start | bytes 98312 | tf_op jit(solution)/shard_map/ppermute | solution.py:353
  49.5 24.6 %collective-permute-start.4 = (bf16[256,512]{1,0:T(8,128)(2,1)S(1)}, bf16[256,512]{1,0:T(8,128)(2,1)S(1)}, u32[]{:S(2)}, u32[]{:S(2)}) collective-permute-start(bf16[256,512]{1,0:T(8,128)(2,1)S(1)} %get-tuple-element.25.table), channel_id=1, source_target_pairs={{0,8},{1,9},{2,10},{3,11},{4,12},{5,13},{6,14},{7,15},{8,0},{9,1},... | collective-permute-start | bytes 786440 | tf_op jit(solution)/shard_map/ppermute | solution.py:405
  52.6 33.1 %all-to-all-start.1 = ((bf16[32,16,512]{2,1,0:T(8,128)(2,1)}), bf16[32,16,512]{2,1,0:T(8,128)(2,1)S(1)}, u32[]{:S(2)}, u32[]{:S(2)}) async-start(bf16[32,16,512]{2,1,0:T(8,128)(2,1)} %bitcast.7), calls=%async_computation.1 | async-start | bytes 1048576 | tf_op jit(solution)/shard_map/all_to_all | solution.py:321
  58.0 31.7 %copy-start.5 = (s32[1,1,1024]{2,1,0:T(1,128)S(1)}, s32[1,1,1024]{2,1,0:T(1,128)}, u32[]{:S(2)}) copy-start(s32[1,1,1024]{2,1,0:T(1,128)} %param.25) | copy-start | bytes 12292
  75.3 31.1 %copy-start.1 = (bf16[512,512]{1,0:T(8,128)(2,1)S(1)}, bf16[512,512]{1,0:T(8,128)(2,1)}, u32[]{:S(2)}) copy-start(bf16[512,512]{1,0:T(8,128)(2,1)} %w_update.4) | copy-start | bytes 1572868
  75.3 31.1 %copy-start.2 = (bf16[512,512]{1,0:T(8,128)(2,1)S(1)}, bf16[512,512]{1,0:T(8,128)(2,1)}, u32[]{:S(2)}) copy-start(bf16[512,512]{1,0:T(8,128)(2,1)} %w_next.3) | copy-start | bytes 1572868
  85.7 20.6 %all-to-all-start.2 = ((bf16[32,16,512]{2,1,0:T(8,128)(2,1)}), bf16[32,16,512]{2,1,0:T(8,128)(2,1)S(1)}, u32[]{:S(2)}, u32[]{:S(2)}) async-start(bf16[32,16,512]{2,1,0:T(8,128)(2,1)} %bitcast.10), calls=%async_computation.2 | async-start | bytes 1048576 | tf_op jit(solution)/shard_map/all_to_all | solution.py:321
  89.6 26.4 %copy-start.7 = (s32[1,1,1024]{2,1,0:T(1,128)S(1)}, s32[1,1,1024]{2,1,0:T(1,128)}, u32[]{:S(2)}) copy-start(s32[1,1,1024]{2,1,0:T(1,128)} %param.26) | copy-start | bytes 12292
  89.6 26.4 %copy-start = (bf16[2,64,512]{2,1,0:T(8,128)(2,1)S(1)}, bf16[2,64,512]{2,1,0:T(8,128)(2,1)}, u32[]{:S(2)}) copy-start(bf16[2,64,512]{2,1,0:T(8,128)(2,1)} %grid.5) | copy-start | bytes 393220
  89.7 26.4 %copy-start.6 = (s32[1,1,1024]{2,1,0:T(1,128)S(1)}, s32[1,1,1024]{2,1,0:T(1,128)}, u32[]{:S(2)}) copy-start(s32[1,1,1024]{2,1,0:T(1,128)} %param.27) | copy-start | bytes 12292
  106.4 18.2 %copy-start.3 = (bf16[512,512]{1,0:T(8,128)(2,1)S(1)}, bf16[512,512]{1,0:T(8,128)(2,1)}, u32[]{:S(2)}) copy-start(bf16[512,512]{1,0:T(8,128)(2,1)} %w_update.5) | copy-start | bytes 1572868
  108.1 16.4 %collective-permute-start.5 = (bf16[256,512]{1,0:T(8,128)(2,1)S(1)}, bf16[256,512]{1,0:T(8,128)(2,1)S(1)}, u32[]{:S(2)}, u32[]{:S(2)}) collective-permute-start(bf16[256,512]{1,0:T(8,128)(2,1)S(1)} %get-tuple-element.28.own), channel_id=1, source_target_pairs={{0,63},{1,2},{2,1},{3,4},{4,3},{5,6},{6,5},{7,8},{8,7},{9,10},{10,... | collective-permute-start | bytes 786440 | tf_op jit(solution)/shard_map/ppermute | solution.py:424
  114.1 10.5 %collective-permute-start.6 = (bf16[256,512]{1,0:T(8,128)(2,1)S(1)}, bf16[256,512]{1,0:T(8,128)(2,1)S(1)}, u32[]{:S(2)}, u32[]{:S(2)}) collective-permute-start(bf16[256,512]{1,0:T(8,128)(2,1)S(1)} %get-tuple-element.28.own), channel_id=1, source_target_pairs={{0,1},{1,0},{2,3},{3,2},{4,5},{5,4},{6,7},{7,6},{8,9},{9,8},{10,11... | collective-permute-start | bytes 786440 | tf_op jit(solution)/shard_map/ppermute | solution.py:425

commit v4 on v2

v4 whole, which is shorter than its diff:
```python
import jax
import jax.numpy as jnp
from jax import lax
from jax.experimental import pallas as pl
from jax.experimental.pallas import tpu as pltpu
from jax.sharding import PartitionSpec as P

HALO = 8
LON_DEV = 64
EPSILON = 1e-05
LANES = 128
CHUNK = 256
CAP = 16
GROUPS = LANES // CAP
HALF = 8


def column(index, rows):
    parts = []
    for i in range(rows.start // LANES, rows.stop // LANES):
        row = jnp.broadcast_to(index[i : i + 1, :], (LANES, LANES))
        parts.append(row.T)
    return jnp.concatenate(parts, axis=0)


def pick(col, count):
    lane = lax.broadcasted_iota(jnp.int32, col.shape, 1)
    parts = [
        jnp.where(col == lane + k, 1.0, 0.0).astype(jnp.bfloat16)
        for k in range(0, count, LANES)
    ]
    return jnp.concatenate(parts, axis=1)


def spread(index, count):
    sub = lax.broadcasted_iota(jnp.int32, (count, LANES), 0)
    parts = [
        jnp.where(index[i : i + 1, :] == sub, 1.0, 0.0).astype(jnp.bfloat16)
        for i in range(index.shape[0])
    ]
    return jnp.concatenate(parts, axis=1)


def dot(a, b):
    return jnp.dot(a, b, preferred_element_type=jnp.float32)


def message(summed):
    half = 0.5 * summed
    return (half * jnp.tanh(half) + half).astype(jnp.bfloat16)


def refresh(latent, summed, weight):
    scaled = summed * lax.rsqrt(jnp.mean(summed * summed, axis=-1, keepdims=True) + EPSILON)
    return (latent.astype(jnp.float32) + dot(scaled.astype(jnp.bfloat16), weight)).astype(
        jnp.bfloat16
    )


def log2(value):
    assert value & (value - 1) == 0
    return value.bit_length() - 1


def roll(value, shift):
    return pltpu.roll(value, shift % LANES, 1) if shift % LANES else value


def halves(index):
    upper = lax.rem(lax.axis_index("gy") // HALF, 2) == 1
    count = index.shape[0] // 2
    low = index[pl.ds(0, count, stride=2), :]
    high = index[pl.ds(1, count, stride=2), :]
    return jnp.where(upper, high, low), jnp.where(upper, low, high)


def apart(slots, out):
    own, mirror = halves(slots)
    lane = lax.broadcasted_iota(jnp.int32, own.shape, 1)
    for g in range(GROUPS):
        first = roll(own, -g * CAP)
        second = roll(mirror, CAP - g * CAP)
        out[pl.ds(g, own.shape[0], stride=GROUPS), :] = jnp.where(lane < CAP, first, second)


def together(rows):
    each = 2 * CAP
    fold = LANES // each
    count = rows.shape[0] // fold
    lane = lax.broadcasted_iota(jnp.int32, (count, LANES), 1)
    kept = jnp.zeros_like(lane)
    for g in range(fold):
        moved = roll(rows[pl.ds(g, count, stride=fold), :], g * each)
        kept = jnp.where((lane >= g * each) & (lane < (g + 1) * each), moved, kept)
    return kept


def edges_kernel(grid, far_out, near_out, sems):
    even = lax.rem(lax.axis_index("gx"), 2) == 0
    last = grid.shape[0] - 1
    near = pltpu.make_async_copy(grid.at[jnp.where(even, last, 0)], near_out, sems.at[0])
    far = pltpu.make_async_copy(grid.at[jnp.where(even, 0, last)], far_out, sems.at[1])
    near.start()
    far.start()
    near.wait()
    far.wait()


def sides_kernel(far, grid, near, far_out, near_out, held, sems):
    even = lax.rem(lax.axis_index("gy"), 2) == 0
    lats, lons, _ = grid.shape
    west = pltpu.make_async_copy(grid.at[:, :HALO], held.at[0], sems.at[0])
    east = pltpu.make_async_copy(grid.at[:, lons - HALO :], held.at[1], sems.at[1])
    west.start()
    east.start()
    west.wait()
    east.wait()

    def put(out, side):
        out[0] = near[side, :]
        for i in range(lats):
            out[i + 1] = held[0 if side.start == 0 else 1, i]
        out[lats + 1] = far[side, :]

    first, last = slice(0, HALO), slice(lons - HALO, lons)

    @pl.when(even)
    def _():
        put(near_out, last)
        put(far_out, first)

    @pl.when(jnp.logical_not(even))
    def _():
        put(near_out, first)
        put(far_out, last)


def places(source, lats, lons):
    band, sector = lax.axis_index("gx"), lax.axis_index("gy")
    lon_total = lons * lax.axis_size("gy")
    lat = (source >> log2(lon_total)) - band * lats + 1
    outer = (lat == 0) | (lat == lats + 1)
    lat = jnp.where(outer & (lax.rem(band, 2) == 0), lats + 1 - lat, lat)
    lon = ((source & (lon_total - 1)) - sector * lons + HALO) & (lon_total - 1)
    inner = (lon >= HALO) & (lon < HALO + lons)
    return lat, lon, inner


def gather_kernel(
    far, grid, near, mesh, w_message, w_update, w_next, source, target, next_source, next_target,
    partial, spread_out, mesh_out, w_out, sides_out, slots_out, order_out,
    held, indices, rows_held, table, sems,
):
    pairs = [(source, indices.at[0]), (target, indices.at[1])]
    pairs += [(grid, held), (w_message, w_out.at[0]), (mesh, mesh_out)]
    pairs += [(next_source, indices.at[2]), (next_target, indices.at[3])]
    pairs += [(w_update, w_out.at[1]), (w_next, w_out.at[2])]
    copies = [pltpu.make_async_copy(a, b, sems.at[i]) for i, (a, b) in enumerate(pairs)]
    for copy in copies:
        copy.start()
    lats, lons, width = grid.shape
    nodes = mesh.shape[0]
    copies[0].wait()
    copies[1].wait()
    lat, lon, inner = places(indices[0], lats, lons)
    src = jnp.where(inner, lat * lons + lon - HALO, -1)
    tgt = indices[1]
    edges = src.shape[0] * LANES
    spread_out[...] = spread(tgt, nodes)
    copies[2].wait()
    copies[3].wait()
    w = w_out[0]
    table[:lons, :] = dot(near[...], w).astype(jnp.bfloat16)
    inside = held[...].reshape(lats * lons, width)
    table[lons : (lats + 1) * lons, :] = dot(inside, w).astype(jnp.bfloat16)
    table[(lats + 1) * lons :, :] = dot(far[...], w).astype(jnp.bfloat16)
    copies[4].wait()
    depth = table.shape[0]
    side = (lats + 2) * HALO
    on_mate = (lon >= HALO) == (lax.rem(lax.axis_index("gy"), 2) == 0)
    edge = jnp.where(on_mate, 0, side) + lat * HALO + (lon & (HALO - 1))
    edge = jnp.where(inner, -1, edge)
    for c in range(0, edges, CHUNK):
        rows = slice(c, c + CHUNK)
        acc = dot(pick(column(src, rows), depth), table[...])
        partial[rows, :] = acc + dot(pick(column(tgt, rows), nodes), mesh_out[...])
        sides_out[rows, :] = pick(column(edge, rows), sides_out.shape[1])
    copies[5].wait()
    copies[6].wait()
    apart(indices.at[2], slots_out)
    apart(indices.at[3], rows_held)
    order_out[...] = together(rows_held)
    copies[7].wait()
    copies[8].wait()


def encode_kernel(
    partial, other, mate, spreading, mesh, weights, sides,
    first_out, next_out, table, messages,
):
    w = weights[0]
    tall, halo, width = mate.shape
    side = tall * halo
    table[:side, :] = dot(mate[...].reshape(side, width), w).astype(jnp.bfloat16)
    table[side : 2 * side, :] = dot(other[...].reshape(side, width), w).astype(jnp.bfloat16)
    table[2 * side :, :] = jnp.zeros((table.shape[0] - 2 * side, width), jnp.bfloat16)
    edges = partial.shape[0]
    for c in range(0, edges, CHUNK):
        rows = slice(c, c + CHUNK)
        messages[rows, :] = message(partial[rows, :] + dot(sides[rows, :], table[...]))
    summed = dot(spreading[...], messages[...])
    first = refresh(mesh[...], summed, weights[1])
    first_out[...] = first
    next_out[...] = dot(first, weights[2]).astype(jnp.bfloat16)


def request_kernel(table, mirror, slots, send_out):
    nodes = table.shape[0]
    asked = together(slots)
    lane = lax.broadcasted_iota(jnp.int32, asked.shape, 1)
    second = (lane & (2 * CAP - 1)) >= CAP
    for ref, req in ((table, jnp.where(second, -1, asked)), (mirror, jnp.where(second, asked, -1))):
        for c in range(0, send_out.shape[0], CHUNK):
            rows = slice(c, c + CHUNK)
            part = dot(pick(column(req, rows), nodes), ref[...]).astype(jnp.bfloat16)
            send_out[rows, :] = part if ref is table else send_out[rows, :] + part


def target_kernel(first, target, partial, spread_out):
    nodes = first.shape[0]
    tgt = target[...]
    for c in range(0, partial.shape[0], CHUNK):
        rows = slice(c, c + CHUNK)
        partial[rows, :] = dot(pick(column(tgt, rows), nodes), first[...])
    spread_out[...] = spread(tgt, nodes)


def process_kernel(
    picked, partial, spreading, first, w_update, w_next, second_out, table_out, messages
):
    for c in range(0, picked.shape[0], CHUNK):
        rows = slice(c, c + CHUNK)
        messages[rows, :] = message(partial[rows, :] + picked[rows, :].astype(jnp.float32))
    second = refresh(first[...], dot(spreading[...], messages[...]), w_update[...])
    second_out[...] = second
    table_out[...] = dot(second, w_next[...]).astype(jnp.bfloat16)


def reach_kernel(own, grid, source, target, partial, picks_out, spread_out):
    latent = grid[...]
    cells = latent.shape[0]
    nodes = own.shape[0]
    src, tgt = source[...], target[...]
    for c in range(0, partial.shape[0], CHUNK):
        rows = slice(c, c + CHUNK)
        col = column(src, rows)
        acc = dot(pick(column(tgt, rows), cells), latent)
        partial[rows, :] = acc + dot(pick(col, nodes), own[...])
        picks_out[rows, :] = pick(col - nodes, 2 * nodes)
    spread_out[...] = spread(tgt, cells)


def decode_kernel(
    partial, other, mate, picks, spreading, grid, w_update, grid_out, messages
):
    nodes = mate.shape[0]
    for c in range(0, partial.shape[0], CHUNK):
        rows = slice(c, c + CHUNK)
        acc = partial[rows, :] + dot(picks[rows, :nodes], mate[...])
        messages[rows, :] = message(acc + dot(picks[rows, nodes:], other[...]))
    summed = dot(spreading[...], messages[...])
    grid_out[...] = refresh(grid[...], summed, w_update[...])


def on_device(
    grid_latent,
    mesh_latent,
    encode_message,
    encode_update,
    process_message,
    process_update,
    decode_message,
    decode_update,
    encode_source,
    encode_target,
    process_source,
    process_target,
    decode_source,
    decode_target,
):
    lat_rows, lon_cols, width = grid_latent.shape
    bands = lax.axis_size("gx")
    sectors = lax.axis_size("gy")
    sector = lax.axis_index("gy")
    mesh_rows = mesh_latent.reshape(-1, width)
    nodes = mesh_rows.shape[0]
    grid_rows = grid_latent.reshape(-1, width)
    cells = grid_rows.shape[0]
    edges = encode_source.size
    bf16 = jnp.bfloat16
    params = pltpu.CompilerParams(vmem_limit_bytes=40 * 1024 * 1024)
    hbm = pl.BlockSpec(memory_space=pltpu.HBM)
    vmem = pl.BlockSpec(memory_space=pltpu.VMEM)
    assert lon_cols == LON_DEV

    def pinned(array):
        return pltpu.with_memory_space_constraint(array, pltpu.HBM)

    partner = [i + 1 if i % 2 else i - 1 for i in range(max(bands, sectors))]
    far_bands = [(i, partner[i]) for i in range(1, bands - 1)]
    near_bands = [(i, i ^ 1) for i in range(bands)]
    far_sectors = [(i, partner[i] % sectors) for i in range(sectors)]
    near_sectors = [(i, i ^ 1) for i in range(sectors)]

    group = [[i for i in range(sectors) if i // HALF % 2 == h] for h in range(2)]

    def exchange(array):
        return lax.all_to_all(array, "gy", 0, 0, axis_index_groups=group, tiled=True)

    band_edge = jax.ShapeDtypeStruct((lon_cols, width), bf16)
    far, near = pl.pallas_call(
        edges_kernel,
        in_specs=[hbm],
        out_specs=(vmem,) * 2,
        out_shape=(band_edge,) * 2,
        scratch_shapes=[pltpu.SemaphoreType.DMA((2,))],
        compiler_params=params,
    )(pinned(grid_latent))
    far = lax.ppermute(far, "gx", far_bands)
    near = lax.ppermute(near, "gx", near_bands)
    sector_edge = jax.ShapeDtypeStruct((lat_rows + 2, HALO, width), bf16)
    other, mate = pl.pallas_call(
        sides_kernel,
        in_specs=[vmem, hbm, vmem],
        out_specs=(vmem,) * 2,
        out_shape=(sector_edge,) * 2,
        scratch_shapes=[
            pltpu.VMEM((2, lat_rows, HALO, width), bf16),
            pltpu.SemaphoreType.DMA((2,)),
        ],
        compiler_params=params,
    )(far, pinned(grid_latent), near)
    other = lax.ppermute(other, "gy", far_sectors)
    mate = lax.ppermute(mate, "gy", near_sectors)

    tall_cells = (lat_rows + 2) * lon_cols
    depth = -(-2 * (lat_rows + 2) * HALO // LANES) * LANES
    index = jax.ShapeDtypeStruct((edges // LANES, LANES), jnp.int32)
    table_shape = jax.ShapeDtypeStruct((nodes, width), bf16)
    partial_shape = jax.ShapeDtypeStruct((edges, width), jnp.float32)
    spread_shape = jax.ShapeDtypeStruct((nodes, edges), bf16)
    slots_shape = jax.ShapeDtypeStruct((sectors // 2, LANES), jnp.int32)
    partial, spreading, mesh_held, weights, sides, slots, order = pl.pallas_call(
        gather_kernel,
        in_specs=[vmem, hbm, vmem] + [hbm] * 8,
        out_specs=(vmem,) * 7,
        out_shape=(
            partial_shape,
            spread_shape,
            table_shape,
            jax.ShapeDtypeStruct((3, width, width), bf16),
            jax.ShapeDtypeStruct((edges, depth), bf16),
            slots_shape,
            index,
        ),
        scratch_shapes=[
            pltpu.VMEM((lat_rows, lon_cols, width), bf16),
            pltpu.VMEM((4, edges // LANES, LANES), jnp.int32),
            pltpu.VMEM(slots_shape.shape, jnp.int32),
            pltpu.VMEM((tall_cells, width), bf16),
            pltpu.SemaphoreType.DMA((9,)),
        ],
        compiler_params=params,
    )(
        far, pinned(grid_latent), near, pinned(mesh_rows), pinned(encode_message),
        pinned(encode_update), pinned(process_message),
        *(
            pinned(array.reshape(-1, LANES))
            for array in (encode_source, encode_target, process_source, process_target)
        ),
    )
    messages = pltpu.VMEM((edges, width), bf16)
    first, following = pl.pallas_call(
        encode_kernel,
        out_shape=(table_shape, table_shape),
        scratch_shapes=[pltpu.VMEM((depth, width), bf16), messages],
        compiler_params=params,
    )(partial, other, mate, spreading, mesh_held, weights, sides)

    following, slots = lax.optimization_barrier((following, slots))
    mirror = lax.ppermute(following, "gy", [(i, i ^ HALF) for i in range(sectors)])
    slots = exchange(slots)
    partial, spreading = pl.pallas_call(
        target_kernel,
        out_shape=(partial_shape, spread_shape),
        compiler_params=params,
    )(first, order)
    send = pl.pallas_call(
        request_kernel,
        out_shape=jax.ShapeDtypeStruct((edges, width), bf16),
        compiler_params=params,
    )(following, mirror, slots)
    picked = exchange(send.reshape(sectors // 2, -1, width)).reshape(edges, width)
    second, table = pl.pallas_call(
        process_kernel,
        out_shape=(table_shape, table_shape),
        scratch_shapes=[messages],
        compiler_params=params,
    )(picked, partial, spreading, first, process_update, decode_message)

    other = lax.ppermute(table, "gy", far_sectors)
    mate = lax.ppermute(table, "gy", near_sectors)
    source = decode_source.reshape(-1, LANES)
    owner = source // nodes % sectors
    piece = jnp.where(owner == sector, 0, jnp.where(owner == sector ^ 1, 1, 2))
    row = piece * nodes + source % nodes
    target = decode_target.reshape(-1, LANES)
    partial, picks, spreading = pl.pallas_call(
        reach_kernel,
        out_shape=(
            partial_shape,
            jax.ShapeDtypeStruct((edges, 2 * nodes), bf16),
            jax.ShapeDtypeStruct((cells, edges), bf16),
        ),
        compiler_params=params,
    )(table, grid_rows, row, target)
    grid_output = pl.pallas_call(
        decode_kernel,
        out_shape=jax.ShapeDtypeStruct((cells, width), bf16),
        scratch_shapes=[messages],
        compiler_params=params,
    )(partial, other, mate, picks, spreading, grid_rows, decode_update)
    return (
        grid_output.reshape(lat_rows, lon_cols, width),
        second.reshape(1, 1, nodes, width),
    )


def solution(mesh):
    edge = P("gx", "gy", None)
    return jax.shard_map(
        on_device,
        mesh=mesh,
        in_specs=(
            P("gx", "gy", None),
            P("gx", "gy", None, None),
            *([P()] * 6),
            *([edge] * 6),
        ),
        out_specs=(P("gx", "gy", None), P("gx", "gy", None, None)),
        check_vma=False,
    )
```

time: 137 us -> 127 us (0.927)
  blocking collectives: 61.3 us -> 26.3 us
  waiting for transfers between devices: 14.4 us -> 35.9 us
  local copies, waits for them, and re-layouts: 0.05 us -> 4.97 us
  starting transfers between devices: 47.3 us -> 44.4 us
  Pallas kernels: 12.1 us -> 14.1 us
    all_to_all x1, blocking collectives: 61.3 us -> 26.3 us  [exchange(): lax.all_to_all(array, 'gy', 0, 0, axis_index_groups=group, tiled=True)]
    all_to_all x1, waiting for transfers between devices: 0.01 us -> 26.6 us  [exchange(): lax.all_to_all(array, 'gy', 0, 0, axis_index_groups=group, tiled=True)]
    all_to_all x1, starting transfers between devices: 16.2 us -> 3.93 us  [exchange(): lax.all_to_all(array, 'gy', 0, 0, axis_index_groups=group, tiled=True)]
    ppermute x1, starting transfers between devices: 8.13 us -> 15.6 us  [on_device(): far = lax.ppermute(far, 'gx', far_bands)]
    ppermute x1, waiting for transfers between devices: 7.11 us -> 0.41 us  [on_device(): far = lax.ppermute(far, 'gx', far_bands)]
    unnamed x16, local copies, waits for them, and re-layouts: 0.05 us -> 4.97 us
    ppermute x1, waiting for transfers between devices: 0.01 us -> 3.82 us  [on_device(): near = lax.ppermute(near, 'gx', near_bands)]
    ppermute x1, waiting for transfers between devices: 7.28 us -> 4.71 us  [on_device(): other = lax.ppermute(table, 'gy', far_sectors)]
  transfers between devices with their start and end apart: 7 -> 8, of which waited for: 2 -> 5; matrix products, arithmetic and copies ran while one was open for 0% -> 0% of each run, Pallas kernels for 2% -> 4%
where the time goes in v4:
time: 127 us
  starting transfers between devices  44.4 us (35%)
  waiting for transfers between devices  35.9 us (28%)
  blocking collectives  26.3 us (21%)
  Pallas kernels  14.1 us (11%)
  local copies, waits for them, and re-layouts  4.97 us (4%)
    all_to_all x1, waiting for transfers between devices, exchange(): lax.all_to_all(array, 'gy', 0, 0, axis_index_groups=group, tiled=True)  26.6 us
    all_to_all x1, blocking collectives, exchange(): lax.all_to_all(array, 'gy', 0, 0, axis_index_groups=group, tiled=True)  26.3 us
    ppermute x1, starting transfers between devices, on_device(): far = lax.ppermute(far, 'gx', far_bands)  15.6 us
    ppermute x1, starting transfers between devices, on_device(): other = lax.ppermute(other, 'gy', far_sectors)  9.08 us
    ppermute x1, starting transfers between devices, on_device(): other = lax.ppermute(table, 'gy', far_sectors)  8.09 us
    unnamed x16, local copies, waits for them, and re-layouts  4.97 us
    ppermute x1, waiting for transfers between devices, on_device(): other = lax.ppermute(table, 'gy', far_sectors)  4.71 us
    all_to_all x1, starting transfers between devices, exchange(): lax.all_to_all(array, 'gy', 0, 0, axis_index_groups=group, tiled=True)  3.93 us
  transfers between devices with their start and end apart: 8, of which 5 were waited for; matrix products, arithmetic and copies ran while one was open for 0% of the time, Pallas kernels for 4%

profile of v4, /device:TPU:6, one launch (start us, length us, event | category | flops | bytes accessed | tf_op | source)
XLA Modules:
  0.0 126.5 jit_solution(927924638453163781)
XLA Ops:
  0.6 0.9 shard_map.149
  1.5 15.6 %collective-permute-start = (bf16[64,512]{1,0:T(8,128)(2,1)S(1)}, bf16[64,512]{1,0:T(8,128)(2,1)S(1)}, u32[]{:S(2)}, u32[]{:S(2)}) collective-permute-start(bf16[64,512]{1,0:T(8,128)(2,1)S(1)} %get-tuple-element.24), channel_id=1, source_target_pairs={{64,128},{128,64},{192,256},{256,192},{320,384},{384,320},{65,129}... | collective-permute-start | bytes 196616 | tf_op jit(solution)/shard_map/ppermute | solution.py:329
  17.2 1.9 %collective-permute-start.1 = (bf16[64,512]{1,0:T(8,128)(2,1)S(1)}, bf16[64,512]{1,0:T(8,128)(2,1)S(1)}, u32[]{:S(2)}, u32[]{:S(2)}) collective-permute-start(bf16[64,512]{1,0:T(8,128)(2,1)S(1)} %get-tuple-element.25), channel_id=1, source_target_pairs={{0,64},{64,0},{128,192},{192,128},{256,320},{320,256},{384,448},{4... | collective-permute-start | bytes 196616 | tf_op jit(solution)/shard_map/ppermute | solution.py:330
  19.5 3.8 %collective-permute-done.1.near = bf16[64,512]{1,0:T(8,128)(2,1)S(1)} collective-permute-done((bf16[64,512]{1,0:T(8,128)(2,1)S(1)}, bf16[64,512]{1,0:T(8,128)(2,1)S(1)}, u32[]{:S(2)}, u32[]{:S(2)}) %collective-permute-start.1) | collective-permute-done | bytes 65568 | tf_op jit(solution)/shard_map/ppermute | solution.py:330
  24.1 9.1 %collective-permute-start.2 = (bf16[4,8,512]{2,1,0:T(8,128)(2,1)S(1)}, bf16[4,8,512]{2,1,0:T(8,128)(2,1)S(1)}, u32[]{:S(2)}, u32[]{:S(2)}) collective-permute-start(bf16[4,8,512]{2,1,0:T(8,128)(2,1)S(1)} %get-tuple-element.27), channel_id=1, source_target_pairs={{0,63},{1,2},{2,1},{3,4},{4,3},{5,6},{6,5},{7,8},{8,7},{9,10},{10,... | collective-permute-start | bytes 98312 | tf_op jit(solution)/shard_map/ppermute | solution.py:343
  33.2 1.9 %collective-permute-start.3 = (bf16[4,8,512]{2,1,0:T(8,128)(2,1)S(1)}, bf16[4,8,512]{2,1,0:T(8,128)(2,1)S(1)}, u32[]{:S(2)}, u32[]{:S(2)}) collective-permute-start(bf16[4,8,512]{2,1,0:T(8,128)(2,1)S(1)} %get-tuple-element.28), channel_id=1, source_target_pairs={{0,1},{1,0},{2,3},{3,2},{4,5},{5,4},{6,7},{7,6},{8,9},{9,8},{10,11... | collective-permute-start | bytes 98312 | tf_op jit(solution)/shard_map/ppermute | solution.py:344
  35.1 2.5 %shard_map.150 = (f32[1024,512]{1,0:T(8,128)S(1)}, bf16[256,1024]{1,0:T(8,128)(2,1)S(1)}, bf16[256,512]{1,0:T(8,128)(2,1)S(1)}, bf16[3,512,512]{2,1,0:T(8,128)(2...) custom-call(bf16[64,512]{1,0:T(8,128)(2,1)S(1)} %collective-permute-done.far, ...), custom_call_target="tpu_custom_call" | custom-call | tf_op jit(solution)/shard_map/pallas_call | solution.py:353
  38.1 1.8 %shard_map.152 = (bf16[256,512]{1,0:T(8,128)(2,1)S(1)}, bf16[256,512]{1,0:T(8,128)(2,1)S(1)}) custom-call(f32[1024,512]{1,0:T(8,128)S(1)} %get-tuple-element.26.partial, bf16[4,8,512]{2,1,0:T(8,128)(2,1)S(1)} %collective-permute-done.2.other, bf16[4,8,512]{2,1,0:T(8,128)(2,1)S(1)} %collective-permute-done.3.mate, ...), custom_call_target="tpu_custom_call" | custom-call | tf_op jit(solution)/shard_map/pallas_call | solution.py:383
  39.8 1.9 %collective-permute-start.4 = (bf16[256,512]{1,0:T(8,128)(2,1)S(1)}, bf16[256,512]{1,0:T(8,128)(2,1)S(1)}, u32[]{:S(2)}, u32[]{:S(2)}) collective-permute-start(bf16[256,512]{1,0:T(8,128)(2,1)S(1)} %get-tuple-element.35.table), channel_id=1, source_target_pairs={{0,8},{1,9},{2,10},{3,11},{4,12},{5,13},{6,14},{7,15},{8,0},{9,1},... | collective-permute-start | bytes 786440 | tf_op jit(solution)/shard_map/ppermute | solution.py:391
  41.8 26.3 %all_to_all.16 = s32[32,1,128]{2,1,0:T(1,128)S(1)} all-to-all(s32[32,1,128]{2,1,0:T(1,128)S(1)} %bitcast.20), channel_id=1, replica_groups={{0,1,2,3,4,5,6,7,16,17,18,19,20,21,22,23,32,33,34,35,36,37,38,39,48,49,..., dimensions={0} | all-to-all | bytes 32768 | tf_op jit(solution)/shard_map/all_to_all | solution.py:318
  68.1 1.8 %shard_map.153 = bf16[1024,512]{1,0:T(8,128)(2,1)} custom-call(bf16[256,512]{1,0:T(8,128)(2,1)S(1)} %get-tuple-element.35.table, bf16[256,512]{1,0:T(8,128)(2,1)S(1)} %collective-permute-done.4.mirror, s32[32,128]{1,0:T(8,128)S(1)} %bitcast.19), custom_call_target="tpu_custom_call" | custom-call | tf_op jit(solution)/shard_map/pallas_call | solution.py:398
  70.0 3.9 %all-to-all-start.1 = ((bf16[32,32,512]{2,1,0:T(8,128)(2,1)}), bf16[32,32,512]{2,1,0:T(8,128)(2,1)S(1)}, u32[]{:S(2)}, u32[]{:S(2)}) async-start(bf16[32,32,512]{2,1,0:T(8,128)(2,1)} %bitcast.8), calls=%async_computation.1 | async-start | bytes 2097152 | tf_op jit(solution)/shard_map/all_to_all | solution.py:318
  74.5 0.8 copy-done.4
  75.3 26.6 %all-to-all-done.1 = bf16[32,32,512]{2,1,0:T(8,128)(2,1)S(1)} async-done(((bf16[32,32,512]{2,1,0:T(8,128)(2,1)}), bf16[32,32,512]{2,1,0:T(8,128)(2,1)S(1)}, u32[]{:S(2)}, u32[]{:S(2)}) %all-to-all-start.1) | async-done | bytes 1048608 | tf_op jit(solution)/shard_map/all_to_all | solution.py:318
  101.8 1.0 copy-done.1
  102.9 1.0 copy-done.2
  103.9 1.0 copy-done.5
  105.0 1.9 %shard_map.155 = (bf16[256,512]{1,0:T(8,128)(2,1)}, bf16[256,512]{1,0:T(8,128)(2,1)}) custom-call(bf16[1024,512]{1,0:T(8,128)(2,1)S(1)} %bitcast.16, f32[1024,512]{1,0:T(8,128)S(1)} %get-tuple-element.39.partial, bf16[256,1024]{1,0:T(8,128)(2,1)S(1)} %copy-done.5, bf16[256,512]{1,0:T(8,128)(2,1)S(1)} %get-tuple-element.37.first, ...), custom_call_target="tpu_custom_call" | custom-call | tf_op jit(solution)/shard_map/pallas_call | solution.py:404
  106.9 8.1 %collective-permute-start.5 = (bf16[256,512]{1,0:T(8,128)(2,1)}, bf16[256,512]{1,0:T(8,128)(2,1)S(1)}, u32[]{:S(2)}, u32[]{:S(2)}) collective-permute-start(bf16[256,512]{1,0:T(8,128)(2,1)} %get-tuple-element.41.own), channel_id=1, source_target_pairs={{0,63},{1,2},{2,1},{3,4},{4,3},{5,6},{6,5},{7,8},{8,7},{9,10},{10,... | collective-permute-start | bytes 786440 | tf_op jit(solution)/shard_map/ppermute | solution.py:411
  115.0 1.9 %collective-permute-start.6 = (bf16[256,512]{1,0:T(8,128)(2,1)}, bf16[256,512]{1,0:T(8,128)(2,1)S(1)}, u32[]{:S(2)}, u32[]{:S(2)}) collective-permute-start(bf16[256,512]{1,0:T(8,128)(2,1)} %get-tuple-element.41.own), channel_id=1, source_target_pairs={{0,1},{1,0},{2,3},{3,2},{4,5},{5,4},{6,7},{7,6},{8,9},{9,8},{10,11... | collective-permute-start | bytes 786440 | tf_op jit(solution)/shard_map/ppermute | solution.py:412
  116.9 1.8 %shard_map.156 = (f32[1024,512]{1,0:T(8,128)S(1)}, bf16[1024,512]{1,0:T(8,128)(2,1)S(1)}, bf16[128,1024]{1,0:T(8,128)(2,1)S(1)}) custom-call(bf16[256,512]{1,0:T(8,128)(2,1)} %get-tuple-element.41.own, bf16[128,512]{1,0:T(8,128)(2,1)S(1)} %bitcast.17, s32[8,128]{1,0:T(8,128)S(1)} %fusion.1.source, s32[8,128]{1,0:T(8,128)S(1)} %bitcast.21), custom_call_target="tpu_custom_call" | custom-call | tf_op jit(solution)/shard_map/pallas_call | solution.py:418
  118.8 4.7 %collective-permute-done.5.other = bf16[256,512]{1,0:T(8,128)(2,1)S(1)} collective-permute-done((bf16[256,512]{1,0:T(8,128)(2,1)}, bf16[256,512]{1,0:T(8,128)(2,1)S(1)}, u32[]{:S(2)}, u32[]{:S(2)}) %collective-permute-start.5) | collective-permute-done | bytes 262176 | tf_op jit(solution)/shard_map/ppermute | solution.py:411
  123.5 1.0 copy-done.3
  124.5 2.0 %shard_map.157 = bf16[128,512]{1,0:T(8,128)(2,1)} custom-call(f32[1024,512]{1,0:T(8,128)S(1)} %get-tuple-element.42.partial, bf16[256,512]{1,0:T(8,128)(2,1)S(1)} %collective-permute-done.5.other, bf16[256,512]{1,0:T(8,128)(2,1)S(1)} %collective-permute-done.6.mate, bf16[1024,512]{1,0:T(8,128)(2,1)S(1)} %get-tuple-element.43.picks, ...), custom_call_target="tpu_custom_call" | custom-call | tf_op jit(solution)/shard_map/pallas_call | solution.py:427
  (19 shorter events, 2.2 us)
Async XLA Ops:
  1.5 18.0 %collective-permute-start = (bf16[64,512]{1,0:T(8,128)(2,1)S(1)}, bf16[64,512]{1,0:T(8,128)(2,1)S(1)}, u32[]{:S(2)}, u32[]{:S(2)}) collective-permute-start(bf16[64,512]{1,0:T(8,128)(2,1)S(1)} %get-tuple-element.24), channel_id=1, source_target_pairs={{64,128},{128,64},{192,256},{256,192},{320,384},{384,320},{65,129}... | collective-permute-start | bytes 196616 | tf_op jit(solution)/shard_map/ppermute | solution.py:329
  17.2 6.2 %collective-permute-start.1 = (bf16[64,512]{1,0:T(8,128)(2,1)S(1)}, bf16[64,512]{1,0:T(8,128)(2,1)S(1)}, u32[]{:S(2)}, u32[]{:S(2)}) collective-permute-start(bf16[64,512]{1,0:T(8,128)(2,1)S(1)} %get-tuple-element.25), channel_id=1, source_target_pairs={{0,64},{64,0},{128,192},{192,128},{256,320},{320,256},{384,448},{4... | collective-permute-start | bytes 196616 | tf_op jit(solution)/shard_map/ppermute | solution.py:330
  24.1 13.9 %collective-permute-start.2 = (bf16[4,8,512]{2,1,0:T(8,128)(2,1)S(1)}, bf16[4,8,512]{2,1,0:T(8,128)(2,1)S(1)}, u32[]{:S(2)}, u32[]{:S(2)}) collective-permute-start(bf16[4,8,512]{2,1,0:T(8,128)(2,1)S(1)} %get-tuple-element.27), channel_id=1, source_target_pairs={{0,63},{1,2},{2,1},{3,4},{4,3},{5,6},{6,5},{7,8},{8,7},{9,10},{10,... | collective-permute-start | bytes 98312 | tf_op jit(solution)/shard_map/ppermute | solution.py:343
  33.2 4.9 %collective-permute-start.3 = (bf16[4,8,512]{2,1,0:T(8,128)(2,1)S(1)}, bf16[4,8,512]{2,1,0:T(8,128)(2,1)S(1)}, u32[]{:S(2)}, u32[]{:S(2)}) collective-permute-start(bf16[4,8,512]{2,1,0:T(8,128)(2,1)S(1)} %get-tuple-element.28), channel_id=1, source_target_pairs={{0,1},{1,0},{2,3},{3,2},{4,5},{5,4},{6,7},{7,6},{8,9},{9,8},{10,11... | collective-permute-start | bytes 98312 | tf_op jit(solution)/shard_map/ppermute | solution.py:344
  39.8 28.3 %collective-permute-start.4 = (bf16[256,512]{1,0:T(8,128)(2,1)S(1)}, bf16[256,512]{1,0:T(8,128)(2,1)S(1)}, u32[]{:S(2)}, u32[]{:S(2)}) collective-permute-start(bf16[256,512]{1,0:T(8,128)(2,1)S(1)} %get-tuple-element.35.table), channel_id=1, source_target_pairs={{0,8},{1,9},{2,10},{3,11},{4,12},{5,13},{6,14},{7,15},{8,0},{9,1},... | collective-permute-start | bytes 786440 | tf_op jit(solution)/shard_map/ppermute | solution.py:391
  70.0 31.9 %all-to-all-start.1 = ((bf16[32,32,512]{2,1,0:T(8,128)(2,1)}), bf16[32,32,512]{2,1,0:T(8,128)(2,1)S(1)}, u32[]{:S(2)}, u32[]{:S(2)}) async-start(bf16[32,32,512]{2,1,0:T(8,128)(2,1)} %bitcast.8), calls=%async_computation.1 | async-start | bytes 2097152 | tf_op jit(solution)/shard_map/all_to_all | solution.py:318
  74.5 0.8 copy-start.4
  101.8 1.0 copy-start.1
  102.9 1.0 copy-start.2
  103.9 1.0 copy-start.5
  105.0 11.9 %copy-start.7 = (s32[1,1,1024]{2,1,0:T(1,128)S(1)}, s32[1,1,1024]{2,1,0:T(1,128)}, u32[]{:S(2)}) copy-start(s32[1,1,1024]{2,1,0:T(1,128)} %param.26) | copy-start | bytes 12292
  105.0 12.0 %copy-start = (bf16[2,64,512]{2,1,0:T(8,128)(2,1)S(1)}, bf16[2,64,512]{2,1,0:T(8,128)(2,1)}, u32[]{:S(2)}) copy-start(bf16[2,64,512]{2,1,0:T(8,128)(2,1)} %grid.5) | copy-start | bytes 393220
  105.0 12.0 %copy-start.6 = (s32[1,1,1024]{2,1,0:T(1,128)S(1)}, s32[1,1,1024]{2,1,0:T(1,128)}, u32[]{:S(2)}) copy-start(s32[1,1,1024]{2,1,0:T(1,128)} %param.27) | copy-start | bytes 12292
  106.9 16.6 %collective-permute-start.5 = (bf16[256,512]{1,0:T(8,128)(2,1)}, bf16[256,512]{1,0:T(8,128)(2,1)S(1)}, u32[]{:S(2)}, u32[]{:S(2)}) collective-permute-start(bf16[256,512]{1,0:T(8,128)(2,1)} %get-tuple-element.41.own), channel_id=1, source_target_pairs={{0,63},{1,2},{2,1},{3,4},{4,3},{5,6},{6,5},{7,8},{8,7},{9,10},{10,... | collective-permute-start | bytes 786440 | tf_op jit(solution)/shard_map/ppermute | solution.py:411
  115.0 8.5 %collective-permute-start.6 = (bf16[256,512]{1,0:T(8,128)(2,1)}, bf16[256,512]{1,0:T(8,128)(2,1)S(1)}, u32[]{:S(2)}, u32[]{:S(2)}) collective-permute-start(bf16[256,512]{1,0:T(8,128)(2,1)} %get-tuple-element.41.own), channel_id=1, source_target_pairs={{0,1},{1,0},{2,3},{3,2},{4,5},{5,4},{6,7},{7,6},{8,9},{9,8},{10,11... | collective-permute-start | bytes 786440 | tf_op jit(solution)/shard_map/ppermute | solution.py:412
  123.5 1.0 copy-start.3

commit v5 on v4

--- a/solution.py
+++ b/solution.py
@@ -218,35 +218,45 @@
     nodes = table.shape[0]
     asked = together(slots)
     lane = lax.broadcasted_iota(jnp.int32, asked.shape, 1)
-    second = (lane & (2 * CAP - 1)) >= CAP
-    for ref, req in ((table, jnp.where(second, -1, asked)), (mirror, jnp.where(second, asked, -1))):
-        for c in range(0, send_out.shape[0], CHUNK):
-            rows = slice(c, c + CHUNK)
-            part = dot(pick(column(req, rows), nodes), ref[...]).astype(jnp.bfloat16)
-            send_out[rows, :] = part if ref is table else send_out[rows, :] + part
-
-
-def target_kernel(first, target, partial, spread_out):
+    asked = asked + jnp.where((lane & (2 * CAP - 1)) >= CAP, nodes, 0)
+    for c in range(0, send_out.shape[0], CHUNK):
+        rows = slice(c, c + CHUNK)
+        col = column(asked, rows)
+        acc = dot(pick(col, nodes), table[...]) + dot(pick(col - nodes, nodes), mirror[...])
+        send_out[rows, :] = acc.astype(jnp.bfloat16)
+
+
+def target_kernel(first, target, w_update, w_next, partial, spread_out, w_out, sems):
+    pairs = ((w_update, w_out.at[0]), (w_next, w_out.at[1]))
+    copies = [pltpu.make_async_copy(a, b, sems.at[i]) for i, (a, b) in enumerate(pairs)]
+    for copy in copies:
+        copy.start()
     nodes = first.shape[0]
     tgt = target[...]
     for c in range(0, partial.shape[0], CHUNK):
         rows = slice(c, c + CHUNK)
         partial[rows, :] = dot(pick(column(tgt, rows), nodes), first[...])
     spread_out[...] = spread(tgt, nodes)
+    for copy in copies:
+        copy.wait()
 
 
 def process_kernel(
-    picked, partial, spreading, first, w_update, w_next, second_out, table_out, messages
+    picked, partial, spreading, first, weights, second_out, table_out, messages
 ):
     for c in range(0, picked.shape[0], CHUNK):
         rows = slice(c, c + CHUNK)
         messages[rows, :] = message(partial[rows, :] + picked[rows, :].astype(jnp.float32))
-    second = refresh(first[...], dot(spreading[...], messages[...]), w_update[...])
+    second = refresh(first[...], dot(spreading[...], messages[...]), weights[0])
     second_out[...] = second
-    table_out[...] = dot(second, w_next[...]).astype(jnp.bfloat16)
-
-
-def reach_kernel(own, grid, source, target, partial, picks_out, spread_out):
+    table_out[...] = dot(second, weights[1]).astype(jnp.bfloat16)
+
+
+def reach_kernel(
+    own, grid, source, target, w_update, partial, picks_out, spread_out, w_out, sem
+):
+    copy = pltpu.make_async_copy(w_update, w_out, sem)
+    copy.start()
     latent = grid[...]
     cells = latent.shape[0]
     nodes = own.shape[0]
@@ -258,6 +268,7 @@
         partial[rows, :] = acc + dot(pick(col, nodes), own[...])
         picks_out[rows, :] = pick(col - nodes, 2 * nodes)
     spread_out[...] = spread(tgt, cells)
+    copy.wait()
 
 
 def decode_kernel(
@@ -390,11 +401,16 @@
     following, slots = lax.optimization_barrier((following, slots))
     mirror = lax.ppermute(following, "gy", [(i, i ^ HALF) for i in range(sectors)])
     slots = exchange(slots)
-    partial, spreading = pl.pallas_call(
+    partial, spreading, weights = pl.pallas_call(
         target_kernel,
-        out_shape=(partial_shape, spread_shape),
-        compiler_params=params,
-    )(first, order)
+        in_specs=[vmem] * 2 + [hbm] * 2,
+        out_specs=(vmem,) * 3,
+        out_shape=(
+            partial_shape, spread_shape, jax.ShapeDtypeStruct((2, width, width), bf16)
+        ),
+        scratch_shapes=[pltpu.SemaphoreType.DMA((2,))],
+        compiler_params=params,
+    )(first, order, pinned(process_update), pinned(decode_message))
     send = pl.pallas_call(
         request_kernel,
         out_shape=jax.ShapeDtypeStruct((edges, width), bf16),
@@ -406,7 +422,7 @@
         out_shape=(table_shape, table_shape),
         scratch_shapes=[messages],
         compiler_params=params,
-    )(picked, partial, spreading, first, process_update, decode_message)
+    )(picked, partial, spreading, first, weights)
 
     other = lax.ppermute(table, "gy", far_sectors)
     mate = lax.ppermute(table, "gy", near_sectors)
@@ -415,21 +431,25 @@
     piece = jnp.where(owner == sector, 0, jnp.where(owner == sector ^ 1, 1, 2))
     row = piece * nodes + source % nodes
     target = decode_target.reshape(-1, LANES)
-    partial, picks, spreading = pl.pallas_call(
+    partial, picks, spreading, update = pl.pallas_call(
         reach_kernel,
+        in_specs=[vmem] * 4 + [hbm],
+        out_specs=(vmem,) * 4,
         out_shape=(
             partial_shape,
             jax.ShapeDtypeStruct((edges, 2 * nodes), bf16),
             jax.ShapeDtypeStruct((cells, edges), bf16),
+            jax.ShapeDtypeStruct((width, width), bf16),
         ),
-        compiler_params=params,
-    )(table, grid_rows, row, target)
+        scratch_shapes=[pltpu.SemaphoreType.DMA(())],
+        compiler_params=params,
+    )(table, grid_rows, row, target, pinned(decode_update))
     grid_output = pl.pallas_call(
         decode_kernel,
         out_shape=jax.ShapeDtypeStruct((cells, width), bf16),
         scratch_shapes=[messages],
         compiler_params=params,
-    )(partial, other, mate, picks, spreading, grid_rows, decode_update)
+    )(partial, other, mate, picks, spreading, grid_rows, update)
     return (
         grid_output.reshape(lat_rows, lon_cols, width),
         second.reshape(1, 1, nodes, width),

time: 127 us -> 125 us (0.984)
  waiting for transfers between devices: 35.9 us -> 34.1 us
    all_to_all x1, waiting for transfers between devices: 26.6 us -> 25 us  [exchange(): lax.all_to_all(array, 'gy', 0, 0, axis_index_groups=group, tiled=True)]
    unnamed x16 -> x14, local copies, waits for them, and re-layouts: 4.97 us -> 4.03 us
  transfers between devices with their start and end apart: 8 -> 8, of which waited for: 5 -> 5; matrix products, arithmetic and copies ran while one was open for 0% -> 0% of each run, Pallas kernels for 4% -> 5%
where the time goes in v5:
time: 125 us
  starting transfers between devices  44.4 us (36%)
  waiting for transfers between devices  34.1 us (27%)
  blocking collectives  26.3 us (21%)
  Pallas kernels  14.9 us (12%)
  local copies, waits for them, and re-layouts  4.03 us (3%)
    all_to_all x1, blocking collectives, exchange(): lax.all_to_all(array, 'gy', 0, 0, axis_index_groups=group, tiled=True)  26.3 us
    all_to_all x1, waiting for transfers between devices, exchange(): lax.all_to_all(array, 'gy', 0, 0, axis_index_groups=group, tiled=True)  25 us
    ppermute x1, starting transfers between devices, on_device(): far = lax.ppermute(far, 'gx', far_bands)  15.6 us
    ppermute x1, starting transfers between devices, on_device(): other = lax.ppermute(other, 'gy', far_sectors)  9.08 us
    ppermute x1, starting transfers between devices, on_device(): other = lax.ppermute(table, 'gy', far_sectors)  8.08 us
    ppermute x1, waiting for transfers between devices, on_device(): other = lax.ppermute(table, 'gy', far_sectors)  4.5 us
    unnamed x14, local copies, waits for them, and re-layouts  4.03 us
    all_to_all x1, starting transfers between devices, exchange(): lax.all_to_all(array, 'gy', 0, 0, axis_index_groups=group, tiled=True)  3.93 us
  transfers between devices with their start and end apart: 8, of which 5 were waited for; matrix products, arithmetic and copies ran while one was open for 0% of the time, Pallas kernels for 5%

profile of v5, /device:TPU:6, one launch (start us, length us, event | category | flops | bytes accessed | tf_op | source)
XLA Modules:
  0.0 124.6 jit_solution(15676461636206813501)
XLA Ops:
  0.6 0.9 shard_map.149
  1.5 15.6 %collective-permute-start = (bf16[64,512]{1,0:T(8,128)(2,1)S(1)}, bf16[64,512]{1,0:T(8,128)(2,1)S(1)}, u32[]{:S(2)}, u32[]{:S(2)}) collective-permute-start(bf16[64,512]{1,0:T(8,128)(2,1)S(1)} %get-tuple-element.26), channel_id=1, source_target_pairs={{64,128},{128,64},{192,256},{256,192},{320,384},{384,320},{65,129}... | collective-permute-start | bytes 196616 | tf_op jit(solution)/shard_map/ppermute | solution.py:340
  17.2 1.9 %collective-permute-start.1 = (bf16[64,512]{1,0:T(8,128)(2,1)S(1)}, bf16[64,512]{1,0:T(8,128)(2,1)S(1)}, u32[]{:S(2)}, u32[]{:S(2)}) collective-permute-start(bf16[64,512]{1,0:T(8,128)(2,1)S(1)} %get-tuple-element.27), channel_id=1, source_target_pairs={{0,64},{64,0},{128,192},{192,128},{256,320},{320,256},{384,448},{4... | collective-permute-start | bytes 196616 | tf_op jit(solution)/shard_map/ppermute | solution.py:341
  19.5 3.8 %collective-permute-done.1.near = bf16[64,512]{1,0:T(8,128)(2,1)S(1)} collective-permute-done((bf16[64,512]{1,0:T(8,128)(2,1)S(1)}, bf16[64,512]{1,0:T(8,128)(2,1)S(1)}, u32[]{:S(2)}, u32[]{:S(2)}) %collective-permute-start.1) | collective-permute-done | bytes 65568 | tf_op jit(solution)/shard_map/ppermute | solution.py:341
  24.1 9.1 %collective-permute-start.2 = (bf16[4,8,512]{2,1,0:T(8,128)(2,1)S(1)}, bf16[4,8,512]{2,1,0:T(8,128)(2,1)S(1)}, u32[]{:S(2)}, u32[]{:S(2)}) collective-permute-start(bf16[4,8,512]{2,1,0:T(8,128)(2,1)S(1)} %get-tuple-element.29), channel_id=1, source_target_pairs={{0,63},{1,2},{2,1},{3,4},{4,3},{5,6},{6,5},{7,8},{8,7},{9,10},{10,... | collective-permute-start | bytes 98312 | tf_op jit(solution)/shard_map/ppermute | solution.py:354
  33.2 1.9 %collective-permute-start.3 = (bf16[4,8,512]{2,1,0:T(8,128)(2,1)S(1)}, bf16[4,8,512]{2,1,0:T(8,128)(2,1)S(1)}, u32[]{:S(2)}, u32[]{:S(2)}) collective-permute-start(bf16[4,8,512]{2,1,0:T(8,128)(2,1)S(1)} %get-tuple-element.30), channel_id=1, source_target_pairs={{0,1},{1,0},{2,3},{3,2},{4,5},{5,4},{6,7},{7,6},{8,9},{9,8},{10,11... | collective-permute-start | bytes 98312 | tf_op jit(solution)/shard_map/ppermute | solution.py:355
  35.1 2.5 %shard_map.150 = (f32[1024,512]{1,0:T(8,128)S(1)}, bf16[256,1024]{1,0:T(8,128)(2,1)S(1)}, bf16[256,512]{1,0:T(8,128)(2,1)S(1)}, bf16[3,512,512]{2,1,0:T(8,128)(2...) custom-call(bf16[64,512]{1,0:T(8,128)(2,1)S(1)} %collective-permute-done.far, ...), custom_call_target="tpu_custom_call" | custom-call | tf_op jit(solution)/shard_map/pallas_call | solution.py:364
  38.1 1.8 %shard_map.152 = (bf16[256,512]{1,0:T(8,128)(2,1)S(1)}, bf16[256,512]{1,0:T(8,128)(2,1)S(1)}) custom-call(f32[1024,512]{1,0:T(8,128)S(1)} %get-tuple-element.28.partial, bf16[4,8,512]{2,1,0:T(8,128)(2,1)S(1)} %collective-permute-done.2.other, bf16[4,8,512]{2,1,0:T(8,128)(2,1)S(1)} %collective-permute-done.3.mate, ...), custom_call_target="tpu_custom_call" | custom-call | tf_op jit(solution)/shard_map/pallas_call | solution.py:394
  39.8 1.9 %collective-permute-start.4 = (bf16[256,512]{1,0:T(8,128)(2,1)S(1)}, bf16[256,512]{1,0:T(8,128)(2,1)S(1)}, u32[]{:S(2)}, u32[]{:S(2)}) collective-permute-start(bf16[256,512]{1,0:T(8,128)(2,1)S(1)} %get-tuple-element.37.table), channel_id=1, source_target_pairs={{0,8},{1,9},{2,10},{3,11},{4,12},{5,13},{6,14},{7,15},{8,0},{9,1},... | collective-permute-start | bytes 786440 | tf_op jit(solution)/shard_map/ppermute | solution.py:402
  41.8 26.3 %all_to_all.16 = s32[32,1,128]{2,1,0:T(1,128)S(1)} all-to-all(s32[32,1,128]{2,1,0:T(1,128)S(1)} %bitcast.20), channel_id=1, replica_groups={{0,1,2,3,4,5,6,7,16,17,18,19,20,21,22,23,32,33,34,35,36,37,38,39,48,49,..., dimensions={0} | all-to-all | bytes 32768 | tf_op jit(solution)/shard_map/all_to_all | solution.py:329
  68.1 1.8 %shard_map.153 = bf16[1024,512]{1,0:T(8,128)(2,1)} custom-call(bf16[256,512]{1,0:T(8,128)(2,1)S(1)} %get-tuple-element.37.table, bf16[256,512]{1,0:T(8,128)(2,1)S(1)} %collective-permute-done.4.mirror, s32[32,128]{1,0:T(8,128)S(1)} %bitcast.19), custom_call_target="tpu_custom_call" | custom-call | tf_op jit(solution)/shard_map/pallas_call | solution.py:414
  70.0 3.9 %all-to-all-start.1 = ((bf16[32,32,512]{2,1,0:T(8,128)(2,1)}), bf16[32,32,512]{2,1,0:T(8,128)(2,1)S(1)}, u32[]{:S(2)}, u32[]{:S(2)}) async-start(bf16[32,32,512]{2,1,0:T(8,128)(2,1)} %bitcast.8), calls=%async_computation.1 | async-start | bytes 2097152 | tf_op jit(solution)/shard_map/all_to_all | solution.py:329
  73.9 1.2 shard_map.154
  75.1 1.0 copy-done.1
  76.1 0.8 copy-done.3
  76.9 25.0 %all-to-all-done.1 = bf16[32,32,512]{2,1,0:T(8,128)(2,1)S(1)} async-done(((bf16[32,32,512]{2,1,0:T(8,128)(2,1)}), bf16[32,32,512]{2,1,0:T(8,128)(2,1)S(1)}, u32[]{:S(2)}, u32[]{:S(2)}) %all-to-all-start.1) | async-done | bytes 1048608 | tf_op jit(solution)/shard_map/all_to_all | solution.py:329
  101.9 1.2 copy-done.2
  103.1 1.0 copy-done.4
  104.1 1.9 %shard_map.155 = (bf16[256,512]{1,0:T(8,128)(2,1)}, bf16[256,512]{1,0:T(8,128)(2,1)}) custom-call(bf16[1024,512]{1,0:T(8,128)(2,1)S(1)} %bitcast.16, f32[1024,512]{1,0:T(8,128)S(1)} %get-tuple-element.41.partial, bf16[256,1024]{1,0:T(8,128)(2,1)S(1)} %copy-done.4, bf16[256,512]{1,0:T(8,128)(2,1)S(1)} %get-tuple-element.39.first, ...), custom_call_target="tpu_custom_call" | custom-call | tf_op jit(solution)/shard_map/pallas_call | solution.py:420
  106.0 8.1 %collective-permute-start.5 = (bf16[256,512]{1,0:T(8,128)(2,1)}, bf16[256,512]{1,0:T(8,128)(2,1)S(1)}, u32[]{:S(2)}, u32[]{:S(2)}) collective-permute-start(bf16[256,512]{1,0:T(8,128)(2,1)} %get-tuple-element.44.own), channel_id=1, source_target_pairs={{0,63},{1,2},{2,1},{3,4},{4,3},{5,6},{6,5},{7,8},{8,7},{9,10},{10,... | collective-permute-start | bytes 786440 | tf_op jit(solution)/shard_map/ppermute | solution.py:427
  114.1 1.9 %collective-permute-start.6 = (bf16[256,512]{1,0:T(8,128)(2,1)}, bf16[256,512]{1,0:T(8,128)(2,1)S(1)}, u32[]{:S(2)}, u32[]{:S(2)}) collective-permute-start(bf16[256,512]{1,0:T(8,128)(2,1)} %get-tuple-element.44.own), channel_id=1, source_target_pairs={{0,1},{1,0},{2,3},{3,2},{4,5},{5,4},{6,7},{7,6},{8,9},{9,8},{10,11... | collective-permute-start | bytes 786440 | tf_op jit(solution)/shard_map/ppermute | solution.py:428
  116.1 2.0 %shard_map.156 = (f32[1024,512]{1,0:T(8,128)S(1)}, bf16[1024,512]{1,0:T(8,128)(2,1)S(1)}, bf16[128,1024]{1,0:T(8,128)(2,1)S(1)}, bf16[512,512]{1,0:T(8,128)(2,1)S(1)}) custom-call(bf16[256,512]{1,0:T(8,128)(2,1)} %get-tuple-element.44.own, bf16[128,512]{1,0:T(8,128)(2,1)S(1)} %bitcast.17, s32[8,128]{1,0:T(8,128)S(1)} %fusion.1.source, ...), custom_call_target="tpu_custom_call" | custom-call | tf_op jit(solution)/shard_map/pallas_call | solution.py:434
  118.1 4.5 %collective-permute-done.5.other = bf16[256,512]{1,0:T(8,128)(2,1)S(1)} collective-permute-done((bf16[256,512]{1,0:T(8,128)(2,1)}, bf16[256,512]{1,0:T(8,128)(2,1)S(1)}, u32[]{:S(2)}, u32[]{:S(2)}) %collective-permute-start.5) | collective-permute-done | bytes 262176 | tf_op jit(solution)/shard_map/ppermute | solution.py:427
  122.6 2.0 %shard_map.157 = bf16[128,512]{1,0:T(8,128)(2,1)} custom-call(f32[1024,512]{1,0:T(8,128)S(1)} %get-tuple-element.45.partial, bf16[256,512]{1,0:T(8,128)(2,1)S(1)} %collective-permute-done.5.other, bf16[256,512]{1,0:T(8,128)(2,1)S(1)} %collective-permute-done.6.mate, bf16[1024,512]{1,0:T(8,128)(2,1)S(1)} %get-tuple-element.46.picks, ...), custom_call_target="tpu_custom_call" | custom-call | tf_op jit(solution)/shard_map/pallas_call | solution.py:447
  (17 shorter events, 1.6 us)
Async XLA Ops:
  1.5 18.0 %collective-permute-start = (bf16[64,512]{1,0:T(8,128)(2,1)S(1)}, bf16[64,512]{1,0:T(8,128)(2,1)S(1)}, u32[]{:S(2)}, u32[]{:S(2)}) collective-permute-start(bf16[64,512]{1,0:T(8,128)(2,1)S(1)} %get-tuple-element.26), channel_id=1, source_target_pairs={{64,128},{128,64},{192,256},{256,192},{320,384},{384,320},{65,129}... | collective-permute-start | bytes 196616 | tf_op jit(solution)/shard_map/ppermute | solution.py:340
  17.2 6.2 %collective-permute-start.1 = (bf16[64,512]{1,0:T(8,128)(2,1)S(1)}, bf16[64,512]{1,0:T(8,128)(2,1)S(1)}, u32[]{:S(2)}, u32[]{:S(2)}) collective-permute-start(bf16[64,512]{1,0:T(8,128)(2,1)S(1)} %get-tuple-element.27), channel_id=1, source_target_pairs={{0,64},{64,0},{128,192},{192,128},{256,320},{320,256},{384,448},{4... | collective-permute-start | bytes 196616 | tf_op jit(solution)/shard_map/ppermute | solution.py:341
  24.1 13.9 %collective-permute-start.2 = (bf16[4,8,512]{2,1,0:T(8,128)(2,1)S(1)}, bf16[4,8,512]{2,1,0:T(8,128)(2,1)S(1)}, u32[]{:S(2)}, u32[]{:S(2)}) collective-permute-start(bf16[4,8,512]{2,1,0:T(8,128)(2,1)S(1)} %get-tuple-element.29), channel_id=1, source_target_pairs={{0,63},{1,2},{2,1},{3,4},{4,3},{5,6},{6,5},{7,8},{8,7},{9,10},{10,... | collective-permute-start | bytes 98312 | tf_op jit(solution)/shard_map/ppermute | solution.py:354
  33.2 4.9 %collective-permute-start.3 = (bf16[4,8,512]{2,1,0:T(8,128)(2,1)S(1)}, bf16[4,8,512]{2,1,0:T(8,128)(2,1)S(1)}, u32[]{:S(2)}, u32[]{:S(2)}) collective-permute-start(bf16[4,8,512]{2,1,0:T(8,128)(2,1)S(1)} %get-tuple-element.30), channel_id=1, source_target_pairs={{0,1},{1,0},{2,3},{3,2},{4,5},{5,4},{6,7},{7,6},{8,9},{9,8},{10,11... | collective-permute-start | bytes 98312 | tf_op jit(solution)/shard_map/ppermute | solution.py:355
  39.8 28.3 %collective-permute-start.4 = (bf16[256,512]{1,0:T(8,128)(2,1)S(1)}, bf16[256,512]{1,0:T(8,128)(2,1)S(1)}, u32[]{:S(2)}, u32[]{:S(2)}) collective-permute-start(bf16[256,512]{1,0:T(8,128)(2,1)S(1)} %get-tuple-element.37.table), channel_id=1, source_target_pairs={{0,8},{1,9},{2,10},{3,11},{4,12},{5,13},{6,14},{7,15},{8,0},{9,1},... | collective-permute-start | bytes 786440 | tf_op jit(solution)/shard_map/ppermute | solution.py:402
  70.0 31.9 %all-to-all-start.1 = ((bf16[32,32,512]{2,1,0:T(8,128)(2,1)}), bf16[32,32,512]{2,1,0:T(8,128)(2,1)S(1)}, u32[]{:S(2)}, u32[]{:S(2)}) async-start(bf16[32,32,512]{2,1,0:T(8,128)(2,1)} %bitcast.8), calls=%async_computation.1 | async-start | bytes 2097152 | tf_op jit(solution)/shard_map/all_to_all | solution.py:329
  75.1 1.0 copy-start.1
  76.1 0.8 copy-start.3
  101.8 1.2 copy-start.2
  103.1 1.0 copy-start.4
  104.1 11.9 %copy-start.6 = (s32[1,1,1024]{2,1,0:T(1,128)S(1)}, s32[1,1,1024]{2,1,0:T(1,128)}, u32[]{:S(2)}) copy-start(s32[1,1,1024]{2,1,0:T(1,128)} %param.26) | copy-start | bytes 12292
  104.1 12.0 %copy-start = (bf16[2,64,512]{2,1,0:T(8,128)(2,1)S(1)}, bf16[2,64,512]{2,1,0:T(8,128)(2,1)}, u32[]{:S(2)}) copy-start(bf16[2,64,512]{2,1,0:T(8,128)(2,1)} %grid.5) | copy-start | bytes 393220
  104.1 12.0 %copy-start.5 = (s32[1,1,1024]{2,1,0:T(1,128)S(1)}, s32[1,1,1024]{2,1,0:T(1,128)}, u32[]{:S(2)}) copy-start(s32[1,1,1024]{2,1,0:T(1,128)} %param.27) | copy-start | bytes 12292
  106.0 16.6 %collective-permute-start.5 = (bf16[256,512]{1,0:T(8,128)(2,1)}, bf16[256,512]{1,0:T(8,128)(2,1)S(1)}, u32[]{:S(2)}, u32[]{:S(2)}) collective-permute-start(bf16[256,512]{1,0:T(8,128)(2,1)} %get-tuple-element.44.own), channel_id=1, source_target_pairs={{0,63},{1,2},{2,1},{3,4},{4,3},{5,6},{6,5},{7,8},{8,7},{9,10},{10,... | collective-permute-start | bytes 786440 | tf_op jit(solution)/shard_map/ppermute | solution.py:427
  114.1 8.5 %collective-permute-start.6 = (bf16[256,512]{1,0:T(8,128)(2,1)}, bf16[256,512]{1,0:T(8,128)(2,1)S(1)}, u32[]{:S(2)}, u32[]{:S(2)}) collective-permute-start(bf16[256,512]{1,0:T(8,128)(2,1)} %get-tuple-element.44.own), channel_id=1, source_target_pairs={{0,1},{1,0},{2,3},{3,2},{4,5},{5,4},{6,7},{7,6},{8,9},{9,8},{10,11... | collective-permute-start | bytes 786440 | tf_op jit(solution)/shard_map/ppermute | solution.py:428

commit v6 on v5

--- a/solution.py
+++ b/solution.py
@@ -226,30 +226,18 @@
         send_out[rows, :] = acc.astype(jnp.bfloat16)
 
 
-def target_kernel(first, target, w_update, w_next, partial, spread_out, w_out, sems):
-    pairs = ((w_update, w_out.at[0]), (w_next, w_out.at[1]))
-    copies = [pltpu.make_async_copy(a, b, sems.at[i]) for i, (a, b) in enumerate(pairs)]
-    for copy in copies:
-        copy.start()
+def process_kernel(
+    picked, target, first, w_update, w_next, second_out, table_out, messages
+):
     nodes = first.shape[0]
     tgt = target[...]
-    for c in range(0, partial.shape[0], CHUNK):
-        rows = slice(c, c + CHUNK)
-        partial[rows, :] = dot(pick(column(tgt, rows), nodes), first[...])
-    spread_out[...] = spread(tgt, nodes)
-    for copy in copies:
-        copy.wait()
-
-
-def process_kernel(
-    picked, partial, spreading, first, weights, second_out, table_out, messages
-):
     for c in range(0, picked.shape[0], CHUNK):
         rows = slice(c, c + CHUNK)
-        messages[rows, :] = message(partial[rows, :] + picked[rows, :].astype(jnp.float32))
-    second = refresh(first[...], dot(spreading[...], messages[...]), weights[0])
+        acc = dot(pick(column(tgt, rows), nodes), first[...])
+        messages[rows, :] = message(acc + picked[rows, :].astype(jnp.float32))
+    second = refresh(first[...], dot(spread(tgt, nodes), messages[...]), w_update[...])
     second_out[...] = second
-    table_out[...] = dot(second, weights[1]).astype(jnp.bfloat16)
+    table_out[...] = dot(second, w_next[...]).astype(jnp.bfloat16)
 
 
 def reach_kernel(
@@ -401,16 +389,6 @@
     following, slots = lax.optimization_barrier((following, slots))
     mirror = lax.ppermute(following, "gy", [(i, i ^ HALF) for i in range(sectors)])
     slots = exchange(slots)
-    partial, spreading, weights = pl.pallas_call(
-        target_kernel,
-        in_specs=[vmem] * 2 + [hbm] * 2,
-        out_specs=(vmem,) * 3,
-        out_shape=(
-            partial_shape, spread_shape, jax.ShapeDtypeStruct((2, width, width), bf16)
-        ),
-        scratch_shapes=[pltpu.SemaphoreType.DMA((2,))],
-        compiler_params=params,
-    )(first, order, pinned(process_update), pinned(decode_message))
     send = pl.pallas_call(
         request_kernel,
         out_shape=jax.ShapeDtypeStruct((edges, width), bf16),
@@ -422,7 +400,7 @@
         out_shape=(table_shape, table_shape),
         scratch_shapes=[messages],
         compiler_params=params,
-    )(picked, partial, spreading, first, weights)
+    )(picked, order, first, process_update, decode_message)
 
     other = lax.ppermute(table, "gy", far_sectors)
     mate = lax.ppermute(table, "gy", near_sectors)

time: 125 us -> 122 us (0.976)
  blocking collectives: 26.3 us -> 57.4 us
  waiting for transfers between devices: 34.1 us -> 8.73 us
  local copies, waits for them, and re-layouts: 4.03 us -> 0.03 us
  starting transfers between devices: 44.4 us -> 41.3 us
  Pallas kernels: 14.9 us -> 12.6 us
    all_to_all x1 -> x2, blocking collectives: 26.3 us -> 57.4 us  [exchange(): lax.all_to_all(array, 'gy', 0, 0, axis_index_groups=group, tiled=True)]
    all_to_all x1 -> x0, waiting for transfers between devices: 25 us -> none  [exchange(): lax.all_to_all(array, 'gy', 0, 0, axis_index_groups=group, tiled=True)]
    unnamed x14 -> x10, local copies, waits for them, and re-layouts: 4.03 us -> 0.03 us
    all_to_all x1 -> x0, starting transfers between devices: 3.93 us -> none  [exchange(): lax.all_to_all(array, 'gy', 0, 0, axis_index_groups=group, tiled=True)]
  transfers between devices with their start and end apart: 8 -> 7, of which waited for: 5 -> 4; matrix products, arithmetic and copies ran while one was open for 0% -> 0% of each run, Pallas kernels for 5% -> 3%
where the time goes in v6:
time: 122 us; the launch traced here: 121 us
  blocking collectives  57.4 us (47%)
  starting transfers between devices  41.3 us (34%)
  Pallas kernels  12.6 us (10%)
  waiting for transfers between devices  8.73 us (7%)
    all_to_all x2, blocking collectives, exchange(): lax.all_to_all(array, 'gy', 0, 0, axis_index_groups=group, tiled=True)  57.4 us
    ppermute x1, starting transfers between devices, on_device(): far = lax.ppermute(far, 'gx', far_bands)  15.6 us
    ppermute x1, starting transfers between devices, on_device(): other = lax.ppermute(other, 'gy', far_sectors)  9.08 us
    ppermute x1, starting transfers between devices, on_device(): other = lax.ppermute(table, 'gy', far_sectors)  8.8 us
    ppermute x1, waiting for transfers between devices, on_device(): other = lax.ppermute(table, 'gy', far_sectors)  4.1 us
    ppermute x1, waiting for transfers between devices, on_device(): near = lax.ppermute(near, 'gx', near_bands)  3.82 us
    pallas_call x1, Pallas kernels, on_device(): pl.pallas_call(gather_kernel, in_specs=[vmem, hbm, vmem] + [hbm] * 8, out...  2.53 us
  transfers between devices with their start and end apart: 7, of which 4 were waited for; matrix products, arithmetic and copies ran while one was open for 0% of the time, Pallas kernels for 3%

profile of v6, /device:TPU:6, one launch (start us, length us, event | category | flops | bytes accessed | tf_op | source)
XLA Modules:
  0.0 121.0 jit_solution(5275446727799878654)
XLA Ops:
  0.6 0.9 shard_map.149
  1.5 15.6 %collective-permute-start = (bf16[64,512]{1,0:T(8,128)(2,1)S(1)}, bf16[64,512]{1,0:T(8,128)(2,1)S(1)}, u32[]{:S(2)}, u32[]{:S(2)}) collective-permute-start(bf16[64,512]{1,0:T(8,128)(2,1)S(1)} %get-tuple-element.23), channel_id=1, source_target_pairs={{64,128},{128,64},{192,256},{256,192},{320,384},{384,320},{65,129}... | collective-permute-start | bytes 196616 | tf_op jit(solution)/shard_map/ppermute | solution.py:328
  17.2 1.9 %collective-permute-start.1 = (bf16[64,512]{1,0:T(8,128)(2,1)S(1)}, bf16[64,512]{1,0:T(8,128)(2,1)S(1)}, u32[]{:S(2)}, u32[]{:S(2)}) collective-permute-start(bf16[64,512]{1,0:T(8,128)(2,1)S(1)} %get-tuple-element.24), channel_id=1, source_target_pairs={{0,64},{64,0},{128,192},{192,128},{256,320},{320,256},{384,448},{4... | collective-permute-start | bytes 196616 | tf_op jit(solution)/shard_map/ppermute | solution.py:329
  19.1 0.4 collective-permute-done.far
  19.5 3.8 %collective-permute-done.1.near = bf16[64,512]{1,0:T(8,128)(2,1)S(1)} collective-permute-done((bf16[64,512]{1,0:T(8,128)(2,1)S(1)}, bf16[64,512]{1,0:T(8,128)(2,1)S(1)}, u32[]{:S(2)}, u32[]{:S(2)}) %collective-permute-start.1) | collective-permute-done | bytes 65568 | tf_op jit(solution)/shard_map/ppermute | solution.py:329
  23.3 0.8 shard_map.151
  24.1 9.1 %collective-permute-start.2 = (bf16[4,8,512]{2,1,0:T(8,128)(2,1)S(1)}, bf16[4,8,512]{2,1,0:T(8,128)(2,1)S(1)}, u32[]{:S(2)}, u32[]{:S(2)}) collective-permute-start(bf16[4,8,512]{2,1,0:T(8,128)(2,1)S(1)} %get-tuple-element.26), channel_id=1, source_target_pairs={{0,63},{1,2},{2,1},{3,4},{4,3},{5,6},{6,5},{7,8},{8,7},{9,10},{10,... | collective-permute-start | bytes 98312 | tf_op jit(solution)/shard_map/ppermute | solution.py:342
  33.2 1.9 %collective-permute-start.3 = (bf16[4,8,512]{2,1,0:T(8,128)(2,1)S(1)}, bf16[4,8,512]{2,1,0:T(8,128)(2,1)S(1)}, u32[]{:S(2)}, u32[]{:S(2)}) collective-permute-start(bf16[4,8,512]{2,1,0:T(8,128)(2,1)S(1)} %get-tuple-element.27), channel_id=1, source_target_pairs={{0,1},{1,0},{2,3},{3,2},{4,5},{5,4},{6,7},{7,6},{8,9},{9,8},{10,11... | collective-permute-start | bytes 98312 | tf_op jit(solution)/shard_map/ppermute | solution.py:343
  35.1 2.5 %shard_map.150 = (f32[1024,512]{1,0:T(8,128)S(1)}, bf16[256,1024]{1,0:T(8,128)(2,1)S(1)}, bf16[256,512]{1,0:T(8,128)(2,1)S(1)}, bf16[3,512,512]{2,1,0:T(8,128)(2...) custom-call(bf16[64,512]{1,0:T(8,128)(2,1)S(1)} %collective-permute-done.far, ...), custom_call_target="tpu_custom_call" | custom-call | tf_op jit(solution)/shard_map/pallas_call | solution.py:352
  37.7 0.4 collective-permute-done.2.other
  38.1 1.8 %shard_map.152 = (bf16[256,512]{1,0:T(8,128)(2,1)S(1)}, bf16[256,512]{1,0:T(8,128)(2,1)S(1)}) custom-call(f32[1024,512]{1,0:T(8,128)S(1)} %get-tuple-element.25.partial, bf16[4,8,512]{2,1,0:T(8,128)(2,1)S(1)} %collective-permute-done.2.other, bf16[4,8,512]{2,1,0:T(8,128)(2,1)S(1)} %collective-permute-done.3.mate, ...), custom_call_target="tpu_custom_call" | custom-call | tf_op jit(solution)/shard_map/pallas_call | solution.py:382
  39.9 0.0 copy-start.2
  39.9 2.1 %collective-permute-start.4 = (bf16[256,512]{1,0:T(8,128)(2,1)S(1)}, bf16[256,512]{1,0:T(8,128)(2,1)S(1)}, u32[]{:S(2)}, u32[]{:S(2)}) collective-permute-start(bf16[256,512]{1,0:T(8,128)(2,1)S(1)} %get-tuple-element.34.table), channel_id=1, source_target_pairs={{0,8},{1,9},{2,10},{3,11},{4,12},{5,13},{6,14},{7,15},{8,0},{9,1},... | collective-permute-start | bytes 786440 | tf_op jit(solution)/shard_map/ppermute | solution.py:390
  41.9 26.3 %all_to_all.16 = s32[32,1,128]{2,1,0:T(1,128)S(1)} all-to-all(s32[32,1,128]{2,1,0:T(1,128)S(1)} %bitcast.21), channel_id=1, replica_groups={{0,1,2,3,4,5,6,7,16,17,18,19,20,21,22,23,32,33,34,35,36,37,38,39,48,49,..., dimensions={0} | all-to-all | bytes 32768 | tf_op jit(solution)/shard_map/all_to_all | solution.py:317
  68.3 0.8 shard_map.153
  69.1 0.0 copy-start.4
  69.1 0.0 copy-start
  69.2 31.1 %all_to_all.17 = bf16[32,32,512]{2,1,0:T(8,128)(2,1)S(1)} all-to-all(bf16[32,32,512]{2,1,0:T(8,128)(2,1)S(1)} %bitcast.17), channel_id=1, replica_groups={{0,1,2,3,4,5,6,7,16,17,18,19,20,21,22,23,32,33,34,35,36,37,38,39,48,49,..., dimensions={0} | all-to-all | bytes 2097152 | tf_op jit(solution)/shard_map/all_to_all | solution.py:317
  100.3 2.2 %shard_map.154 = (bf16[256,512]{1,0:T(8,128)(2,1)}, bf16[256,512]{1,0:T(8,128)(2,1)S(1)}) custom-call(bf16[1024,512]{1,0:T(8,128)(2,1)S(1)} %bitcast.16, s32[8,128]{1,0:T(8,128)S(1)} %get-tuple-element.36.target, bf16[256,512]{1,0:T(8,128)(2,1)S(1)} %get-tuple-element.37.first, bf16[512,512]{1,0:T(8,128)(2,1)S(1)} %copy-done.1, bf16[512,512]{1,0:T(8,128)(2,1)S(1)} %copy-done.2), custom_call_target="tpu_custom_call" | custom-call | tf_op jit(solution)/shard_map/pallas_call | solution.py:398
  102.5 8.8 %collective-permute-start.5 = (bf16[256,512]{1,0:T(8,128)(2,1)S(1)}, bf16[256,512]{1,0:T(8,128)(2,1)S(1)}, u32[]{:S(2)}, u32[]{:S(2)}) collective-permute-start(bf16[256,512]{1,0:T(8,128)(2,1)S(1)} %get-tuple-element.38.own), channel_id=1, source_target_pairs={{0,63},{1,2},{2,1},{3,4},{4,3},{5,6},{6,5},{7,8},{8,7},{9,10},{10,... | collective-permute-start | bytes 786440 | tf_op jit(solution)/shard_map/ppermute | solution.py:405
  111.3 1.9 %collective-permute-start.6 = (bf16[256,512]{1,0:T(8,128)(2,1)S(1)}, bf16[256,512]{1,0:T(8,128)(2,1)S(1)}, u32[]{:S(2)}, u32[]{:S(2)}) collective-permute-start(bf16[256,512]{1,0:T(8,128)(2,1)S(1)} %get-tuple-element.38.own), channel_id=1, source_target_pairs={{0,1},{1,0},{2,3},{3,2},{4,5},{5,4},{6,7},{7,6},{8,9},{9,8},{10,11... | collective-permute-start | bytes 786440 | tf_op jit(solution)/shard_map/ppermute | solution.py:406
  113.3 1.6 %shard_map.155 = (f32[1024,512]{1,0:T(8,128)S(1)}, bf16[1024,512]{1,0:T(8,128)(2,1)S(1)}, bf16[128,1024]{1,0:T(8,128)(2,1)S(1)}, bf16[512,512]{1,0:T(8,128)(2,1)S(1)}) custom-call(bf16[256,512]{1,0:T(8,128)(2,1)S(1)} %get-tuple-element.38.own, bf16[128,512]{1,0:T(8,128)(2,1)S(1)} %bitcast.18, s32[8,128]{1,0:T(8,128)S(1)} %fusion.1.source, ...), custom_call_target="tpu_custom_call" | custom-call | tf_op jit(solution)/shard_map/pallas_call | solution.py:412
  114.9 4.1 %collective-permute-done.5.other = bf16[256,512]{1,0:T(8,128)(2,1)S(1)} collective-permute-done((bf16[256,512]{1,0:T(8,128)(2,1)S(1)}, bf16[256,512]{1,0:T(8,128)(2,1)S(1)}, u32[]{:S(2)}, u32[]{:S(2)}) %collective-permute-start.5) | collective-permute-done | bytes 262176 | tf_op jit(solution)/shard_map/ppermute | solution.py:405
  119.0 2.0 %shard_map.156 = bf16[128,512]{1,0:T(8,128)(2,1)} custom-call(f32[1024,512]{1,0:T(8,128)S(1)} %get-tuple-element.39.partial, bf16[256,512]{1,0:T(8,128)(2,1)S(1)} %collective-permute-done.5.other, bf16[256,512]{1,0:T(8,128)(2,1)S(1)} %collective-permute-done.6.mate, bf16[1024,512]{1,0:T(8,128)(2,1)S(1)} %get-tuple-element.40.picks, ...), custom_call_target="tpu_custom_call" | custom-call | tf_op jit(solution)/shard_map/pallas_call | solution.py:425
  (11 shorter events, 0.0 us)
Async XLA Ops:
  1.5 18.0 %collective-permute-start = (bf16[64,512]{1,0:T(8,128)(2,1)S(1)}, bf16[64,512]{1,0:T(8,128)(2,1)S(1)}, u32[]{:S(2)}, u32[]{:S(2)}) collective-permute-start(bf16[64,512]{1,0:T(8,128)(2,1)S(1)} %get-tuple-element.23), channel_id=1, source_target_pairs={{64,128},{128,64},{192,256},{256,192},{320,384},{384,320},{65,129}... | collective-permute-start | bytes 196616 | tf_op jit(solution)/shard_map/ppermute | solution.py:328
  17.2 6.2 %collective-permute-start.1 = (bf16[64,512]{1,0:T(8,128)(2,1)S(1)}, bf16[64,512]{1,0:T(8,128)(2,1)S(1)}, u32[]{:S(2)}, u32[]{:S(2)}) collective-permute-start(bf16[64,512]{1,0:T(8,128)(2,1)S(1)} %get-tuple-element.24), channel_id=1, source_target_pairs={{0,64},{64,0},{128,192},{192,128},{256,320},{320,256},{384,448},{4... | collective-permute-start | bytes 196616 | tf_op jit(solution)/shard_map/ppermute | solution.py:329
  24.1 13.9 %collective-permute-start.2 = (bf16[4,8,512]{2,1,0:T(8,128)(2,1)S(1)}, bf16[4,8,512]{2,1,0:T(8,128)(2,1)S(1)}, u32[]{:S(2)}, u32[]{:S(2)}) collective-permute-start(bf16[4,8,512]{2,1,0:T(8,128)(2,1)S(1)} %get-tuple-element.26), channel_id=1, source_target_pairs={{0,63},{1,2},{2,1},{3,4},{4,3},{5,6},{6,5},{7,8},{8,7},{9,10},{10,... | collective-permute-start | bytes 98312 | tf_op jit(solution)/shard_map/ppermute | solution.py:342
  33.2 4.9 %collective-permute-start.3 = (bf16[4,8,512]{2,1,0:T(8,128)(2,1)S(1)}, bf16[4,8,512]{2,1,0:T(8,128)(2,1)S(1)}, u32[]{:S(2)}, u32[]{:S(2)}) collective-permute-start(bf16[4,8,512]{2,1,0:T(8,128)(2,1)S(1)} %get-tuple-element.27), channel_id=1, source_target_pairs={{0,1},{1,0},{2,3},{3,2},{4,5},{5,4},{6,7},{7,6},{8,9},{9,8},{10,11... | collective-permute-start | bytes 98312 | tf_op jit(solution)/shard_map/ppermute | solution.py:343
  39.8 60.4 %copy-start.1 = (bf16[512,512]{1,0:T(8,128)(2,1)S(1)}, bf16[512,512]{1,0:T(8,128)(2,1)}, u32[]{:S(2)}) copy-start(bf16[512,512]{1,0:T(8,128)(2,1)} %w_update.4) | copy-start | bytes 1572868
  39.9 60.4 %copy-start.2 = (bf16[512,512]{1,0:T(8,128)(2,1)S(1)}, bf16[512,512]{1,0:T(8,128)(2,1)}, u32[]{:S(2)}) copy-start(bf16[512,512]{1,0:T(8,128)(2,1)} %w_next.3) | copy-start | bytes 1572868
  39.9 28.4 %collective-permute-start.4 = (bf16[256,512]{1,0:T(8,128)(2,1)S(1)}, bf16[256,512]{1,0:T(8,128)(2,1)S(1)}, u32[]{:S(2)}, u32[]{:S(2)}) collective-permute-start(bf16[256,512]{1,0:T(8,128)(2,1)S(1)} %get-tuple-element.34.table), channel_id=1, source_target_pairs={{0,8},{1,9},{2,10},{3,11},{4,12},{5,13},{6,14},{7,15},{8,0},{9,1},... | collective-permute-start | bytes 786440 | tf_op jit(solution)/shard_map/ppermute | solution.py:390
  69.1 44.1 %copy-start.4 = (s32[1,1,1024]{2,1,0:T(1,128)S(1)}, s32[1,1,1024]{2,1,0:T(1,128)}, u32[]{:S(2)}) copy-start(s32[1,1,1024]{2,1,0:T(1,128)} %param.26) | copy-start | bytes 12292
  69.1 44.1 %copy-start = (bf16[2,64,512]{2,1,0:T(8,128)(2,1)S(1)}, bf16[2,64,512]{2,1,0:T(8,128)(2,1)}, u32[]{:S(2)}) copy-start(bf16[2,64,512]{2,1,0:T(8,128)(2,1)} %grid.5) | copy-start | bytes 393220
  69.1 44.1 %copy-start.3 = (s32[1,1,1024]{2,1,0:T(1,128)S(1)}, s32[1,1,1024]{2,1,0:T(1,128)}, u32[]{:S(2)}) copy-start(s32[1,1,1024]{2,1,0:T(1,128)} %param.27) | copy-start | bytes 12292
  102.5 16.5 %collective-permute-start.5 = (bf16[256,512]{1,0:T(8,128)(2,1)S(1)}, bf16[256,512]{1,0:T(8,128)(2,1)S(1)}, u32[]{:S(2)}, u32[]{:S(2)}) collective-permute-start(bf16[256,512]{1,0:T(8,128)(2,1)S(1)} %get-tuple-element.38.own), channel_id=1, source_target_pairs={{0,63},{1,2},{2,1},{3,4},{4,3},{5,6},{6,5},{7,8},{8,7},{9,10},{10,... | collective-permute-start | bytes 786440 | tf_op jit(solution)/shard_map/ppermute | solution.py:405
  111.3 7.7 %collective-permute-start.6 = (bf16[256,512]{1,0:T(8,128)(2,1)S(1)}, bf16[256,512]{1,0:T(8,128)(2,1)S(1)}, u32[]{:S(2)}, u32[]{:S(2)}) collective-permute-start(bf16[256,512]{1,0:T(8,128)(2,1)S(1)} %get-tuple-element.38.own), channel_id=1, source_target_pairs={{0,1},{1,0},{2,3},{3,2},{4,5},{5,4},{6,7},{7,6},{8,9},{9,8},{10,11... | collective-permute-start | bytes 786440 | tf_op jit(solution)/shard_map/ppermute | solution.py:406

commit v7 on v6

--- a/solution.py
+++ b/solution.py
@@ -13,6 +13,8 @@
 CAP = 16
 GROUPS = LANES // CAP
 HALF = 8
+CORES = 2
+PLANES = HALF // CORES
 
 
 def column(index, rows):
@@ -93,6 +95,24 @@
         moved = roll(rows[pl.ds(g, count, stride=fold), :], g * each)
         kept = jnp.where((lane >= g * each) & (lane < (g + 1) * each), moved, kept)
     return kept
+
+
+def by_plane(rows, out):
+    count = rows.shape[0] // HALF
+    each = 2 * CAP
+    lane = lax.broadcasted_iota(jnp.int32, (count, LANES), 1)
+    for core in range(CORES):
+        kept = jnp.zeros_like(lane)
+        for p in range(PLANES):
+            moved = roll(rows[pl.ds(p * CORES + core, count, stride=HALF), :], p * each)
+            kept = jnp.where((lane >= p * each) & (lane < (p + 1) * each), moved, kept)
+        out[pl.ds(core, count, stride=CORES), :] = kept
+
+
+def planes_kernel(slots, slots_out):
+    count = slots.shape[0]
+    for p in range(PLANES):
+        slots_out[p * count : (p + 1) * count, :] = roll(slots[...], -p * 2 * CAP)
 
 
 def edges_kernel(grid, far_out, near_out, sems):
@@ -187,7 +207,8 @@
         sides_out[rows, :] = pick(column(edge, rows), sides_out.shape[1])
     copies[5].wait()
     copies[6].wait()
-    apart(indices.at[2], slots_out)
+    apart(indices.at[2], rows_held)
+    by_plane(rows_held, slots_out)
     apart(indices.at[3], rows_held)
     order_out[...] = together(rows_held)
     copies[7].wait()
@@ -214,9 +235,15 @@
     next_out[...] = dot(first, weights[2]).astype(jnp.bfloat16)
 
 
-def request_kernel(table, mirror, slots, send_out):
+def request_kernel(table, mirror, slots, send_out, held):
     nodes = table.shape[0]
-    asked = together(slots)
+    plane = slots.shape[0] // PLANES
+    count = plane // CORES
+    for p in range(PLANES):
+        for core in range(CORES):
+            part = slots[pl.ds(p * plane + core, count, stride=CORES), :]
+            held[pl.ds(p * CORES + core, count, stride=HALF), :] = part
+    asked = together(held)
     lane = lax.broadcasted_iota(jnp.int32, asked.shape, 1)
     asked = asked + jnp.where((lane & (2 * CAP - 1)) >= CAP, nodes, 0)
     for c in range(0, send_out.shape[0], CHUNK):
@@ -227,7 +254,7 @@
 
 
 def process_kernel(
-    picked, target, first, w_update, w_next, second_out, table_out, messages
+    picked, target, first, w_update, w_next, second_out, table_out, messages, held, sem
 ):
     nodes = first.shape[0]
     tgt = target[...]
@@ -236,8 +263,11 @@
         acc = dot(pick(column(tgt, rows), nodes), first[...])
         messages[rows, :] = message(acc + picked[rows, :].astype(jnp.float32))
     second = refresh(first[...], dot(spread(tgt, nodes), messages[...]), w_update[...])
-    second_out[...] = second
+    held[...] = second
+    copy = pltpu.make_async_copy(held, second_out, sem)
+    copy.start()
     table_out[...] = dot(second, w_next[...]).astype(jnp.bfloat16)
+    copy.wait()
 
 
 def reach_kernel(
@@ -313,8 +343,13 @@
 
     group = [[i for i in range(sectors) if i // HALF % 2 == h] for h in range(2)]
 
-    def exchange(array):
-        return lax.all_to_all(array, "gy", 0, 0, axis_index_groups=group, tiled=True)
+    every = range(sectors)
+    plane_groups = [[i for i in every if i // CORES % HALF == p] for p in range(HALF)]
+    columns = [i for i in every if i // CORES % PLANES == 0]
+    column_groups = [[i + p * CORES for p in range(PLANES)] for i in columns]
+
+    def exchange(array, groups):
+        return lax.all_to_all(array, "gy", 0, 0, axis_index_groups=groups, tiled=True)
 
     band_edge = jax.ShapeDtypeStruct((lon_cols, width), bf16)
     far, near = pl.pallas_call(
@@ -348,7 +383,8 @@
     table_shape = jax.ShapeDtypeStruct((nodes, width), bf16)
     partial_shape = jax.ShapeDtypeStruct((edges, width), jnp.float32)
     spread_shape = jax.ShapeDtypeStruct((nodes, edges), bf16)
-    slots_shape = jax.ShapeDtypeStruct((sectors // 2, LANES), jnp.int32)
+    rows_shape = jax.ShapeDtypeStruct((sectors // 2, LANES), jnp.int32)
+    plane_shape = jax.ShapeDtypeStruct((sectors // 2 // PLANES, LANES), jnp.int32)
     partial, spreading, mesh_held, weights, sides, slots, order = pl.pallas_call(
         gather_kernel,
         in_specs=[vmem, hbm, vmem] + [hbm] * 8,
@@ -359,13 +395,13 @@
             table_shape,
             jax.ShapeDtypeStruct((3, width, width), bf16),
             jax.ShapeDtypeStruct((edges, depth), bf16),
-            slots_shape,
+            plane_shape,
             index,
         ),
         scratch_shapes=[
             pltpu.VMEM((lat_rows, lon_cols, width), bf16),
             pltpu.VMEM((4, edges // LANES, LANES), jnp.int32),
-            pltpu.VMEM(slots_shape.shape, jnp.int32),
+            pltpu.VMEM(rows_shape.shape, jnp.int32),
             pltpu.VMEM((tall_cells, width), bf16),
             pltpu.SemaphoreType.DMA((9,)),
         ],
@@ -388,17 +424,23 @@
 
     following, slots = lax.optimization_barrier((following, slots))
     mirror = lax.ppermute(following, "gy", [(i, i ^ HALF) for i in range(sectors)])
-    slots = exchange(slots)
+    slots = exchange(slots, plane_groups)
+    slots = pl.pallas_call(planes_kernel, out_shape=rows_shape, compiler_params=params)(slots)
+    slots = exchange(slots, column_groups)
     send = pl.pallas_call(
         request_kernel,
         out_shape=jax.ShapeDtypeStruct((edges, width), bf16),
+        scratch_shapes=[pltpu.VMEM(rows_shape.shape, jnp.int32)],
         compiler_params=params,
     )(following, mirror, slots)
-    picked = exchange(send.reshape(sectors // 2, -1, width)).reshape(edges, width)
+    picked = exchange(send.reshape(sectors // 2, -1, width), group).reshape(edges, width)
     second, table = pl.pallas_call(
         process_kernel,
+        out_specs=(hbm, vmem),
         out_shape=(table_shape, table_shape),
-        scratch_shapes=[messages],
+        scratch_shapes=[
+            messages, pltpu.VMEM((nodes, width), bf16), pltpu.SemaphoreType.DMA(())
+        ],
         compiler_params=params,
     )(picked, order, first, process_update, decode_message)
 

time: 122 us -> 121 us (level)
    all_to_all x2 -> x3, blocking collectives: 57.4 us -> 56.5 us  [exchange(): lax.all_to_all(array, 'gy', 0, 0, axis_index_groups=groups, tiled=True)]
  transfers between devices with their start and end apart: 7 -> 7, of which waited for: 4 -> 4; matrix products, arithmetic and copies ran while one was open for 0% -> 0% of each run, Pallas kernels for 3% -> 4%
where the time goes in v7:
time: 121 us; the launch traced here: 120 us
  blocking collectives  56.5 us (47%)
  starting transfers between devices  41.6 us (34%)
  Pallas kernels  12.7 us (10%)
  waiting for transfers between devices  8.62 us (7%)
    all_to_all x3, blocking collectives, exchange(): lax.all_to_all(array, 'gy', 0, 0, axis_index_groups=groups, tiled=True)  56.5 us
    ppermute x1, starting transfers between devices, on_device(): far = lax.ppermute(far, 'gx', far_bands)  15.6 us
    ppermute x1, starting transfers between devices, on_device(): other = lax.ppermute(other, 'gy', far_sectors)  9.08 us
    ppermute x1, starting transfers between devices, on_device(): other = lax.ppermute(table, 'gy', far_sectors)  9.08 us
    ppermute x1, waiting for transfers between devices, on_device(): other = lax.ppermute(table, 'gy', far_sectors)  4 us
    ppermute x1, waiting for transfers between devices, on_device(): near = lax.ppermute(near, 'gx', near_bands)  3.82 us
    pallas_call x1, Pallas kernels, on_device(): pl.pallas_call(gather_kernel, in_specs=[vmem, hbm, vmem] + [hbm] * 8, out...  2.55 us
  transfers between devices with their start and end apart: 7, of which 4 were waited for; matrix products, arithmetic and copies ran while one was open for 0% of the time, Pallas kernels for 4%

profile of v7, /device:TPU:6, one launch (start us, length us, event | category | flops | bytes accessed | tf_op | source)
XLA Modules:
  0.0 120.3 jit_solution(2839469821222098649)
XLA Ops:
  0.6 0.9 shard_map.149
  1.5 15.6 %collective-permute-start = (bf16[64,512]{1,0:T(8,128)(2,1)S(1)}, bf16[64,512]{1,0:T(8,128)(2,1)S(1)}, u32[]{:S(2)}, u32[]{:S(2)}) collective-permute-start(bf16[64,512]{1,0:T(8,128)(2,1)S(1)} %get-tuple-element.23), channel_id=1, source_target_pairs={{64,128},{128,64},{192,256},{256,192},{320,384},{384,320},{65,129}... | collective-permute-start | bytes 196616 | tf_op jit(solution)/shard_map/ppermute | solution.py:363
  17.2 1.9 %collective-permute-start.1 = (bf16[64,512]{1,0:T(8,128)(2,1)S(1)}, bf16[64,512]{1,0:T(8,128)(2,1)S(1)}, u32[]{:S(2)}, u32[]{:S(2)}) collective-permute-start(bf16[64,512]{1,0:T(8,128)(2,1)S(1)} %get-tuple-element.24), channel_id=1, source_target_pairs={{0,64},{64,0},{128,192},{192,128},{256,320},{320,256},{384,448},{4... | collective-permute-start | bytes 196616 | tf_op jit(solution)/shard_map/ppermute | solution.py:364
  19.1 0.4 collective-permute-done.far
  19.5 3.8 %collective-permute-done.1.near = bf16[64,512]{1,0:T(8,128)(2,1)S(1)} collective-permute-done((bf16[64,512]{1,0:T(8,128)(2,1)S(1)}, bf16[64,512]{1,0:T(8,128)(2,1)S(1)}, u32[]{:S(2)}, u32[]{:S(2)}) %collective-permute-start.1) | collective-permute-done | bytes 65568 | tf_op jit(solution)/shard_map/ppermute | solution.py:364
  23.3 0.8 shard_map.151
  24.1 9.1 %collective-permute-start.2 = (bf16[4,8,512]{2,1,0:T(8,128)(2,1)S(1)}, bf16[4,8,512]{2,1,0:T(8,128)(2,1)S(1)}, u32[]{:S(2)}, u32[]{:S(2)}) collective-permute-start(bf16[4,8,512]{2,1,0:T(8,128)(2,1)S(1)} %get-tuple-element.26), channel_id=1, source_target_pairs={{0,63},{1,2},{2,1},{3,4},{4,3},{5,6},{6,5},{7,8},{8,7},{9,10},{10,... | collective-permute-start | bytes 98312 | tf_op jit(solution)/shard_map/ppermute | solution.py:377
  33.2 1.9 %collective-permute-start.3 = (bf16[4,8,512]{2,1,0:T(8,128)(2,1)S(1)}, bf16[4,8,512]{2,1,0:T(8,128)(2,1)S(1)}, u32[]{:S(2)}, u32[]{:S(2)}) collective-permute-start(bf16[4,8,512]{2,1,0:T(8,128)(2,1)S(1)} %get-tuple-element.27), channel_id=1, source_target_pairs={{0,1},{1,0},{2,3},{3,2},{4,5},{5,4},{6,7},{7,6},{8,9},{9,8},{10,11... | collective-permute-start | bytes 98312 | tf_op jit(solution)/shard_map/ppermute | solution.py:378
  35.1 2.5 %shard_map.150 = (f32[1024,512]{1,0:T(8,128)S(1)}, bf16[256,1024]{1,0:T(8,128)(2,1)S(1)}, bf16[256,512]{1,0:T(8,128)(2,1)S(1)}, bf16[3,512,512]{2,1,0:T(8,128)(2...) custom-call(bf16[64,512]{1,0:T(8,128)(2,1)S(1)} %collective-permute-done.far, ...), custom_call_target="tpu_custom_call" | custom-call | tf_op jit(solution)/shard_map/pallas_call | solution.py:388
  37.7 0.4 collective-permute-done.2.other
  38.1 1.8 %shard_map.152 = (bf16[256,512]{1,0:T(8,128)(2,1)S(1)}, bf16[256,512]{1,0:T(8,128)(2,1)S(1)}) custom-call(f32[1024,512]{1,0:T(8,128)S(1)} %get-tuple-element.25.partial, bf16[4,8,512]{2,1,0:T(8,128)(2,1)S(1)} %collective-permute-done.2.other, bf16[4,8,512]{2,1,0:T(8,128)(2,1)S(1)} %collective-permute-done.3.mate, ...), custom_call_target="tpu_custom_call" | custom-call | tf_op jit(solution)/shard_map/pallas_call | solution.py:418
  39.9 0.0 copy-start.1
  39.9 2.1 %collective-permute-start.4 = (bf16[256,512]{1,0:T(8,128)(2,1)S(1)}, bf16[256,512]{1,0:T(8,128)(2,1)S(1)}, u32[]{:S(2)}, u32[]{:S(2)}) collective-permute-start(bf16[256,512]{1,0:T(8,128)(2,1)S(1)} %get-tuple-element.34.table), channel_id=1, source_target_pairs={{0,8},{1,9},{2,10},{3,11},{4,12},{5,13},{6,14},{7,15},{8,0},{9,1},... | collective-permute-start | bytes 786440 | tf_op jit(solution)/shard_map/ppermute | solution.py:426
  41.9 8.3 %all_to_all.27 = s32[8,1,128]{2,1,0:T(1,128)S(1)} all-to-all(s32[8,1,128]{2,1,0:T(1,128)S(1)} %bitcast.26), channel_id=1, replica_groups={{0,1,16,17,32,33,48,49},{2,3,18,19,34,35,50,51},{4,5,20,21,36,37,52,53}..., dimensions={0} | all-to-all | bytes 8192 | tf_op jit(solution)/shard_map/all_to_all | solution.py:352
  50.3 0.1 shard_map.153
  50.3 15.4 %all_to_all.28 = s32[4,8,128]{2,1,0:T(8,128)S(1)} all-to-all(s32[4,8,128]{2,1,0:T(8,128)S(1)} %bitcast.23), channel_id=1, replica_groups={{0,2,4,6},{1,3,5,7},{8,10,12,14},{9,11,13,15},{16,18,20,22},{17,19,21,2..., dimensions={0} | all-to-all | bytes 32768 | tf_op jit(solution)/shard_map/all_to_all | solution.py:352
  65.7 0.8 shard_map.154
  66.6 32.7 %all_to_all.29 = bf16[32,32,512]{2,1,0:T(8,128)(2,1)S(1)} all-to-all(bf16[32,32,512]{2,1,0:T(8,128)(2,1)S(1)} %bitcast.19), channel_id=1, replica_groups={{0,1,2,3,4,5,6,7,16,17,18,19,20,21,22,23,32,33,34,35,36,37,38,39,48,49,..., dimensions={0} | all-to-all | bytes 2097152 | tf_op jit(solution)/shard_map/all_to_all | solution.py:352
  99.4 2.2 %shard_map.155 = (bf16[256,512]{1,0:T(8,128)(2,1)}, bf16[256,512]{1,0:T(8,128)(2,1)S(1)}) custom-call(bf16[1024,512]{1,0:T(8,128)(2,1)S(1)} %bitcast.18, s32[8,128]{1,0:T(8,128)S(1)} %get-tuple-element.36.target, bf16[256,512]{1,0:T(8,128)(2,1)S(1)} %get-tuple-element.37.first, bf16[512,512]{1,0:T(8,128)(2,1)S(1)} %copy-done.1, bf16[512,512]{1,0:T(8,128)(2,1)S(1)} %copy-done.2), custom_call_target="tpu_custom_call" | custom-call | tf_op jit(solution)/shard_map/pallas_call | solution.py:437
  101.6 9.1 %collective-permute-start.5 = (bf16[256,512]{1,0:T(8,128)(2,1)S(1)}, bf16[256,512]{1,0:T(8,128)(2,1)S(1)}, u32[]{:S(2)}, u32[]{:S(2)}) collective-permute-start(bf16[256,512]{1,0:T(8,128)(2,1)S(1)} %get-tuple-element.38.own), channel_id=1, source_target_pairs={{0,63},{1,2},{2,1},{3,4},{4,3},{5,6},{6,5},{7,8},{8,7},{9,10},{10,... | collective-permute-start | bytes 786440 | tf_op jit(solution)/shard_map/ppermute | solution.py:447
  110.7 1.9 %collective-permute-start.6 = (bf16[256,512]{1,0:T(8,128)(2,1)S(1)}, bf16[256,512]{1,0:T(8,128)(2,1)S(1)}, u32[]{:S(2)}, u32[]{:S(2)}) collective-permute-start(bf16[256,512]{1,0:T(8,128)(2,1)S(1)} %get-tuple-element.38.own), channel_id=1, source_target_pairs={{0,1},{1,0},{2,3},{3,2},{4,5},{5,4},{6,7},{7,6},{8,9},{9,8},{10,11... | collective-permute-start | bytes 786440 | tf_op jit(solution)/shard_map/ppermute | solution.py:448
  112.7 1.6 %shard_map.156 = (f32[1024,512]{1,0:T(8,128)S(1)}, bf16[1024,512]{1,0:T(8,128)(2,1)S(1)}, bf16[128,1024]{1,0:T(8,128)(2,1)S(1)}, bf16[512,512]{1,0:T(8,128)(2,1)S(1)}) custom-call(bf16[256,512]{1,0:T(8,128)(2,1)S(1)} %get-tuple-element.38.own, bf16[128,512]{1,0:T(8,128)(2,1)S(1)} %bitcast.20, s32[8,128]{1,0:T(8,128)S(1)} %fusion.1.source, ...), custom_call_target="tpu_custom_call" | custom-call | tf_op jit(solution)/shard_map/pallas_call | solution.py:454
  114.3 4.0 %collective-permute-done.5.other = bf16[256,512]{1,0:T(8,128)(2,1)S(1)} collective-permute-done((bf16[256,512]{1,0:T(8,128)(2,1)S(1)}, bf16[256,512]{1,0:T(8,128)(2,1)S(1)}, u32[]{:S(2)}, u32[]{:S(2)}) %collective-permute-start.5) | collective-permute-done | bytes 262176 | tf_op jit(solution)/shard_map/ppermute | solution.py:447
  118.3 2.0 %shard_map.157 = bf16[128,512]{1,0:T(8,128)(2,1)} custom-call(f32[1024,512]{1,0:T(8,128)S(1)} %get-tuple-element.39.partial, bf16[256,512]{1,0:T(8,128)(2,1)S(1)} %collective-permute-done.5.other, bf16[256,512]{1,0:T(8,128)(2,1)S(1)} %collective-permute-done.6.mate, bf16[1024,512]{1,0:T(8,128)(2,1)S(1)} %get-tuple-element.40.picks, ...), custom_call_target="tpu_custom_call" | custom-call | tf_op jit(solution)/shard_map/pallas_call | solution.py:467
  (13 shorter events, 0.1 us)
Async XLA Ops:
  1.5 18.0 %collective-permute-start = (bf16[64,512]{1,0:T(8,128)(2,1)S(1)}, bf16[64,512]{1,0:T(8,128)(2,1)S(1)}, u32[]{:S(2)}, u32[]{:S(2)}) collective-permute-start(bf16[64,512]{1,0:T(8,128)(2,1)S(1)} %get-tuple-element.23), channel_id=1, source_target_pairs={{64,128},{128,64},{192,256},{256,192},{320,384},{384,320},{65,129}... | collective-permute-start | bytes 196616 | tf_op jit(solution)/shard_map/ppermute | solution.py:363
  17.2 6.2 %collective-permute-start.1 = (bf16[64,512]{1,0:T(8,128)(2,1)S(1)}, bf16[64,512]{1,0:T(8,128)(2,1)S(1)}, u32[]{:S(2)}, u32[]{:S(2)}) collective-permute-start(bf16[64,512]{1,0:T(8,128)(2,1)S(1)} %get-tuple-element.24), channel_id=1, source_target_pairs={{0,64},{64,0},{128,192},{192,128},{256,320},{320,256},{384,448},{4... | collective-permute-start | bytes 196616 | tf_op jit(solution)/shard_map/ppermute | solution.py:364
  24.1 13.9 %collective-permute-start.2 = (bf16[4,8,512]{2,1,0:T(8,128)(2,1)S(1)}, bf16[4,8,512]{2,1,0:T(8,128)(2,1)S(1)}, u32[]{:S(2)}, u32[]{:S(2)}) collective-permute-start(bf16[4,8,512]{2,1,0:T(8,128)(2,1)S(1)} %get-tuple-element.26), channel_id=1, source_target_pairs={{0,63},{1,2},{2,1},{3,4},{4,3},{5,6},{6,5},{7,8},{8,7},{9,10},{10,... | collective-permute-start | bytes 98312 | tf_op jit(solution)/shard_map/ppermute | solution.py:377
  33.2 4.9 %collective-permute-start.3 = (bf16[4,8,512]{2,1,0:T(8,128)(2,1)S(1)}, bf16[4,8,512]{2,1,0:T(8,128)(2,1)S(1)}, u32[]{:S(2)}, u32[]{:S(2)}) collective-permute-start(bf16[4,8,512]{2,1,0:T(8,128)(2,1)S(1)} %get-tuple-element.27), channel_id=1, source_target_pairs={{0,1},{1,0},{2,3},{3,2},{4,5},{5,4},{6,7},{7,6},{8,9},{9,8},{10,11... | collective-permute-start | bytes 98312 | tf_op jit(solution)/shard_map/ppermute | solution.py:378
  39.9 59.5 %copy-start.1 = (bf16[512,512]{1,0:T(8,128)(2,1)S(1)}, bf16[512,512]{1,0:T(8,128)(2,1)}, u32[]{:S(2)}) copy-start(bf16[512,512]{1,0:T(8,128)(2,1)} %w_update.4) | copy-start | bytes 1572868
  39.9 59.5 %copy-start.2 = (bf16[512,512]{1,0:T(8,128)(2,1)S(1)}, bf16[512,512]{1,0:T(8,128)(2,1)}, u32[]{:S(2)}) copy-start(bf16[512,512]{1,0:T(8,128)(2,1)} %w_next.3) | copy-start | bytes 1572868
  39.9 25.9 %collective-permute-start.4 = (bf16[256,512]{1,0:T(8,128)(2,1)S(1)}, bf16[256,512]{1,0:T(8,128)(2,1)S(1)}, u32[]{:S(2)}, u32[]{:S(2)}) collective-permute-start(bf16[256,512]{1,0:T(8,128)(2,1)S(1)} %get-tuple-element.34.table), channel_id=1, source_target_pairs={{0,8},{1,9},{2,10},{3,11},{4,12},{5,13},{6,14},{7,15},{8,0},{9,1},... | collective-permute-start | bytes 786440 | tf_op jit(solution)/shard_map/ppermute | solution.py:426
  66.6 46.1 %copy-start.4 = (s32[1,1,1024]{2,1,0:T(1,128)S(1)}, s32[1,1,1024]{2,1,0:T(1,128)}, u32[]{:S(2)}) copy-start(s32[1,1,1024]{2,1,0:T(1,128)} %param.26) | copy-start | bytes 12292
  66.6 46.1 %copy-start = (bf16[2,64,512]{2,1,0:T(8,128)(2,1)S(1)}, bf16[2,64,512]{2,1,0:T(8,128)(2,1)}, u32[]{:S(2)}) copy-start(bf16[2,64,512]{2,1,0:T(8,128)(2,1)} %grid.5) | copy-start | bytes 393220
  66.6 46.1 %copy-start.3 = (s32[1,1,1024]{2,1,0:T(1,128)S(1)}, s32[1,1,1024]{2,1,0:T(1,128)}, u32[]{:S(2)}) copy-start(s32[1,1,1024]{2,1,0:T(1,128)} %param.27) | copy-start | bytes 12292
  101.6 16.7 %collective-permute-start.5 = (bf16[256,512]{1,0:T(8,128)(2,1)S(1)}, bf16[256,512]{1,0:T(8,128)(2,1)S(1)}, u32[]{:S(2)}, u32[]{:S(2)}) collective-permute-start(bf16[256,512]{1,0:T(8,128)(2,1)S(1)} %get-tuple-element.38.own), channel_id=1, source_target_pairs={{0,63},{1,2},{2,1},{3,4},{4,3},{5,6},{6,5},{7,8},{8,7},{9,10},{10,... | collective-permute-start | bytes 786440 | tf_op jit(solution)/shard_map/ppermute | solution.py:447
  110.7 7.6 %collective-permute-start.6 = (bf16[256,512]{1,0:T(8,128)(2,1)S(1)}, bf16[256,512]{1,0:T(8,128)(2,1)S(1)}, u32[]{:S(2)}, u32[]{:S(2)}) collective-permute-start(bf16[256,512]{1,0:T(8,128)(2,1)S(1)} %get-tuple-element.38.own), channel_id=1, source_target_pairs={{0,1},{1,0},{2,3},{3,2},{4,5},{5,4},{6,7},{7,6},{8,9},{9,8},{10,11... | collective-permute-start | bytes 786440 | tf_op jit(solution)/shard_map/ppermute | solution.py:448

commit v8 on v7

--- a/solution.py
+++ b/solution.py
@@ -68,45 +68,51 @@
     return pltpu.roll(value, shift % LANES, 1) if shift % LANES else value
 
 
-def halves(index):
+def apart(slots, out):
     upper = lax.rem(lax.axis_index("gy") // HALF, 2) == 1
-    count = index.shape[0] // 2
-    low = index[pl.ds(0, count, stride=2), :]
-    high = index[pl.ds(1, count, stride=2), :]
-    return jnp.where(upper, high, low), jnp.where(upper, low, high)
-
-
-def apart(slots, out):
-    own, mirror = halves(slots)
-    lane = lax.broadcasted_iota(jnp.int32, own.shape, 1)
+    lane = lax.broadcasted_iota(jnp.int32, (1, LANES), 1)
+    whole = slots[...]
     for g in range(GROUPS):
-        first = roll(own, -g * CAP)
-        second = roll(mirror, CAP - g * CAP)
-        out[pl.ds(g, own.shape[0], stride=GROUPS), :] = jnp.where(lane < CAP, first, second)
-
-
-def together(rows):
+        first = roll(whole, -g * CAP)
+        second = roll(whole, CAP - g * CAP)
+        for y in range(whole.shape[0] // 2):
+            low, high = slice(2 * y, 2 * y + 1), slice(2 * y + 1, 2 * y + 2)
+            own = jnp.where(upper, first[high], first[low])
+            mirror = jnp.where(upper, second[low], second[high])
+            at = y * GROUPS + g
+            out[at : at + 1, :] = jnp.where(lane < CAP, own, mirror)
+
+
+def weave(rows, lines, out):
+    lane = lax.broadcasted_iota(jnp.int32, (1, LANES), 1)
     each = 2 * CAP
-    fold = LANES // each
-    count = rows.shape[0] // fold
-    lane = lax.broadcasted_iota(jnp.int32, (count, LANES), 1)
-    kept = jnp.zeros_like(lane)
-    for g in range(fold):
-        moved = roll(rows[pl.ds(g, count, stride=fold), :], g * each)
-        kept = jnp.where((lane >= g * each) & (lane < (g + 1) * each), moved, kept)
-    return kept
-
-
-def by_plane(rows, out):
-    count = rows.shape[0] // HALF
-    each = 2 * CAP
-    lane = lax.broadcasted_iota(jnp.int32, (count, LANES), 1)
-    for core in range(CORES):
-        kept = jnp.zeros_like(lane)
-        for p in range(PLANES):
-            moved = roll(rows[pl.ds(p * CORES + core, count, stride=HALF), :], p * each)
-            kept = jnp.where((lane >= p * each) & (lane < (p + 1) * each), moved, kept)
-        out[pl.ds(core, count, stride=CORES), :] = kept
+    moved = [roll(rows, g * each) for g in range(LANES // each)]
+    for i, line in enumerate(lines):
+        kept = moved[0][line[0] : line[0] + 1]
+        for g in range(1, len(line)):
+            kept = jnp.where(lane >= g * each, moved[g][line[g] : line[g] + 1], kept)
+        out[i : i + 1, :] = kept
+
+
+def in_order(count):
+    fold = LANES // (2 * CAP)
+    return [[i + g for g in range(fold)] for i in range(0, count, fold)]
+
+
+def plane_first(rows, count):
+    def place(i):
+        y, p, core = i // HALF, i % HALF // CORES, i % CORES
+        return p * (count // PLANES) + y * CORES + core
+
+    return [[place(i) for i in line] for line in rows]
+
+
+def beside(count):
+    return [
+        [y * HALF + p * CORES + core for p in range(PLANES)]
+        for y in range(count // HALF)
+        for core in range(CORES)
+    ]
 
 
 def planes_kernel(slots, slots_out):
@@ -208,9 +214,9 @@
     copies[5].wait()
     copies[6].wait()
     apart(indices.at[2], rows_held)
-    by_plane(rows_held, slots_out)
+    weave(rows_held[...], beside(rows_held.shape[0]), slots_out)
     apart(indices.at[3], rows_held)
-    order_out[...] = together(rows_held)
+    weave(rows_held[...], in_order(rows_held.shape[0]), order_out)
     copies[7].wait()
     copies[8].wait()
 
@@ -237,13 +243,9 @@
 
 def request_kernel(table, mirror, slots, send_out, held):
     nodes = table.shape[0]
-    plane = slots.shape[0] // PLANES
-    count = plane // CORES
-    for p in range(PLANES):
-        for core in range(CORES):
-            part = slots[pl.ds(p * plane + core, count, stride=CORES), :]
-            held[pl.ds(p * CORES + core, count, stride=HALF), :] = part
-    asked = together(held)
+    count = slots.shape[0]
+    weave(slots[...], plane_first(in_order(count), count), held)
+    asked = held[...]
     lane = lax.broadcasted_iota(jnp.int32, asked.shape, 1)
     asked = asked + jnp.where((lane & (2 * CAP - 1)) >= CAP, nodes, 0)
     for c in range(0, send_out.shape[0], CHUNK):
@@ -430,7 +432,7 @@
     send = pl.pallas_call(
         request_kernel,
         out_shape=jax.ShapeDtypeStruct((edges, width), bf16),
-        scratch_shapes=[pltpu.VMEM(rows_shape.shape, jnp.int32)],
+        scratch_shapes=[pltpu.VMEM(index.shape, jnp.int32)],
         compiler_params=params,
     )(following, mirror, slots)
     picked = exchange(send.reshape(sectors // 2, -1, width), group).reshape(edges, width)

time: 121 us -> 121 us (level)
  no operation moved by 1% of the time
where the time goes in v8:
time: 121 us; the launch traced here: 120 us
  blocking collectives  56.5 us (47%)
  starting transfers between devices  41.6 us (34%)
  Pallas kernels  12.7 us (10%)
  waiting for transfers between devices  8.62 us (7%)
    all_to_all x3, blocking collectives, exchange(): lax.all_to_all(array, 'gy', 0, 0, axis_index_groups=groups, tiled=True)  56.5 us
    ppermute x1, starting transfers between devices, on_device(): far = lax.ppermute(far, 'gx', far_bands)  15.6 us
    ppermute x1, starting transfers between devices, on_device(): other = lax.ppermute(other, 'gy', far_sectors)  9.08 us
    ppermute x1, starting transfers between devices, on_device(): other = lax.ppermute(table, 'gy', far_sectors)  9.07 us
    ppermute x1, waiting for transfers between devices, on_device(): other = lax.ppermute(table, 'gy', far_sectors)  4 us
    ppermute x1, waiting for transfers between devices, on_device(): near = lax.ppermute(near, 'gx', near_bands)  3.82 us
    pallas_call x1, Pallas kernels, on_device(): pl.pallas_call(gather_kernel, in_specs=[vmem, hbm, vmem] + [hbm] * 8, out...  2.55 us
  transfers between devices with their start and end apart: 7, of which 4 were waited for; matrix products, arithmetic and copies ran while one was open for 0% of the time, Pallas kernels for 4%

profile of v8, /device:TPU:6, one launch (start us, length us, event | category | flops | bytes accessed | tf_op | source)
XLA Modules:
  0.0 120.3 jit_solution(14271175400425970621)
XLA Ops:
  0.6 0.9 shard_map.149
  1.5 15.6 %collective-permute-start = (bf16[64,512]{1,0:T(8,128)(2,1)S(1)}, bf16[64,512]{1,0:T(8,128)(2,1)S(1)}, u32[]{:S(2)}, u32[]{:S(2)}) collective-permute-start(bf16[64,512]{1,0:T(8,128)(2,1)S(1)} %get-tuple-element.23), channel_id=1, source_target_pairs={{64,128},{128,64},{192,256},{256,192},{320,384},{384,320},{65,129}... | collective-permute-start | bytes 196616 | tf_op jit(solution)/shard_map/ppermute | solution.py:365
  17.2 1.9 %collective-permute-start.1 = (bf16[64,512]{1,0:T(8,128)(2,1)S(1)}, bf16[64,512]{1,0:T(8,128)(2,1)S(1)}, u32[]{:S(2)}, u32[]{:S(2)}) collective-permute-start(bf16[64,512]{1,0:T(8,128)(2,1)S(1)} %get-tuple-element.24), channel_id=1, source_target_pairs={{0,64},{64,0},{128,192},{192,128},{256,320},{320,256},{384,448},{4... | collective-permute-start | bytes 196616 | tf_op jit(solution)/shard_map/ppermute | solution.py:366
  19.1 0.4 collective-permute-done.far
  19.5 3.8 %collective-permute-done.1.near = bf16[64,512]{1,0:T(8,128)(2,1)S(1)} collective-permute-done((bf16[64,512]{1,0:T(8,128)(2,1)S(1)}, bf16[64,512]{1,0:T(8,128)(2,1)S(1)}, u32[]{:S(2)}, u32[]{:S(2)}) %collective-permute-start.1) | collective-permute-done | bytes 65568 | tf_op jit(solution)/shard_map/ppermute | solution.py:366
  23.3 0.8 shard_map.151
  24.1 9.1 %collective-permute-start.2 = (bf16[4,8,512]{2,1,0:T(8,128)(2,1)S(1)}, bf16[4,8,512]{2,1,0:T(8,128)(2,1)S(1)}, u32[]{:S(2)}, u32[]{:S(2)}) collective-permute-start(bf16[4,8,512]{2,1,0:T(8,128)(2,1)S(1)} %get-tuple-element.26), channel_id=1, source_target_pairs={{0,63},{1,2},{2,1},{3,4},{4,3},{5,6},{6,5},{7,8},{8,7},{9,10},{10,... | collective-permute-start | bytes 98312 | tf_op jit(solution)/shard_map/ppermute | solution.py:379
  33.2 1.9 %collective-permute-start.3 = (bf16[4,8,512]{2,1,0:T(8,128)(2,1)S(1)}, bf16[4,8,512]{2,1,0:T(8,128)(2,1)S(1)}, u32[]{:S(2)}, u32[]{:S(2)}) collective-permute-start(bf16[4,8,512]{2,1,0:T(8,128)(2,1)S(1)} %get-tuple-element.27), channel_id=1, source_target_pairs={{0,1},{1,0},{2,3},{3,2},{4,5},{5,4},{6,7},{7,6},{8,9},{9,8},{10,11... | collective-permute-start | bytes 98312 | tf_op jit(solution)/shard_map/ppermute | solution.py:380
  35.1 2.5 %shard_map.150 = (f32[1024,512]{1,0:T(8,128)S(1)}, bf16[256,1024]{1,0:T(8,128)(2,1)S(1)}, bf16[256,512]{1,0:T(8,128)(2,1)S(1)}, bf16[3,512,512]{2,1,0:T(8,128)(2...) custom-call(bf16[64,512]{1,0:T(8,128)(2,1)S(1)} %collective-permute-done.far, ...), custom_call_target="tpu_custom_call" | custom-call | tf_op jit(solution)/shard_map/pallas_call | solution.py:390
  37.7 0.4 collective-permute-done.2.other
  38.1 1.8 %shard_map.152 = (bf16[256,512]{1,0:T(8,128)(2,1)S(1)}, bf16[256,512]{1,0:T(8,128)(2,1)S(1)}) custom-call(f32[1024,512]{1,0:T(8,128)S(1)} %get-tuple-element.25.partial, bf16[4,8,512]{2,1,0:T(8,128)(2,1)S(1)} %collective-permute-done.2.other, bf16[4,8,512]{2,1,0:T(8,128)(2,1)S(1)} %collective-permute-done.3.mate, ...), custom_call_target="tpu_custom_call" | custom-call | tf_op jit(solution)/shard_map/pallas_call | solution.py:420
  39.9 2.1 %collective-permute-start.4 = (bf16[256,512]{1,0:T(8,128)(2,1)S(1)}, bf16[256,512]{1,0:T(8,128)(2,1)S(1)}, u32[]{:S(2)}, u32[]{:S(2)}) collective-permute-start(bf16[256,512]{1,0:T(8,128)(2,1)S(1)} %get-tuple-element.34.table), channel_id=1, source_target_pairs={{0,8},{1,9},{2,10},{3,11},{4,12},{5,13},{6,14},{7,15},{8,0},{9,1},... | collective-permute-start | bytes 786440 | tf_op jit(solution)/shard_map/ppermute | solution.py:428
  41.9 8.3 %all_to_all.27 = s32[8,1,128]{2,1,0:T(1,128)S(1)} all-to-all(s32[8,1,128]{2,1,0:T(1,128)S(1)} %bitcast.26), channel_id=1, replica_groups={{0,1,16,17,32,33,48,49},{2,3,18,19,34,35,50,51},{4,5,20,21,36,37,52,53}..., dimensions={0} | all-to-all | bytes 8192 | tf_op jit(solution)/shard_map/all_to_all | solution.py:354
  50.3 0.1 shard_map.153
  50.3 15.4 %all_to_all.28 = s32[4,8,128]{2,1,0:T(8,128)S(1)} all-to-all(s32[4,8,128]{2,1,0:T(8,128)S(1)} %bitcast.23), channel_id=1, replica_groups={{0,2,4,6},{1,3,5,7},{8,10,12,14},{9,11,13,15},{16,18,20,22},{17,19,21,2..., dimensions={0} | all-to-all | bytes 32768 | tf_op jit(solution)/shard_map/all_to_all | solution.py:354
  65.7 0.8 shard_map.154
  66.6 0.0 copy-start
  66.6 32.7 %all_to_all.29 = bf16[32,32,512]{2,1,0:T(8,128)(2,1)S(1)} all-to-all(bf16[32,32,512]{2,1,0:T(8,128)(2,1)S(1)} %bitcast.19), channel_id=1, replica_groups={{0,1,2,3,4,5,6,7,16,17,18,19,20,21,22,23,32,33,34,35,36,37,38,39,48,49,..., dimensions={0} | all-to-all | bytes 2097152 | tf_op jit(solution)/shard_map/all_to_all | solution.py:354
  99.4 2.2 %shard_map.155 = (bf16[256,512]{1,0:T(8,128)(2,1)}, bf16[256,512]{1,0:T(8,128)(2,1)S(1)}) custom-call(bf16[1024,512]{1,0:T(8,128)(2,1)S(1)} %bitcast.18, s32[8,128]{1,0:T(8,128)S(1)} %get-tuple-element.36.target, bf16[256,512]{1,0:T(8,128)(2,1)S(1)} %get-tuple-element.37.first, bf16[512,512]{1,0:T(8,128)(2,1)S(1)} %copy-done.1, bf16[512,512]{1,0:T(8,128)(2,1)S(1)} %copy-done.2), custom_call_target="tpu_custom_call" | custom-call | tf_op jit(solution)/shard_map/pallas_call | solution.py:439
  101.6 9.1 %collective-permute-start.5 = (bf16[256,512]{1,0:T(8,128)(2,1)S(1)}, bf16[256,512]{1,0:T(8,128)(2,1)S(1)}, u32[]{:S(2)}, u32[]{:S(2)}) collective-permute-start(bf16[256,512]{1,0:T(8,128)(2,1)S(1)} %get-tuple-element.38.own), channel_id=1, source_target_pairs={{0,63},{1,2},{2,1},{3,4},{4,3},{5,6},{6,5},{7,8},{8,7},{9,10},{10,... | collective-permute-start | bytes 786440 | tf_op jit(solution)/shard_map/ppermute | solution.py:449
  110.7 1.9 %collective-permute-start.6 = (bf16[256,512]{1,0:T(8,128)(2,1)S(1)}, bf16[256,512]{1,0:T(8,128)(2,1)S(1)}, u32[]{:S(2)}, u32[]{:S(2)}) collective-permute-start(bf16[256,512]{1,0:T(8,128)(2,1)S(1)} %get-tuple-element.38.own), channel_id=1, source_target_pairs={{0,1},{1,0},{2,3},{3,2},{4,5},{5,4},{6,7},{7,6},{8,9},{9,8},{10,11... | collective-permute-start | bytes 786440 | tf_op jit(solution)/shard_map/ppermute | solution.py:450
  112.7 1.6 %shard_map.156 = (f32[1024,512]{1,0:T(8,128)S(1)}, bf16[1024,512]{1,0:T(8,128)(2,1)S(1)}, bf16[128,1024]{1,0:T(8,128)(2,1)S(1)}, bf16[512,512]{1,0:T(8,128)(2,1)S(1)}) custom-call(bf16[256,512]{1,0:T(8,128)(2,1)S(1)} %get-tuple-element.38.own, bf16[128,512]{1,0:T(8,128)(2,1)S(1)} %bitcast.20, s32[8,128]{1,0:T(8,128)S(1)} %fusion.1.source, ...), custom_call_target="tpu_custom_call" | custom-call | tf_op jit(solution)/shard_map/pallas_call | solution.py:456
  114.3 4.0 %collective-permute-done.5.other = bf16[256,512]{1,0:T(8,128)(2,1)S(1)} collective-permute-done((bf16[256,512]{1,0:T(8,128)(2,1)S(1)}, bf16[256,512]{1,0:T(8,128)(2,1)S(1)}, u32[]{:S(2)}, u32[]{:S(2)}) %collective-permute-start.5) | collective-permute-done | bytes 262176 | tf_op jit(solution)/shard_map/ppermute | solution.py:449
  118.3 2.0 %shard_map.157 = bf16[128,512]{1,0:T(8,128)(2,1)} custom-call(f32[1024,512]{1,0:T(8,128)S(1)} %get-tuple-element.39.partial, bf16[256,512]{1,0:T(8,128)(2,1)S(1)} %collective-permute-done.5.other, bf16[256,512]{1,0:T(8,128)(2,1)S(1)} %collective-permute-done.6.mate, bf16[1024,512]{1,0:T(8,128)(2,1)S(1)} %get-tuple-element.40.picks, ...), custom_call_target="tpu_custom_call" | custom-call | tf_op jit(solution)/shard_map/pallas_call | solution.py:469
  (13 shorter events, 0.1 us)
Async XLA Ops:
  1.5 18.0 %collective-permute-start = (bf16[64,512]{1,0:T(8,128)(2,1)S(1)}, bf16[64,512]{1,0:T(8,128)(2,1)S(1)}, u32[]{:S(2)}, u32[]{:S(2)}) collective-permute-start(bf16[64,512]{1,0:T(8,128)(2,1)S(1)} %get-tuple-element.23), channel_id=1, source_target_pairs={{64,128},{128,64},{192,256},{256,192},{320,384},{384,320},{65,129}... | collective-permute-start | bytes 196616 | tf_op jit(solution)/shard_map/ppermute | solution.py:365
  17.2 6.2 %collective-permute-start.1 = (bf16[64,512]{1,0:T(8,128)(2,1)S(1)}, bf16[64,512]{1,0:T(8,128)(2,1)S(1)}, u32[]{:S(2)}, u32[]{:S(2)}) collective-permute-start(bf16[64,512]{1,0:T(8,128)(2,1)S(1)} %get-tuple-element.24), channel_id=1, source_target_pairs={{0,64},{64,0},{128,192},{192,128},{256,320},{320,256},{384,448},{4... | collective-permute-start | bytes 196616 | tf_op jit(solution)/shard_map/ppermute | solution.py:366
  24.1 13.9 %collective-permute-start.2 = (bf16[4,8,512]{2,1,0:T(8,128)(2,1)S(1)}, bf16[4,8,512]{2,1,0:T(8,128)(2,1)S(1)}, u32[]{:S(2)}, u32[]{:S(2)}) collective-permute-start(bf16[4,8,512]{2,1,0:T(8,128)(2,1)S(1)} %get-tuple-element.26), channel_id=1, source_target_pairs={{0,63},{1,2},{2,1},{3,4},{4,3},{5,6},{6,5},{7,8},{8,7},{9,10},{10,... | collective-permute-start | bytes 98312 | tf_op jit(solution)/shard_map/ppermute | solution.py:379
  33.2 4.9 %collective-permute-start.3 = (bf16[4,8,512]{2,1,0:T(8,128)(2,1)S(1)}, bf16[4,8,512]{2,1,0:T(8,128)(2,1)S(1)}, u32[]{:S(2)}, u32[]{:S(2)}) collective-permute-start(bf16[4,8,512]{2,1,0:T(8,128)(2,1)S(1)} %get-tuple-element.27), channel_id=1, source_target_pairs={{0,1},{1,0},{2,3},{3,2},{4,5},{5,4},{6,7},{7,6},{8,9},{9,8},{10,11... | collective-permute-start | bytes 98312 | tf_op jit(solution)/shard_map/ppermute | solution.py:380
  39.9 59.5 %copy-start.1 = (bf16[512,512]{1,0:T(8,128)(2,1)S(1)}, bf16[512,512]{1,0:T(8,128)(2,1)}, u32[]{:S(2)}) copy-start(bf16[512,512]{1,0:T(8,128)(2,1)} %w_update.4) | copy-start | bytes 1572868
  39.9 59.5 %copy-start.2 = (bf16[512,512]{1,0:T(8,128)(2,1)S(1)}, bf16[512,512]{1,0:T(8,128)(2,1)}, u32[]{:S(2)}) copy-start(bf16[512,512]{1,0:T(8,128)(2,1)} %w_next.3) | copy-start | bytes 1572868
  39.9 25.9 %collective-permute-start.4 = (bf16[256,512]{1,0:T(8,128)(2,1)S(1)}, bf16[256,512]{1,0:T(8,128)(2,1)S(1)}, u32[]{:S(2)}, u32[]{:S(2)}) collective-permute-start(bf16[256,512]{1,0:T(8,128)(2,1)S(1)} %get-tuple-element.34.table), channel_id=1, source_target_pairs={{0,8},{1,9},{2,10},{3,11},{4,12},{5,13},{6,14},{7,15},{8,0},{9,1},... | collective-permute-start | bytes 786440 | tf_op jit(solution)/shard_map/ppermute | solution.py:428
  66.6 46.1 %copy-start.4 = (s32[1,1,1024]{2,1,0:T(1,128)S(1)}, s32[1,1,1024]{2,1,0:T(1,128)}, u32[]{:S(2)}) copy-start(s32[1,1,1024]{2,1,0:T(1,128)} %param.26) | copy-start | bytes 12292
  66.6 46.1 %copy-start = (bf16[2,64,512]{2,1,0:T(8,128)(2,1)S(1)}, bf16[2,64,512]{2,1,0:T(8,128)(2,1)}, u32[]{:S(2)}) copy-start(bf16[2,64,512]{2,1,0:T(8,128)(2,1)} %grid.5) | copy-start | bytes 393220
  66.6 46.1 %copy-start.3 = (s32[1,1,1024]{2,1,0:T(1,128)S(1)}, s32[1,1,1024]{2,1,0:T(1,128)}, u32[]{:S(2)}) copy-start(s32[1,1,1024]{2,1,0:T(1,128)} %param.27) | copy-start | bytes 12292
  101.6 16.7 %collective-permute-start.5 = (bf16[256,512]{1,0:T(8,128)(2,1)S(1)}, bf16[256,512]{1,0:T(8,128)(2,1)S(1)}, u32[]{:S(2)}, u32[]{:S(2)}) collective-permute-start(bf16[256,512]{1,0:T(8,128)(2,1)S(1)} %get-tuple-element.38.own), channel_id=1, source_target_pairs={{0,63},{1,2},{2,1},{3,4},{4,3},{5,6},{6,5},{7,8},{8,7},{9,10},{10,... | collective-permute-start | bytes 786440 | tf_op jit(solution)/shard_map/ppermute | solution.py:449
  110.7 7.6 %collective-permute-start.6 = (bf16[256,512]{1,0:T(8,128)(2,1)S(1)}, bf16[256,512]{1,0:T(8,128)(2,1)S(1)}, u32[]{:S(2)}, u32[]{:S(2)}) collective-permute-start(bf16[256,512]{1,0:T(8,128)(2,1)S(1)} %get-tuple-element.38.own), channel_id=1, source_target_pairs={{0,1},{1,0},{2,3},{3,2},{4,5},{5,4},{6,7},{7,6},{8,9},{9,8},{10,11... | collective-permute-start | bytes 786440 | tf_op jit(solution)/shard_map/ppermute | solution.py:450

commit v9 on v8

--- a/solution.py
+++ b/solution.py
@@ -9,7 +9,7 @@
 LON_DEV = 64
 EPSILON = 1e-05
 LANES = 128
-CHUNK = 256
+CHUNK = 1024
 CAP = 16
 GROUPS = LANES // CAP
 HALF = 8

time: 121 us -> 121 us (level)
  transfers between devices with their start and end apart: 7 -> 7, of which waited for: 4 -> 4; matrix products, arithmetic and copies ran while one was open for 0% -> 0% of each run, Pallas kernels for 4% -> 3%
where the time goes in v9:
time: 121 us; the launch traced here: 120 us
  blocking collectives  56.5 us (47%)
  starting transfers between devices  41.6 us (34%)
  Pallas kernels  12.1 us (10%)
  waiting for transfers between devices  9.16 us (8%)
    all_to_all x3, blocking collectives, exchange(): lax.all_to_all(array, 'gy', 0, 0, axis_index_groups=groups, tiled=True)  56.5 us
    ppermute x1, starting transfers between devices, on_device(): far = lax.ppermute(far, 'gx', far_bands)  15.6 us
    ppermute x1, starting transfers between devices, on_device(): other = lax.ppermute(other, 'gy', far_sectors)  9.08 us
    ppermute x1, starting transfers between devices, on_device(): other = lax.ppermute(table, 'gy', far_sectors)  9.07 us
    ppermute x1, waiting for transfers between devices, on_device(): other = lax.ppermute(table, 'gy', far_sectors)  4.54 us
    ppermute x1, waiting for transfers between devices, on_device(): near = lax.ppermute(near, 'gx', near_bands)  3.82 us
    pallas_call x1, Pallas kernels, on_device(): pl.pallas_call(gather_kernel, in_specs=[vmem, hbm, vmem] + [hbm] * 8, out...  2.55 us
  transfers between devices with their start and end apart: 7, of which 4 were waited for; matrix products, arithmetic and copies ran while one was open for 0% of the time, Pallas kernels for 3%

profile of v9, /device:TPU:6, one launch (start us, length us, event | category | flops | bytes accessed | tf_op | source)
XLA Modules:
  0.0 120.2 jit_solution(8899141023681768560)
XLA Ops:
  0.6 0.9 shard_map.149
  1.5 15.6 %collective-permute-start = (bf16[64,512]{1,0:T(8,128)(2,1)S(1)}, bf16[64,512]{1,0:T(8,128)(2,1)S(1)}, u32[]{:S(2)}, u32[]{:S(2)}) collective-permute-start(bf16[64,512]{1,0:T(8,128)(2,1)S(1)} %get-tuple-element.23), channel_id=1, source_target_pairs={{64,128},{128,64},{192,256},{256,192},{320,384},{384,320},{65,129}... | collective-permute-start | bytes 196616 | tf_op jit(solution)/shard_map/ppermute | solution.py:365
  17.2 1.9 %collective-permute-start.1 = (bf16[64,512]{1,0:T(8,128)(2,1)S(1)}, bf16[64,512]{1,0:T(8,128)(2,1)S(1)}, u32[]{:S(2)}, u32[]{:S(2)}) collective-permute-start(bf16[64,512]{1,0:T(8,128)(2,1)S(1)} %get-tuple-element.24), channel_id=1, source_target_pairs={{0,64},{64,0},{128,192},{192,128},{256,320},{320,256},{384,448},{4... | collective-permute-start | bytes 196616 | tf_op jit(solution)/shard_map/ppermute | solution.py:366
  19.1 0.4 collective-permute-done.far
  19.5 3.8 %collective-permute-done.1.near = bf16[64,512]{1,0:T(8,128)(2,1)S(1)} collective-permute-done((bf16[64,512]{1,0:T(8,128)(2,1)S(1)}, bf16[64,512]{1,0:T(8,128)(2,1)S(1)}, u32[]{:S(2)}, u32[]{:S(2)}) %collective-permute-start.1) | collective-permute-done | bytes 65568 | tf_op jit(solution)/shard_map/ppermute | solution.py:366
  23.3 0.8 shard_map.151
  24.1 9.1 %collective-permute-start.2 = (bf16[4,8,512]{2,1,0:T(8,128)(2,1)S(1)}, bf16[4,8,512]{2,1,0:T(8,128)(2,1)S(1)}, u32[]{:S(2)}, u32[]{:S(2)}) collective-permute-start(bf16[4,8,512]{2,1,0:T(8,128)(2,1)S(1)} %get-tuple-element.26), channel_id=1, source_target_pairs={{0,63},{1,2},{2,1},{3,4},{4,3},{5,6},{6,5},{7,8},{8,7},{9,10},{10,... | collective-permute-start | bytes 98312 | tf_op jit(solution)/shard_map/ppermute | solution.py:379
  33.2 1.9 %collective-permute-start.3 = (bf16[4,8,512]{2,1,0:T(8,128)(2,1)S(1)}, bf16[4,8,512]{2,1,0:T(8,128)(2,1)S(1)}, u32[]{:S(2)}, u32[]{:S(2)}) collective-permute-start(bf16[4,8,512]{2,1,0:T(8,128)(2,1)S(1)} %get-tuple-element.27), channel_id=1, source_target_pairs={{0,1},{1,0},{2,3},{3,2},{4,5},{5,4},{6,7},{7,6},{8,9},{9,8},{10,11... | collective-permute-start | bytes 98312 | tf_op jit(solution)/shard_map/ppermute | solution.py:380
  35.1 2.5 %shard_map.150 = (f32[1024,512]{1,0:T(8,128)S(1)}, bf16[256,1024]{1,0:T(8,128)(2,1)S(1)}, bf16[256,512]{1,0:T(8,128)(2,1)S(1)}, bf16[3,512,512]{2,1,0:T(8,128)(2...) custom-call(bf16[64,512]{1,0:T(8,128)(2,1)S(1)} %collective-permute-done.far, ...), custom_call_target="tpu_custom_call" | custom-call | tf_op jit(solution)/shard_map/pallas_call | solution.py:390
  37.7 0.4 collective-permute-done.2.other
  38.1 1.7 %shard_map.152 = (bf16[256,512]{1,0:T(8,128)(2,1)S(1)}, bf16[256,512]{1,0:T(8,128)(2,1)S(1)}) custom-call(f32[1024,512]{1,0:T(8,128)S(1)} %get-tuple-element.25.partial, bf16[4,8,512]{2,1,0:T(8,128)(2,1)S(1)} %collective-permute-done.2.other, bf16[4,8,512]{2,1,0:T(8,128)(2,1)S(1)} %collective-permute-done.3.mate, ...), custom_call_target="tpu_custom_call" | custom-call | tf_op jit(solution)/shard_map/pallas_call | solution.py:420
  39.8 2.1 %collective-permute-start.4 = (bf16[256,512]{1,0:T(8,128)(2,1)S(1)}, bf16[256,512]{1,0:T(8,128)(2,1)S(1)}, u32[]{:S(2)}, u32[]{:S(2)}) collective-permute-start(bf16[256,512]{1,0:T(8,128)(2,1)S(1)} %get-tuple-element.34.table), channel_id=1, source_target_pairs={{0,8},{1,9},{2,10},{3,11},{4,12},{5,13},{6,14},{7,15},{8,0},{9,1},... | collective-permute-start | bytes 786440 | tf_op jit(solution)/shard_map/ppermute | solution.py:428
  41.8 8.3 %all_to_all.27 = s32[8,1,128]{2,1,0:T(1,128)S(1)} all-to-all(s32[8,1,128]{2,1,0:T(1,128)S(1)} %bitcast.26), channel_id=1, replica_groups={{0,1,16,17,32,33,48,49},{2,3,18,19,34,35,50,51},{4,5,20,21,36,37,52,53}..., dimensions={0} | all-to-all | bytes 8192 | tf_op jit(solution)/shard_map/all_to_all | solution.py:354
  50.2 0.1 shard_map.153
  50.2 15.4 %all_to_all.28 = s32[4,8,128]{2,1,0:T(8,128)S(1)} all-to-all(s32[4,8,128]{2,1,0:T(8,128)S(1)} %bitcast.23), channel_id=1, replica_groups={{0,2,4,6},{1,3,5,7},{8,10,12,14},{9,11,13,15},{16,18,20,22},{17,19,21,2..., dimensions={0} | all-to-all | bytes 32768 | tf_op jit(solution)/shard_map/all_to_all | solution.py:354
  65.7 0.8 shard_map.154
  66.5 0.0 copy-start.4
  66.5 32.7 %all_to_all.29 = bf16[32,32,512]{2,1,0:T(8,128)(2,1)S(1)} all-to-all(bf16[32,32,512]{2,1,0:T(8,128)(2,1)S(1)} %bitcast.19), channel_id=1, replica_groups={{0,1,2,3,4,5,6,7,16,17,18,19,20,21,22,23,32,33,34,35,36,37,38,39,48,49,..., dimensions={0} | all-to-all | bytes 2097152 | tf_op jit(solution)/shard_map/all_to_all | solution.py:354
  99.3 2.2 %shard_map.155 = (bf16[256,512]{1,0:T(8,128)(2,1)}, bf16[256,512]{1,0:T(8,128)(2,1)S(1)}) custom-call(bf16[1024,512]{1,0:T(8,128)(2,1)S(1)} %bitcast.18, s32[8,128]{1,0:T(8,128)S(1)} %get-tuple-element.36.target, bf16[256,512]{1,0:T(8,128)(2,1)S(1)} %get-tuple-element.37.first, bf16[512,512]{1,0:T(8,128)(2,1)S(1)} %copy-done.1, bf16[512,512]{1,0:T(8,128)(2,1)S(1)} %copy-done.2), custom_call_target="tpu_custom_call" | custom-call | tf_op jit(solution)/shard_map/pallas_call | solution.py:439
  101.5 9.1 %collective-permute-start.5 = (bf16[256,512]{1,0:T(8,128)(2,1)S(1)}, bf16[256,512]{1,0:T(8,128)(2,1)S(1)}, u32[]{:S(2)}, u32[]{:S(2)}) collective-permute-start(bf16[256,512]{1,0:T(8,128)(2,1)S(1)} %get-tuple-element.38.own), channel_id=1, source_target_pairs={{0,63},{1,2},{2,1},{3,4},{4,3},{5,6},{6,5},{7,8},{8,7},{9,10},{10,... | collective-permute-start | bytes 786440 | tf_op jit(solution)/shard_map/ppermute | solution.py:449
  110.6 1.9 %collective-permute-start.6 = (bf16[256,512]{1,0:T(8,128)(2,1)S(1)}, bf16[256,512]{1,0:T(8,128)(2,1)S(1)}, u32[]{:S(2)}, u32[]{:S(2)}) collective-permute-start(bf16[256,512]{1,0:T(8,128)(2,1)S(1)} %get-tuple-element.38.own), channel_id=1, source_target_pairs={{0,1},{1,0},{2,3},{3,2},{4,5},{5,4},{6,7},{7,6},{8,9},{9,8},{10,11... | collective-permute-start | bytes 786440 | tf_op jit(solution)/shard_map/ppermute | solution.py:450
  112.5 1.1 shard_map.156
  113.6 4.5 %collective-permute-done.5.other = bf16[256,512]{1,0:T(8,128)(2,1)S(1)} collective-permute-done((bf16[256,512]{1,0:T(8,128)(2,1)S(1)}, bf16[256,512]{1,0:T(8,128)(2,1)S(1)}, u32[]{:S(2)}, u32[]{:S(2)}) %collective-permute-start.5) | collective-permute-done | bytes 262176 | tf_op jit(solution)/shard_map/ppermute | solution.py:449
  118.2 2.0 %shard_map.157 = bf16[128,512]{1,0:T(8,128)(2,1)} custom-call(f32[1024,512]{1,0:T(8,128)S(1)} %get-tuple-element.39.partial, bf16[256,512]{1,0:T(8,128)(2,1)S(1)} %collective-permute-done.5.other, bf16[256,512]{1,0:T(8,128)(2,1)S(1)} %collective-permute-done.6.mate, bf16[1024,512]{1,0:T(8,128)(2,1)S(1)} %get-tuple-element.40.picks, ...), custom_call_target="tpu_custom_call" | custom-call | tf_op jit(solution)/shard_map/pallas_call | solution.py:469
  (13 shorter events, 0.1 us)
Async XLA Ops:
  1.5 18.0 %collective-permute-start = (bf16[64,512]{1,0:T(8,128)(2,1)S(1)}, bf16[64,512]{1,0:T(8,128)(2,1)S(1)}, u32[]{:S(2)}, u32[]{:S(2)}) collective-permute-start(bf16[64,512]{1,0:T(8,128)(2,1)S(1)} %get-tuple-element.23), channel_id=1, source_target_pairs={{64,128},{128,64},{192,256},{256,192},{320,384},{384,320},{65,129}... | collective-permute-start | bytes 196616 | tf_op jit(solution)/shard_map/ppermute | solution.py:365
  17.2 6.2 %collective-permute-start.1 = (bf16[64,512]{1,0:T(8,128)(2,1)S(1)}, bf16[64,512]{1,0:T(8,128)(2,1)S(1)}, u32[]{:S(2)}, u32[]{:S(2)}) collective-permute-start(bf16[64,512]{1,0:T(8,128)(2,1)S(1)} %get-tuple-element.24), channel_id=1, source_target_pairs={{0,64},{64,0},{128,192},{192,128},{256,320},{320,256},{384,448},{4... | collective-permute-start | bytes 196616 | tf_op jit(solution)/shard_map/ppermute | solution.py:366
  24.1 13.9 %collective-permute-start.2 = (bf16[4,8,512]{2,1,0:T(8,128)(2,1)S(1)}, bf16[4,8,512]{2,1,0:T(8,128)(2,1)S(1)}, u32[]{:S(2)}, u32[]{:S(2)}) collective-permute-start(bf16[4,8,512]{2,1,0:T(8,128)(2,1)S(1)} %get-tuple-element.26), channel_id=1, source_target_pairs={{0,63},{1,2},{2,1},{3,4},{4,3},{5,6},{6,5},{7,8},{8,7},{9,10},{10,... | collective-permute-start | bytes 98312 | tf_op jit(solution)/shard_map/ppermute | solution.py:379
  33.2 4.9 %collective-permute-start.3 = (bf16[4,8,512]{2,1,0:T(8,128)(2,1)S(1)}, bf16[4,8,512]{2,1,0:T(8,128)(2,1)S(1)}, u32[]{:S(2)}, u32[]{:S(2)}) collective-permute-start(bf16[4,8,512]{2,1,0:T(8,128)(2,1)S(1)} %get-tuple-element.27), channel_id=1, source_target_pairs={{0,1},{1,0},{2,3},{3,2},{4,5},{5,4},{6,7},{7,6},{8,9},{9,8},{10,11... | collective-permute-start | bytes 98312 | tf_op jit(solution)/shard_map/ppermute | solution.py:380
  39.8 59.5 %copy-start.1 = (bf16[512,512]{1,0:T(8,128)(2,1)S(1)}, bf16[512,512]{1,0:T(8,128)(2,1)}, u32[]{:S(2)}) copy-start(bf16[512,512]{1,0:T(8,128)(2,1)} %w_update.4) | copy-start | bytes 1572868
  39.8 59.5 %copy-start.2 = (bf16[512,512]{1,0:T(8,128)(2,1)S(1)}, bf16[512,512]{1,0:T(8,128)(2,1)}, u32[]{:S(2)}) copy-start(bf16[512,512]{1,0:T(8,128)(2,1)} %w_next.3) | copy-start | bytes 1572868
  39.8 25.9 %collective-permute-start.4 = (bf16[256,512]{1,0:T(8,128)(2,1)S(1)}, bf16[256,512]{1,0:T(8,128)(2,1)S(1)}, u32[]{:S(2)}, u32[]{:S(2)}) collective-permute-start(bf16[256,512]{1,0:T(8,128)(2,1)S(1)} %get-tuple-element.34.table), channel_id=1, source_target_pairs={{0,8},{1,9},{2,10},{3,11},{4,12},{5,13},{6,14},{7,15},{8,0},{9,1},... | collective-permute-start | bytes 786440 | tf_op jit(solution)/shard_map/ppermute | solution.py:428
  66.5 46.0 %copy-start.4 = (s32[1,1,1024]{2,1,0:T(1,128)S(1)}, s32[1,1,1024]{2,1,0:T(1,128)}, u32[]{:S(2)}) copy-start(s32[1,1,1024]{2,1,0:T(1,128)} %param.26) | copy-start | bytes 12292
  66.5 46.0 %copy-start = (bf16[2,64,512]{2,1,0:T(8,128)(2,1)S(1)}, bf16[2,64,512]{2,1,0:T(8,128)(2,1)}, u32[]{:S(2)}) copy-start(bf16[2,64,512]{2,1,0:T(8,128)(2,1)} %grid.5) | copy-start | bytes 393220
  66.5 46.0 %copy-start.3 = (s32[1,1,1024]{2,1,0:T(1,128)S(1)}, s32[1,1,1024]{2,1,0:T(1,128)}, u32[]{:S(2)}) copy-start(s32[1,1,1024]{2,1,0:T(1,128)} %param.27) | copy-start | bytes 12292
  101.5 16.7 %collective-permute-start.5 = (bf16[256,512]{1,0:T(8,128)(2,1)S(1)}, bf16[256,512]{1,0:T(8,128)(2,1)S(1)}, u32[]{:S(2)}, u32[]{:S(2)}) collective-permute-start(bf16[256,512]{1,0:T(8,128)(2,1)S(1)} %get-tuple-element.38.own), channel_id=1, source_target_pairs={{0,63},{1,2},{2,1},{3,4},{4,3},{5,6},{6,5},{7,8},{8,7},{9,10},{10,... | collective-permute-start | bytes 786440 | tf_op jit(solution)/shard_map/ppermute | solution.py:449
  110.6 7.6 %collective-permute-start.6 = (bf16[256,512]{1,0:T(8,128)(2,1)S(1)}, bf16[256,512]{1,0:T(8,128)(2,1)S(1)}, u32[]{:S(2)}, u32[]{:S(2)}) collective-permute-start(bf16[256,512]{1,0:T(8,128)(2,1)S(1)} %get-tuple-element.38.own), channel_id=1, source_target_pairs={{0,1},{1,0},{2,3},{3,2},{4,5},{5,4},{6,7},{7,6},{8,9},{9,8},{10,11... | collective-permute-start | bytes 786440 | tf_op jit(solution)/shard_map/ppermute | solution.py:450

commit v10 on v8

--- a/solution.py
+++ b/solution.py
@@ -241,7 +241,7 @@
     next_out[...] = dot(first, weights[2]).astype(jnp.bfloat16)
 
 
-def request_kernel(table, mirror, slots, send_out, held):
+def request_kernel(table, upper, lower, slots, send_out, held):
     nodes = table.shape[0]
     count = slots.shape[0]
     weave(slots[...], plane_first(in_order(count), count), held)
@@ -251,7 +251,9 @@
     for c in range(0, send_out.shape[0], CHUNK):
         rows = slice(c, c + CHUNK)
         col = column(asked, rows)
-        acc = dot(pick(col, nodes), table[...]) + dot(pick(col - nodes, nodes), mirror[...])
+        acc = dot(pick(col, nodes), table[...])
+        acc = acc + dot(pick(col - nodes, nodes // 2), upper[...])
+        acc = acc + dot(pick(col - nodes - nodes // 2, nodes // 2), lower[...])
         send_out[rows, :] = acc.astype(jnp.bfloat16)
 
 
@@ -425,7 +427,9 @@
     )(partial, other, mate, spreading, mesh_held, weights, sides)
 
     following, slots = lax.optimization_barrier((following, slots))
-    mirror = lax.ppermute(following, "gy", [(i, i ^ HALF) for i in range(sectors)])
+    swapped = [(i, i ^ HALF) for i in range(sectors)]
+    upper = lax.ppermute(following[: nodes // 2], "gy", swapped)
+    lower = lax.ppermute(following[nodes // 2 :], "gy", swapped)
     slots = exchange(slots, plane_groups)
     slots = pl.pallas_call(planes_kernel, out_shape=rows_shape, compiler_params=params)(slots)
     slots = exchange(slots, column_groups)
@@ -434,7 +438,7 @@
         out_shape=jax.ShapeDtypeStruct((edges, width), bf16),
         scratch_shapes=[pltpu.VMEM(index.shape, jnp.int32)],
         compiler_params=params,
-    )(following, mirror, slots)
+    )(following, upper, lower, slots)
     picked = exchange(send.reshape(sectors // 2, -1, width), group).reshape(edges, width)
     second, table = pl.pallas_call(
         process_kernel,

time: 121 us -> 121 us (level)
  blocking collectives: 56.5 us -> 48.6 us
  starting transfers between devices: 41.6 us -> 49.4 us
    all_to_all x3, blocking collectives: 56.5 us -> 48.6 us  [exchange(): lax.all_to_all(array, 'gy', 0, 0, axis_index_groups=groups, tiled=True)]
    ppermute x1 -> x2, starting transfers between devices: 2.05 us -> 9.88 us  [the longest x1 7.83 us: on_device(): lower = lax.ppermute(following[nodes // 2:], 'gy', swapped)]
  transfers between devices with their start and end apart: 7 -> 8, of which waited for: 4 -> 4; matrix products, arithmetic and copies ran while one was open for 0% -> 0% of each run, Pallas kernels for 4% -> 3%
where the time goes in v10:
time: 121 us
  starting transfers between devices  49.4 us (41%)
  blocking collectives  48.6 us (40%)
  Pallas kernels  13 us (11%)
  waiting for transfers between devices  8.62 us (7%)
    all_to_all x3, blocking collectives, exchange(): lax.all_to_all(array, 'gy', 0, 0, axis_index_groups=groups, tiled=True)  48.6 us
    ppermute x1, starting transfers between devices, on_device(): far = lax.ppermute(far, 'gx', far_bands)  15.6 us
    ppermute x1, starting transfers between devices, on_device(): other = lax.ppermute(other, 'gy', far_sectors)  9.08 us
    ppermute x1, starting transfers between devices, on_device(): other = lax.ppermute(table, 'gy', far_sectors)  9.08 us
    ppermute x1, starting transfers between devices, on_device(): lower = lax.ppermute(following[nodes // 2:], 'gy', swapped)  7.83 us
    ppermute x1, waiting for transfers between devices, on_device(): other = lax.ppermute(table, 'gy', far_sectors)  4 us
    ppermute x1, waiting for transfers between devices, on_device(): near = lax.ppermute(near, 'gx', near_bands)  3.82 us
    pallas_call x1, Pallas kernels, on_device(): pl.pallas_call(gather_kernel, in_specs=[vmem, hbm, vmem] + [hbm] * 8, out...  2.55 us
  transfers between devices with their start and end apart: 8, of which 4 were waited for; matrix products, arithmetic and copies ran while one was open for 0% of the time, Pallas kernels for 3%

profile of v10, /device:TPU:6, one launch (start us, length us, event | category | flops | bytes accessed | tf_op | source)
XLA Modules:
  0.0 120.6 jit_solution(5344515674225429965)
XLA Ops:
  0.6 0.9 shard_map.149
  1.5 15.6 %collective-permute-start = (bf16[64,512]{1,0:T(8,128)(2,1)S(1)}, bf16[64,512]{1,0:T(8,128)(2,1)S(1)}, u32[]{:S(2)}, u32[]{:S(2)}) collective-permute-start(bf16[64,512]{1,0:T(8,128)(2,1)S(1)} %get-tuple-element.23), channel_id=1, source_target_pairs={{64,128},{128,64},{192,256},{256,192},{320,384},{384,320},{65,129}... | collective-permute-start | bytes 196616 | tf_op jit(solution)/shard_map/ppermute | solution.py:367
  17.2 1.9 %collective-permute-start.1 = (bf16[64,512]{1,0:T(8,128)(2,1)S(1)}, bf16[64,512]{1,0:T(8,128)(2,1)S(1)}, u32[]{:S(2)}, u32[]{:S(2)}) collective-permute-start(bf16[64,512]{1,0:T(8,128)(2,1)S(1)} %get-tuple-element.24), channel_id=1, source_target_pairs={{0,64},{64,0},{128,192},{192,128},{256,320},{320,256},{384,448},{4... | collective-permute-start | bytes 196616 | tf_op jit(solution)/shard_map/ppermute | solution.py:368
  19.1 0.4 collective-permute-done.far
  19.5 3.8 %collective-permute-done.1.near = bf16[64,512]{1,0:T(8,128)(2,1)S(1)} collective-permute-done((bf16[64,512]{1,0:T(8,128)(2,1)S(1)}, bf16[64,512]{1,0:T(8,128)(2,1)S(1)}, u32[]{:S(2)}, u32[]{:S(2)}) %collective-permute-start.1) | collective-permute-done | bytes 65568 | tf_op jit(solution)/shard_map/ppermute | solution.py:368
  23.3 0.8 shard_map.151
  24.1 9.1 %collective-permute-start.2 = (bf16[4,8,512]{2,1,0:T(8,128)(2,1)S(1)}, bf16[4,8,512]{2,1,0:T(8,128)(2,1)S(1)}, u32[]{:S(2)}, u32[]{:S(2)}) collective-permute-start(bf16[4,8,512]{2,1,0:T(8,128)(2,1)S(1)} %get-tuple-element.26), channel_id=1, source_target_pairs={{0,63},{1,2},{2,1},{3,4},{4,3},{5,6},{6,5},{7,8},{8,7},{9,10},{10,... | collective-permute-start | bytes 98312 | tf_op jit(solution)/shard_map/ppermute | solution.py:381
  33.2 1.9 %collective-permute-start.3 = (bf16[4,8,512]{2,1,0:T(8,128)(2,1)S(1)}, bf16[4,8,512]{2,1,0:T(8,128)(2,1)S(1)}, u32[]{:S(2)}, u32[]{:S(2)}) collective-permute-start(bf16[4,8,512]{2,1,0:T(8,128)(2,1)S(1)} %get-tuple-element.27), channel_id=1, source_target_pairs={{0,1},{1,0},{2,3},{3,2},{4,5},{5,4},{6,7},{7,6},{8,9},{9,8},{10,11... | collective-permute-start | bytes 98312 | tf_op jit(solution)/shard_map/ppermute | solution.py:382
  35.1 2.5 %shard_map.150 = (f32[1024,512]{1,0:T(8,128)S(1)}, bf16[256,1024]{1,0:T(8,128)(2,1)S(1)}, bf16[256,512]{1,0:T(8,128)(2,1)S(1)}, bf16[3,512,512]{2,1,0:T(8,128)(2...) custom-call(bf16[64,512]{1,0:T(8,128)(2,1)S(1)} %collective-permute-done.far, ...), custom_call_target="tpu_custom_call" | custom-call | tf_op jit(solution)/shard_map/pallas_call | solution.py:392
  37.7 0.4 collective-permute-done.2.other
  38.1 1.8 %shard_map.152 = (bf16[256,512]{1,0:T(8,128)(2,1)S(1)}, bf16[256,512]{1,0:T(8,128)(2,1)S(1)}) custom-call(f32[1024,512]{1,0:T(8,128)S(1)} %get-tuple-element.25.partial, bf16[4,8,512]{2,1,0:T(8,128)(2,1)S(1)} %collective-permute-done.2.other, bf16[4,8,512]{2,1,0:T(8,128)(2,1)S(1)} %collective-permute-done.3.mate, ...), custom_call_target="tpu_custom_call" | custom-call | tf_op jit(solution)/shard_map/pallas_call | solution.py:422
  39.9 2.1 %collective-permute-start.4 = (bf16[128,512]{1,0:T(8,128)(2,1)S(1)}, bf16[128,512]{1,0:T(8,128)(2,1)S(1)}, u32[]{:S(2)}, u32[]{:S(2)}) collective-permute-start(bf16[128,512]{1,0:T(8,128)(2,1)S(1)} %get-tuple-element.45), channel_id=1, source_target_pairs={{0,8},{1,9},{2,10},{3,11},{4,12},{5,13},{6,14},{7,15},{8,0},{9,1},... | collective-permute-start | bytes 393224 | tf_op jit(solution)/shard_map/ppermute | solution.py:431
  42.0 7.8 %collective-permute-start.5 = (bf16[128,512]{1,0:T(8,128)(2,1)S(1)}, bf16[128,512]{1,0:T(8,128)(2,1)S(1)}, u32[]{:S(2)}, u32[]{:S(2)}) collective-permute-start(bf16[128,512]{1,0:T(8,128)(2,1)S(1)} %get-tuple-element.44), channel_id=1, source_target_pairs={{0,8},{1,9},{2,10},{3,11},{4,12},{5,13},{6,14},{7,15},{8,0},{9,1},... | collective-permute-start | bytes 393224 | tf_op jit(solution)/shard_map/ppermute | solution.py:432
  49.8 8.3 %all_to_all.27 = s32[8,1,128]{2,1,0:T(1,128)S(1)} all-to-all(s32[8,1,128]{2,1,0:T(1,128)S(1)} %bitcast.26), channel_id=1, replica_groups={{0,1,16,17,32,33,48,49},{2,3,18,19,34,35,50,51},{4,5,20,21,36,37,52,53}..., dimensions={0} | all-to-all | bytes 8192 | tf_op jit(solution)/shard_map/all_to_all | solution.py:356
  58.1 0.1 shard_map.153
  58.2 8.0 %all_to_all.28 = s32[4,8,128]{2,1,0:T(8,128)S(1)} all-to-all(s32[4,8,128]{2,1,0:T(8,128)S(1)} %bitcast.23), channel_id=1, replica_groups={{0,2,4,6},{1,3,5,7},{8,10,12,14},{9,11,13,15},{16,18,20,22},{17,19,21,2..., dimensions={0} | all-to-all | bytes 32768 | tf_op jit(solution)/shard_map/all_to_all | solution.py:356
  66.2 1.1 shard_map.154
  67.3 32.4 %all_to_all.29 = bf16[32,32,512]{2,1,0:T(8,128)(2,1)S(1)} all-to-all(bf16[32,32,512]{2,1,0:T(8,128)(2,1)S(1)} %bitcast.19), channel_id=1, replica_groups={{0,1,2,3,4,5,6,7,16,17,18,19,20,21,22,23,32,33,34,35,36,37,38,39,48,49,..., dimensions={0} | all-to-all | bytes 2097152 | tf_op jit(solution)/shard_map/all_to_all | solution.py:356
  99.7 2.2 %shard_map.155 = (bf16[256,512]{1,0:T(8,128)(2,1)}, bf16[256,512]{1,0:T(8,128)(2,1)S(1)}) custom-call(bf16[1024,512]{1,0:T(8,128)(2,1)S(1)} %bitcast.18, s32[8,128]{1,0:T(8,128)S(1)} %get-tuple-element.36.target, bf16[256,512]{1,0:T(8,128)(2,1)S(1)} %get-tuple-element.37.first, bf16[512,512]{1,0:T(8,128)(2,1)S(1)} %copy-done.1, bf16[512,512]{1,0:T(8,128)(2,1)S(1)} %copy-done.2), custom_call_target="tpu_custom_call" | custom-call | tf_op jit(solution)/shard_map/pallas_call | solution.py:443
  101.9 9.1 %collective-permute-start.6 = (bf16[256,512]{1,0:T(8,128)(2,1)S(1)}, bf16[256,512]{1,0:T(8,128)(2,1)S(1)}, u32[]{:S(2)}, u32[]{:S(2)}) collective-permute-start(bf16[256,512]{1,0:T(8,128)(2,1)S(1)} %get-tuple-element.38.own), channel_id=1, source_target_pairs={{0,63},{1,2},{2,1},{3,4},{4,3},{5,6},{6,5},{7,8},{8,7},{9,10},{10,... | collective-permute-start | bytes 786440 | tf_op jit(solution)/shard_map/ppermute | solution.py:453
  111.0 1.9 %collective-permute-start.7 = (bf16[256,512]{1,0:T(8,128)(2,1)S(1)}, bf16[256,512]{1,0:T(8,128)(2,1)S(1)}, u32[]{:S(2)}, u32[]{:S(2)}) collective-permute-start(bf16[256,512]{1,0:T(8,128)(2,1)S(1)} %get-tuple-element.38.own), channel_id=1, source_target_pairs={{0,1},{1,0},{2,3},{3,2},{4,5},{5,4},{6,7},{7,6},{8,9},{9,8},{10,11... | collective-permute-start | bytes 786440 | tf_op jit(solution)/shard_map/ppermute | solution.py:454
  113.0 1.6 %shard_map.156 = (f32[1024,512]{1,0:T(8,128)S(1)}, bf16[1024,512]{1,0:T(8,128)(2,1)S(1)}, bf16[128,1024]{1,0:T(8,128)(2,1)S(1)}, bf16[512,512]{1,0:T(8,128)(2,1)S(1)}) custom-call(bf16[256,512]{1,0:T(8,128)(2,1)S(1)} %get-tuple-element.38.own, bf16[128,512]{1,0:T(8,128)(2,1)S(1)} %bitcast.20, s32[8,128]{1,0:T(8,128)S(1)} %fusion.1.source, ...), custom_call_target="tpu_custom_call" | custom-call | tf_op jit(solution)/shard_map/pallas_call | solution.py:460
  114.6 4.0 %collective-permute-done.6.other = bf16[256,512]{1,0:T(8,128)(2,1)S(1)} collective-permute-done((bf16[256,512]{1,0:T(8,128)(2,1)S(1)}, bf16[256,512]{1,0:T(8,128)(2,1)S(1)}, u32[]{:S(2)}, u32[]{:S(2)}) %collective-permute-start.6) | collective-permute-done | bytes 262176 | tf_op jit(solution)/shard_map/ppermute | solution.py:453
  118.6 2.0 %shard_map.157 = bf16[128,512]{1,0:T(8,128)(2,1)} custom-call(f32[1024,512]{1,0:T(8,128)S(1)} %get-tuple-element.39.partial, bf16[256,512]{1,0:T(8,128)(2,1)S(1)} %collective-permute-done.6.other, bf16[256,512]{1,0:T(8,128)(2,1)S(1)} %collective-permute-done.7.mate, bf16[1024,512]{1,0:T(8,128)(2,1)S(1)} %get-tuple-element.40.picks, ...), custom_call_target="tpu_custom_call" | custom-call | tf_op jit(solution)/shard_map/pallas_call | solution.py:473
  (16 shorter events, 0.1 us)
Async XLA Ops:
  1.5 18.0 %collective-permute-start = (bf16[64,512]{1,0:T(8,128)(2,1)S(1)}, bf16[64,512]{1,0:T(8,128)(2,1)S(1)}, u32[]{:S(2)}, u32[]{:S(2)}) collective-permute-start(bf16[64,512]{1,0:T(8,128)(2,1)S(1)} %get-tuple-element.23), channel_id=1, source_target_pairs={{64,128},{128,64},{192,256},{256,192},{320,384},{384,320},{65,129}... | collective-permute-start | bytes 196616 | tf_op jit(solution)/shard_map/ppermute | solution.py:367
  17.2 6.2 %collective-permute-start.1 = (bf16[64,512]{1,0:T(8,128)(2,1)S(1)}, bf16[64,512]{1,0:T(8,128)(2,1)S(1)}, u32[]{:S(2)}, u32[]{:S(2)}) collective-permute-start(bf16[64,512]{1,0:T(8,128)(2,1)S(1)} %get-tuple-element.24), channel_id=1, source_target_pairs={{0,64},{64,0},{128,192},{192,128},{256,320},{320,256},{384,448},{4... | collective-permute-start | bytes 196616 | tf_op jit(solution)/shard_map/ppermute | solution.py:368
  24.1 13.9 %collective-permute-start.2 = (bf16[4,8,512]{2,1,0:T(8,128)(2,1)S(1)}, bf16[4,8,512]{2,1,0:T(8,128)(2,1)S(1)}, u32[]{:S(2)}, u32[]{:S(2)}) collective-permute-start(bf16[4,8,512]{2,1,0:T(8,128)(2,1)S(1)} %get-tuple-element.26), channel_id=1, source_target_pairs={{0,63},{1,2},{2,1},{3,4},{4,3},{5,6},{6,5},{7,8},{8,7},{9,10},{10,... | collective-permute-start | bytes 98312 | tf_op jit(solution)/shard_map/ppermute | solution.py:381
  33.2 4.9 %collective-permute-start.3 = (bf16[4,8,512]{2,1,0:T(8,128)(2,1)S(1)}, bf16[4,8,512]{2,1,0:T(8,128)(2,1)S(1)}, u32[]{:S(2)}, u32[]{:S(2)}) collective-permute-start(bf16[4,8,512]{2,1,0:T(8,128)(2,1)S(1)} %get-tuple-element.27), channel_id=1, source_target_pairs={{0,1},{1,0},{2,3},{3,2},{4,5},{5,4},{6,7},{7,6},{8,9},{9,8},{10,11... | collective-permute-start | bytes 98312 | tf_op jit(solution)/shard_map/ppermute | solution.py:382
  39.9 59.8 %copy-start.1 = (bf16[512,512]{1,0:T(8,128)(2,1)S(1)}, bf16[512,512]{1,0:T(8,128)(2,1)}, u32[]{:S(2)}) copy-start(bf16[512,512]{1,0:T(8,128)(2,1)} %w_update.4) | copy-start | bytes 1572868
  39.9 59.8 %copy-start.2 = (bf16[512,512]{1,0:T(8,128)(2,1)S(1)}, bf16[512,512]{1,0:T(8,128)(2,1)}, u32[]{:S(2)}) copy-start(bf16[512,512]{1,0:T(8,128)(2,1)} %w_next.3) | copy-start | bytes 1572868
  39.9 26.2 %collective-permute-start.4 = (bf16[128,512]{1,0:T(8,128)(2,1)S(1)}, bf16[128,512]{1,0:T(8,128)(2,1)S(1)}, u32[]{:S(2)}, u32[]{:S(2)}) collective-permute-start(bf16[128,512]{1,0:T(8,128)(2,1)S(1)} %get-tuple-element.45), channel_id=1, source_target_pairs={{0,8},{1,9},{2,10},{3,11},{4,12},{5,13},{6,14},{7,15},{8,0},{9,1},... | collective-permute-start | bytes 393224 | tf_op jit(solution)/shard_map/ppermute | solution.py:431
  42.0 24.2 %collective-permute-start.5 = (bf16[128,512]{1,0:T(8,128)(2,1)S(1)}, bf16[128,512]{1,0:T(8,128)(2,1)S(1)}, u32[]{:S(2)}, u32[]{:S(2)}) collective-permute-start(bf16[128,512]{1,0:T(8,128)(2,1)S(1)} %get-tuple-element.44), channel_id=1, source_target_pairs={{0,8},{1,9},{2,10},{3,11},{4,12},{5,13},{6,14},{7,15},{8,0},{9,1},... | collective-permute-start | bytes 393224 | tf_op jit(solution)/shard_map/ppermute | solution.py:432
  67.3 45.7 %copy-start.4 = (s32[1,1,1024]{2,1,0:T(1,128)S(1)}, s32[1,1,1024]{2,1,0:T(1,128)}, u32[]{:S(2)}) copy-start(s32[1,1,1024]{2,1,0:T(1,128)} %param.26) | copy-start | bytes 12292
  67.3 45.7 %copy-start = (bf16[2,64,512]{2,1,0:T(8,128)(2,1)S(1)}, bf16[2,64,512]{2,1,0:T(8,128)(2,1)}, u32[]{:S(2)}) copy-start(bf16[2,64,512]{2,1,0:T(8,128)(2,1)} %grid.5) | copy-start | bytes 393220
  67.3 45.7 %copy-start.3 = (s32[1,1,1024]{2,1,0:T(1,128)S(1)}, s32[1,1,1024]{2,1,0:T(1,128)}, u32[]{:S(2)}) copy-start(s32[1,1,1024]{2,1,0:T(1,128)} %param.27) | copy-start | bytes 12292
  101.9 16.7 %collective-permute-start.6 = (bf16[256,512]{1,0:T(8,128)(2,1)S(1)}, bf16[256,512]{1,0:T(8,128)(2,1)S(1)}, u32[]{:S(2)}, u32[]{:S(2)}) collective-permute-start(bf16[256,512]{1,0:T(8,128)(2,1)S(1)} %get-tuple-element.38.own), channel_id=1, source_target_pairs={{0,63},{1,2},{2,1},{3,4},{4,3},{5,6},{6,5},{7,8},{8,7},{9,10},{10,... | collective-permute-start | bytes 786440 | tf_op jit(solution)/shard_map/ppermute | solution.py:453
  111.0 7.6 %collective-permute-start.7 = (bf16[256,512]{1,0:T(8,128)(2,1)S(1)}, bf16[256,512]{1,0:T(8,128)(2,1)S(1)}, u32[]{:S(2)}, u32[]{:S(2)}) collective-permute-start(bf16[256,512]{1,0:T(8,128)(2,1)S(1)} %get-tuple-element.38.own), channel_id=1, source_target_pairs={{0,1},{1,0},{2,3},{3,2},{4,5},{5,4},{6,7},{7,6},{8,9},{9,8},{10,11... | collective-permute-start | bytes 786440 | tf_op jit(solution)/shard_map/ppermute | solution.py:454
